TPU v7x, 32 devices: a whole 2x2x4 slice. The times are simulated.
32 devices in a mesh: slab: 8 (over z, x), skip: 4 (over y, core).
Axes of the slice: x: 2, y: 2, z: 4, core: 2. Of those that a mesh axis runs over, the one named last changes fastest.
Arguments:
- decoder_tokens: bfloat16 [65536, 192], P(('slab', 'skip')), may hold values from -6 to 6
- skip_tokens: bfloat16 [65536, 192], P(('slab', 'skip')), may hold values from -6 to 6
- cotangent: bfloat16 [65536, 192], P(('slab', 'skip')), may hold values from -6 to 6
- extents: int32 [8], P('slab'), may hold values from 8 to 16
- assignment: int32 [8, 128], P('slab', 'skip'), may hold values from 0 to 127, as said below
- mat_master: float32 [32, 13824], P(('slab', 'skip'))
- mat_first: float32 [32, 13824], P(('slab', 'skip')), may hold values from -0.0024414062 to 0.0024414062
- mat_second: float32 [32, 13824], P(('slab', 'skip')), may hold values from 2.2384885e-09 to 8.953954e-09
- mat_average: float32 [32, 13824], P(('slab', 'skip'))
- vec_master: float32 [32, 72], P(('slab', 'skip'))
- vec_first: float32 [32, 72], P(('slab', 'skip')), may hold values from -0.0024414062 to 0.0024414062
- vec_second: float32 [32, 72], P(('slab', 'skip')), may hold values from 2.2384885e-09 to 8.953954e-09
- vec_average: float32 [32, 72], P(('slab', 'skip'))
- table_master: float32 [343, 6], replicated, may hold values from -4 to 4
- table_first: float32 [343, 6], replicated, may hold values from -0.0024414062 to 0.0024414062
- table_second: float32 [343, 6], replicated, may hold values from 2.2384885e-09 to 8.953954e-09
- table_average: float32 [343, 6], replicated, may hold values from -4 to 4
Outputs:
- layer_output: bfloat16 [65536, 192], P(('slab', 'skip'))
- grad_decoder: float32 [65536, 192], P(('slab', 'skip'))
- grad_skip: float32 [65536, 192], P(('slab', 'skip'))
- global_norm: float32 [], replicated
- mat_grad: float32 [32, 13824], P(('slab', 'skip'))
- mat_master_new: float32 [32, 13824], P(('slab', 'skip'))
- mat_first_new: float32 [32, 13824], P(('slab', 'skip'))
- mat_second_new: float32 [32, 13824], P(('slab', 'skip'))
- mat_average_new: float32 [32, 13824], P(('slab', 'skip'))
- mat_low: bfloat16 [32, 13824], P(('slab', 'skip'))
- vec_grad: float32 [32, 72], P(('slab', 'skip'))
- vec_master_new: float32 [32, 72], P(('slab', 'skip'))
- vec_first_new: float32 [32, 72], P(('slab', 'skip'))
- vec_second_new: float32 [32, 72], P(('slab', 'skip'))
- vec_average_new: float32 [32, 72], P(('slab', 'skip'))
- vec_low: bfloat16 [32, 72], P(('slab', 'skip'))
- table_grad: float32 [343, 6], replicated
- table_master_new: float32 [343, 6], replicated
- table_first_new: float32 [343, 6], replicated
- table_second_new: float32 [343, 6], replicated
- table_average_new: float32 [343, 6], replicated
- table_low: bfloat16 [343, 6], replicated
Inputs may be any that keep to these rules, and one draw needn't show every extreme that they name: `assignment`: each row is a permutation of the slab's windows. The 32 entries held by one index of skip name at most 8 windows of any one aligned block of 32, and exactly 8 of some block.
All inputs are finite; a program needn't handle non-finite values.
Results may differ from a plain program's by a relative error of at most 0.012.
The roundings to bfloat16 on the way count: a program that leaves them out, or rounds other values in their place, can miss the bound.
Values may be sent and summed in bfloat16 or wider, within the bound.
No kernel may reach another device: no remote copies, remote signals or barrier semaphores. Data moves between devices by JAX's collectives and lax.ppermute only.
A program may use at most 128 MiB of HBM per device.

v0:
```python
import jax
import jax.numpy as jnp
from jax import lax
from jax.sharding import PartitionSpec as P

C = 192
HEADS = 6
HEAD_DIM = 32
HIDDEN_SIZE = 768
WS = 4
DEPTH = 16
STEP = 10


EPS = 1e-05
MASK_FILL = -1000000000.0
CLIP = 1.0
BETA_ONE = 0.9
BETA_TWO = 0.999
RATE = 0.3
MATRIX_DECAY = 0.05
ADAM_EPS = 1e-08
EMA_RATE = 0.9


def unpack_matrices(packed):
    device_count = packed.shape[0]
    shapes = ((C, C), (C, 2 * C), (C, C), (C, HIDDEN_SIZE), (HIDDEN_SIZE, C))
    result = []
    offset = 0
    for row_count, column_count in shapes:
        piece_width = row_count * column_count // device_count
        result.append(packed[:, offset : offset + piece_width].reshape(row_count, column_count))
        offset = offset + piece_width
    return result


def unpack_vectors(packed):
    flat = packed.reshape(-1)
    lengths = (C, C, C, C, C, C, C, HIDDEN_SIZE, C)
    result = []
    offset = 0
    for length in lengths:
        result.append(flat[offset : offset + length])
        offset = offset + length
    return result


def position_lookup():
    token_place = jnp.arange(WS**3, dtype=jnp.int32)
    span_size = 2 * WS - 1
    coordinates = (token_place // (WS * WS), token_place // WS % WS, token_place % WS)
    offsets = [coordinate[:, None] - coordinate[None, :] + WS - 1 for coordinate in coordinates]
    relative = (offsets[0] * span_size + offsets[1]) * span_size + offsets[2]
    return (relative.reshape(-1, 1) == jnp.arange(span_size**3, dtype=jnp.int32)[None, :]).astype(
        jnp.float32
    )


def normalize(value_in):
    center = value_in - jnp.mean(value_in, axis=-1, keepdims=True)
    scale = lax.rsqrt(jnp.mean(center * center, axis=-1, keepdims=True) + EPS)
    return (center * scale, scale)


def norm_back(grad_out, normed, scale, gain):
    grad_hat = grad_out * gain
    return scale * (
        grad_hat
        - jnp.mean(grad_hat, axis=-1, keepdims=True)
        - normed * jnp.mean(grad_hat * normed, axis=-1, keepdims=True)
    )


def exact_gelu(value_in):
    return jax.nn.gelu(value_in, approximate=False)


def adamw_update(master, first, second, average, grad, factor, decay):
    clipped = grad * factor
    first_new = BETA_ONE * first + (1.0 - BETA_ONE) * clipped
    second_new = BETA_TWO * second + (1.0 - BETA_TWO) * clipped * clipped
    first_hat = first_new / (1.0 - BETA_ONE**STEP)
    second_hat = second_new / (1.0 - BETA_TWO**STEP)
    master_new = master - RATE * (first_hat / (jnp.sqrt(second_hat) + ADAM_EPS) + decay * master)
    average_new = EMA_RATE * average + (1.0 - EMA_RATE) * master_new
    return (
        clipped,
        master_new,
        first_new,
        second_new,
        average_new,
        master_new.astype(jnp.bfloat16),
    )


def on_device(
    decoder_tokens,
    skip_tokens,
    cotangent,
    extents,
    assignment,
    mat_master,
    mat_first,
    mat_second,
    mat_average,
    vec_master,
    vec_first,
    vec_second,
    vec_average,
    table_master,
    table_first,
    table_second,
    table_average,
):
    mat_gathered, vec_gathered = (
        lax.all_gather(mat_master.astype(jnp.bfloat16), ("slab", "skip"), axis=0, tiled=True),
        lax.all_gather(vec_master.astype(jnp.bfloat16), ("slab", "skip"), axis=0, tiled=True),
    )
    device_count = mat_gathered.shape[0]
    w_query, w_pair, w_output, w_up, w_down = unpack_matrices(mat_gathered)
    (
        gain_one,
        shift_one,
        bias_query,
        bias_value,
        bias_output,
        gain_two,
        shift_two,
        bias_up,
        bias_down,
    ) = unpack_vectors(vec_gathered.astype(jnp.float32))
    skip_count = lax.axis_size("skip")
    window_count = assignment.shape[1]
    token_count = decoder_tokens.shape[0]
    window_tokens = token_count // window_count
    chosen = assignment[0]
    depth_slot = chosen % (DEPTH // WS)
    layers = jnp.clip(extents[0] - WS * depth_slot, 0, WS)
    depth_index = jnp.arange(window_tokens, dtype=jnp.int32) // (WS * WS)
    token_valid = jnp.where(depth_index[None, :] < layers[:, None], 1.0, 0.0).astype(jnp.float32)
    row_valid = token_valid.reshape(-1, 1)
    slab_tokens = lax.all_gather(skip_tokens, "skip", axis=0, tiled=True)
    picked = slab_tokens.reshape(-1, window_tokens, C)[chosen]
    query_in = decoder_tokens.astype(jnp.float32)
    skip_in = picked.reshape(token_count, C).astype(jnp.float32)
    query_hat, query_scale = normalize(query_in)
    skip_hat, skip_scale = normalize(skip_in)
    query_norm = (query_hat * gain_one + shift_one).astype(jnp.bfloat16)
    skip_norm = (skip_hat * gain_one + shift_one).astype(jnp.bfloat16)
    scale_factor = HEAD_DIM ** (-0.5)
    query_rows = (
        (jnp.dot(query_norm, w_query, preferred_element_type=jnp.float32) + bias_query)
        * scale_factor
    ).astype(jnp.bfloat16)
    pair_rows = jnp.dot(skip_norm, w_pair, preferred_element_type=jnp.float32)
    key_rows = pair_rows[:, :C].astype(jnp.bfloat16)
    value_rows = (pair_rows[:, C:] + bias_value).astype(jnp.bfloat16)
    split_shape = (window_count, window_tokens, HEADS, HEAD_DIM)
    query_split = query_rows.reshape(split_shape)
    key_split = key_rows.reshape(split_shape)
    value_split = value_rows.reshape(split_shape)
    lookup = position_lookup()
    position_bias = jnp.dot(lookup, table_master, precision=lax.Precision.HIGHEST)
    position_bias = position_bias.reshape(window_tokens, window_tokens, HEADS).transpose(2, 0, 1)
    key_fill = jnp.where(token_valid > 0, 0.0, MASK_FILL)[:, None, None, :]

    def score_block():
        raw_scores = jnp.einsum(
            "wihd,wjhd->whij", query_split, key_split, preferred_element_type=jnp.float32
        )
        return raw_scores + position_bias[None] + key_fill

    scores = score_block()
    top_score = jnp.max(scores, axis=-1, keepdims=True)
    log_total = top_score + jnp.log(jnp.sum(jnp.exp(scores - top_score), axis=-1, keepdims=True))
    prob_low = jnp.exp(scores - log_total).astype(jnp.bfloat16)
    attended = jnp.einsum(
        "whij,wjhd->wihd", prob_low, value_split, preferred_element_type=jnp.float32
    )
    attended = attended.reshape(token_count, C).astype(jnp.bfloat16)
    middle = (
        query_in + jnp.dot(attended, w_output, preferred_element_type=jnp.float32) + bias_output
    )
    middle_hat, middle_scale = normalize(middle)
    hidden_norm = (middle_hat * gain_two + shift_two).astype(jnp.bfloat16)
    upper = jnp.dot(hidden_norm, w_up, preferred_element_type=jnp.float32) + bias_up
    activated, gelu_back = jax.vjp(exact_gelu, upper)
    activated_low = activated.astype(jnp.bfloat16)
    mlp_out = jnp.dot(activated_low, w_down, preferred_element_type=jnp.float32) + bias_down
    layer_out = (row_valid * (middle + mlp_out)).astype(jnp.bfloat16)
    grad_out = cotangent.astype(jnp.float32) * row_valid
    grad_mlp = grad_out.astype(jnp.bfloat16)
    grad_w_down = jnp.dot(activated_low.T, grad_mlp, preferred_element_type=jnp.float32)
    grad_bias_down = jnp.sum(grad_mlp.astype(jnp.float32), axis=0)
    grad_act = jnp.dot(grad_mlp, w_down.T, preferred_element_type=jnp.float32)
    grad_upper = gelu_back(grad_act)[0].astype(jnp.bfloat16)
    grad_w_up = jnp.dot(hidden_norm.T, grad_upper, preferred_element_type=jnp.float32)
    grad_bias_up = jnp.sum(grad_upper.astype(jnp.float32), axis=0)
    grad_hidden = jnp.dot(grad_upper, w_up.T, preferred_element_type=jnp.float32)
    grad_gain_two = jnp.sum(grad_hidden * middle_hat, axis=0)
    grad_shift_two = jnp.sum(grad_hidden, axis=0)
    grad_middle = grad_out + norm_back(grad_hidden, middle_hat, middle_scale, gain_two)
    grad_branch = grad_middle.astype(jnp.bfloat16)
    grad_w_output = jnp.dot(attended.T, grad_branch, preferred_element_type=jnp.float32)
    grad_bias_output = jnp.sum(grad_branch.astype(jnp.float32), axis=0)
    grad_attended = jnp.dot(grad_branch, w_output.T, preferred_element_type=jnp.float32).astype(
        jnp.bfloat16
    )
    grad_split = grad_attended.reshape(split_shape)
    probs_again = jnp.exp(score_block() - log_total)
    grad_probs = jnp.einsum(
        "wihd,wjhd->whij", grad_split, value_split, preferred_element_type=jnp.float32
    )
    grad_scores = probs_again * (
        grad_probs - jnp.sum(probs_again * grad_probs, axis=-1, keepdims=True)
    )
    grad_scores = grad_scores.astype(jnp.bfloat16)
    score_total = (
        jnp.sum(grad_scores.astype(jnp.float32), axis=0).transpose(1, 2, 0).reshape(-1, HEADS)
    )
    grad_table = jnp.dot(lookup.T, score_total, precision=lax.Precision.HIGHEST)
    grad_query = jnp.einsum(
        "whij,wjhd->wihd", grad_scores, key_split, preferred_element_type=jnp.float32
    )
    grad_query = grad_query.reshape(token_count, C).astype(jnp.bfloat16)
    grad_key = jnp.einsum(
        "whij,wihd->wjhd", grad_scores, query_split, preferred_element_type=jnp.float32
    )
    grad_value = jnp.einsum(
        "whij,wihd->wjhd", prob_low, grad_split, preferred_element_type=jnp.float32
    )
    grad_pair = jnp.concatenate(
        [grad_key.reshape(token_count, C), grad_value.reshape(token_count, C)], axis=1
    ).astype(jnp.bfloat16)
    grad_w_query = (
        jnp.dot(query_norm.T, grad_query, preferred_element_type=jnp.float32) * scale_factor
    )
    grad_bias_query = jnp.sum(grad_query.astype(jnp.float32), axis=0) * scale_factor
    grad_query_norm = (
        jnp.dot(grad_query, w_query.T, preferred_element_type=jnp.float32) * scale_factor
    )
    grad_w_pair = jnp.dot(skip_norm.T, grad_pair, preferred_element_type=jnp.float32)
    grad_bias_value = jnp.sum(grad_pair[:, C:].astype(jnp.float32), axis=0)
    grad_skip_norm = jnp.dot(grad_pair, w_pair.T, preferred_element_type=jnp.float32)
    grad_gain_one = jnp.sum(grad_query_norm * query_hat, axis=0) + jnp.sum(
        grad_skip_norm * skip_hat, axis=0
    )
    grad_shift_one = jnp.sum(grad_query_norm, axis=0) + jnp.sum(grad_skip_norm, axis=0)
    grad_decoder = grad_middle + norm_back(grad_query_norm, query_hat, query_scale, gain_one)
    grad_picked = norm_back(grad_skip_norm, skip_hat, skip_scale, gain_one).reshape(
        window_count, window_tokens, C
    )
    slab_grad = (
        jnp.zeros((skip_count * window_count, window_tokens, C), jnp.float32)
        .at[chosen]
        .set(grad_picked)
    )
    grad_skip = lax.psum_scatter(
        slab_grad.reshape(-1, C).astype(jnp.bfloat16), "skip", scatter_dimension=0, tiled=True
    ).astype(jnp.float32)
    grad_matrices = jnp.concatenate(
        [
            grad_part.reshape(device_count, -1)
            for grad_part in (grad_w_query, grad_w_pair, grad_w_output, grad_w_up, grad_w_down)
        ],
        axis=1,
    )
    grad_vectors = jnp.concatenate(
        [
            grad_gain_one,
            grad_shift_one,
            grad_bias_query,
            grad_bias_value,
            grad_bias_output,
            grad_gain_two,
            grad_shift_two,
            grad_bias_up,
            grad_bias_down,
        ]
    ).reshape(device_count, -1)
    mat_total, vec_total, table_total = lax.psum(
        (grad_matrices, grad_vectors, grad_table), ("slab", "skip")
    )
    squares = (
        jnp.sum(mat_total * mat_total)
        + jnp.sum(vec_total * vec_total)
        + jnp.sum(table_total * table_total)
    )
    position = lax.axis_index(("slab", "skip"))
    mat_share = lax.dynamic_slice_in_dim(mat_total, position, 1, 0)
    vec_share = lax.dynamic_slice_in_dim(vec_total, position, 1, 0)
    global_norm = jnp.sqrt(squares)
    factor = CLIP / jnp.maximum(global_norm, CLIP)
    mat_outs = adamw_update(
        mat_master, mat_first, mat_second, mat_average, mat_share, factor, MATRIX_DECAY
    )
    vec_outs = adamw_update(vec_master, vec_first, vec_second, vec_average, vec_share, factor, 0.0)
    table_outs = adamw_update(
        table_master, table_first, table_second, table_average, table_total, factor, 0.0
    )
    return (
        layer_out,
        grad_decoder,
        grad_skip,
        global_norm,
        mat_outs[0],
        mat_outs[1],
        mat_outs[2],
        mat_outs[3],
        mat_outs[4],
        mat_outs[5],
        vec_outs[0],
        vec_outs[1],
        vec_outs[2],
        vec_outs[3],
        vec_outs[4],
        vec_outs[5],
        table_outs[0],
        table_outs[1],
        table_outs[2],
        table_outs[3],
        table_outs[4],
        table_outs[5],
    )


def solution(mesh):
    return jax.shard_map(
        on_device,
        mesh=mesh,
        in_specs=(
            P(("slab", "skip"), None),
            P(("slab", "skip"), None),
            P(("slab", "skip"), None),
            P("slab"),
            P("slab", "skip"),
            P(("slab", "skip"), None),
            P(("slab", "skip"), None),
            P(("slab", "skip"), None),
            P(("slab", "skip"), None),
            P(("slab", "skip"), None),
            P(("slab", "skip"), None),
            P(("slab", "skip"), None),
            P(("slab", "skip"), None),
            P(),
            P(),
            P(),
            P(),
        ),
        out_specs=(
            P(("slab", "skip"), None),
            P(("slab", "skip"), None),
            P(("slab", "skip"), None),
            P(),
            P(("slab", "skip"), None),
            P(("slab", "skip"), None),
            P(("slab", "skip"), None),
            P(("slab", "skip"), None),
            P(("slab", "skip"), None),
            P(("slab", "skip"), None),
            P(("slab", "skip"), None),
            P(("slab", "skip"), None),
            P(("slab", "skip"), None),
            P(("slab", "skip"), None),
            P(("slab", "skip"), None),
            P(("slab", "skip"), None),
            P(),
            P(),
            P(),
            P(),
            P(),
            P(),
        ),
        check_vma=False,
    )
```

profile of v0, /device:TPU:0, one launch (start us, length us, event | category | flops | bytes accessed | tf_op | source)
XLA Modules:
  0.0 495.7 jit_solution(8929930955416173283)
XLA Ops:
  8.6 43.0 %all-gather = bf16[32,1,72]{2,1,0:T(2,128)(2,1)S(1)} all-gather(bf16[1,1,72]{2,1,0:T(2,128)(2,1)S(1)} %convert_bitcast_fusion.1), channel_id=1, replica_groups=mesh['slab'=8,'skip'=4] {'slab','skip'}, dimensions={0}, use_global_device_ids=true | all-gather | bytes 4752 | tf_op jit(solution)/shard_map/all_gather | solution.py:118
  52.6 41.6 %all-gather.1 = bf16[32,1,13824]{2,1,0:T(2,128)(2,1)S(1)} all-gather(bf16[1,1,13824]{2,1,0:T(2,128)(2,1)S(1)} %convert_bitcast_fusion), channel_id=1, replica_groups=mesh['slab'=8,'skip'=4] {'slab','skip'}, dimensions={0}, use_global_device_ids=true | all-gather | bytes 912384 | tf_op jit(solution)/shard_map/all_gather | solution.py:117
  99.5 3.5 fusion.7
  106.3 5.9 %copy.96 = bf16[8192,192]{1,0:T(8,128)(2,1)} copy(bf16[8192,192]{0,1:T(8,128)(2,1)} %all-gather.4.cloned.1.call-done) | data formatting | bytes 6291456 | tf_op jit(solution)/shard_map/all_gather | solution.py:143
  123.6 4.6 fusion.8
  136.4 6.1 %fusion.34 = bf16[32,64,6,32]{1,3,2,0:T(8,128)(2,1)S(1)} fusion(bf16[32,64,6,32]{1,0,3,2:T(8,128)(2,1)S(1)} %reshape.566, f32[32,6,64,64]{2,3,1,0:T(8,128)} %copy-done, f32[32,6,64]{2,1,0:T(8,128)S(1)} %log_add_fusion, f32[32,64]{1,0:T(8,128)S(1)} %get-tuple-element.138, f32[6,64,64]{1,2,0:T(8,128)S(1)} %bitcast.90), kind=kOutput, calls=%fused_computation.86 | convolution fusion | flops 53870592 | bytes 4874240 | tf_op jit(solution)/shard_map/whij,wjhd->wihd/dot_general | solution.py:178
  148.8 15.4 %multiply_convert_fusion.1 = (bf16[2048,768]{1,0:T(8,128)(2,1)}, f32[2048,768]{1,0:T(8,128)S(1)}, f32[2048,768]{1,0:T(8,128)S(1)}) fusion(f32[768]{0:T(1024)S(1)} %copy-done.75, bf16[192,768]{1,0:T(8,128)(2,1)S(1)} %copy-done.36, f32[2048,192]{0,1:T(8,128)S(1)} %get-tuple-element.142, f32[192]{0:T(256)S(1)} %copy-done.83, f32[192]{0:T(256)S(1)} %copy-done.77, ...), kind=kOutput, calls=%fused_computation.9 | convolution fusion | flops 709754880 | bytes 17617408 | tf_op jit(solution)/shard_map/dot_general | solution.py:187
  164.2 4.3 convert_reduce_fusion.1
  174.5 3.6 reshape.574
  178.0 7.2 %fusion.37 = bf16[32,64,6,32]{1,3,2,0:T(8,128)(2,1)} fusion(bf16[32,64,6,32]{1,0,3,2:T(8,128)(2,1)} %reshape.574, f32[32,6,64,64]{2,3,1,0:T(8,128)} %copy-done, f32[32,6,64]{2,1,0:T(8,128)S(1)} %log_add_fusion, f32[32,64]{1,0:T(8,128)S(1)} %get-tuple-element.138, f32[6,64,64]{1,2,0:T(8,128)S(1)} %bitcast.91), kind=kOutput, calls=%fused_computation.89 | convolution fusion | flops 53870592 | bytes 4874240 | tf_op jit(solution)/shard_map/whij,wihd->wjhd/dot_general | solution.py:230
  185.3 7.7 %multiply_reduce_fusion = (f32[32,6,64]{2,1,0:T(8,128)}, f32[32,6,64,64]{2,3,1,0:T(8,128)}) fusion(f32[32,6,64,64]{2,3,1,0:T(8,128)S(1)} %bitcast.85, f32[32,6,64]{2,1,0:T(8,128)S(1)} %log_add_fusion, f32[32,64]{1,0:T(8,128)S(1)} %get-tuple-element.138, f32[6,64,64]{1,2,0:T(8,128)S(1)} %bitcast.92, bf16[32,64,6,32]{1,0,3,2:T(8,128)(2,1)S(1)} %copy-done.6, ...), kind=kOutput, calls=%fused_computation.7 | convolution fusion | flops 54251520 | bytes 8069120 | tf_op jit(solution)/shard_map/wihd,wjhd->whij/dot_general | solution.py:212
  193.1 6.9 %convert_reduce_fusion = (f32[6,64,64]{1,2,0:T(8,128)}, bf16[32,6,64,64]{2,3,1,0:T(8,128)(2,1)S(1)}) fusion(f32[32,6,64,64]{2,3,1,0:T(8,128)} %get-tuple-element.146, f32[32,6,64]{2,1,0:T(8,128)} %get-tuple-element.145, f32[32,6,64]{2,1,0:T(8,128)S(1)} %log_add_fusion, f32[32,64]{1,0:T(8,128)S(1)} %get-tuple-element.138, f32[32,6,64,64]{2,3,1,0:T(8,128)} %copy-done, ...), kind=kLoop, calls=%fused_computation.4 | loop fusion | flops 6266880 | bytes 8167424 | tf_op jit(solution)/shard_map/reduce_sum | solution.py:220
  209.7 3.6 reshape.576
  213.2 3.6 copy.110
  216.8 3.5 reshape.575
  224.6 4.6 multiply_reduce_fusion.4
  234.4 3.8 convert_element_type.167
  247.5 37.2 %all-reduce = (f32[32,72]{1,0:T(8,128)S(1)}, f32[343,6]{0,1:T(8,128)S(1)}) all-reduce(f32[32,72]{1,0:T(8,128)S(1)} %copy-done.41, f32[343,6]{0,1:T(8,128)S(1)} %fusion.6), channel_id=1, replica_groups=mesh['slab'=8,'skip'=4] {'slab','skip'}, use_global_device_ids=true, to_apply=%region_30.31 | all-reduce | flops 4362 | bytes 34896 | tf_op jit(solution)/shard_map/psum | solution.py:282
  293.4 4.0 fusion.53
  311.3 4.3 broadcast_in_dim.17
  315.6 6.3 %scatter_fusion = f32[128,64,192]{2,1,0:T(8,128)} fusion(f32[128,64,192]{2,1,0:T(8,128)} %broadcast_in_dim.17, s32[32]{0:T(128)S(1)} %copy-done.82, f32[32,64,192]{2,1,0:T(8,128)} %bitcast.94), kind=kCustom, calls=%fused_computation.1 | custom fusion | bytes 4718720 | tf_op jit(solution)/shard_map/scatter | solution.py:257
  321.9 6.3 %convert_element_type.170 = bf16[128,64,192]{2,1,0:T(8,128)(2,1)} convert(f32[128,64,192]{2,1,0:T(8,128)} %scatter_fusion) | non-fusion elementwise | flops 1572864 | bytes 9437184 | tf_op jit(solution)/shard_map/convert_element_type | solution.py:260
  335.3 103.4 %all-reduce.3.cloned.1.call-done = f32[32,13824]{1,0:T(8,128)} async-done(((f32[32,13824]{1,0:T(8,128)}), f32[32,13824]{1,0:T(8,128)}) %all-reduce.3.cloned.1.call-update) | async-done | bytes 1769488 | tf_op jit(solution)/shard_map/psum | solution.py:282
  448.5 36.7 %reduce-scatter.2.cloned.1.call-done = bf16[2048,192]{1,0:T(8,128)(2,1)} async-done(((bf16[8192,192]{1,0:T(8,128)(2,1)}), bf16[2048,192]{1,0:T(8,128)(2,1)}) %reduce-scatter.2.cloned.1.call-update) | async-done | bytes 786448 | tf_op jit(solution)/shard_map/reduce_scatter | solution.py:259
  (310 shorter events, 109.5 us)
Async XLA Ops:
  7.2 99.1 %all-gather.4.cloned.1.call-start = ((), (), s32[]{:S(2)}) async-start(), calls=%async_computation.1 | async-start | bytes 3932160 | tf_op jit(solution)/shard_map/all_gather | solution.py:143
  7.9 430.7 %all-reduce.3.cloned.1.call-start = ((), (), s32[]{:S(2)}) async-start(), calls=%async_computation.3 | async-start | bytes 3538944 | tf_op jit(solution)/shard_map/psum | solution.py:282
  99.3 24.3 %copy-start.8 = (bf16[32,64,6,32]{1,0,3,2:T(8,128)(2,1)}, bf16[32,64,6,32]{1,0,3,2:T(8,128)(2,1)S(1)}, u32[]{:S(2)}) copy-start(bf16[32,64,6,32]{1,0,3,2:T(8,128)(2,1)S(1)} %reshape.568) | copy-start | bytes 2359300
  106.2 58.0 %copy-start.25 = (bf16[768,192]{1,0:T(8,128)(2,1)}, bf16[768,192]{1,0:T(8,128)(2,1)S(1)}, u32[]{:S(2)}) copy-start(bf16[768,192]{1,0:T(8,128)(2,1)S(1)} %reshape.573) | copy-start | bytes 884740
  148.2 22.4 %copy-start.1 = (f32[2048,192]{0,1:T(8,128)}, f32[2048,192]{0,1:T(8,128)S(1)}, u32[]{:S(2)}) copy-start(f32[2048,192]{0,1:T(8,128)S(1)} %get-tuple-element.142) | copy-start | bytes 4718596
  148.5 22.1 %copy-start.53 = (f32[2048]{0:T(1024)}, f32[2048]{0:T(1024)S(1)}, u32[]{:S(2)}) copy-start(f32[2048]{0:T(1024)S(1)} %add_rsqrt_fusion.1) | copy-start | bytes 24580
  193.0 36.1 %copy-start.46 = (f32[2048]{0:T(1024)}, f32[2048]{0:T(1024)S(1)}, u32[]{:S(2)}) copy-start(f32[2048]{0:T(1024)S(1)} %rsqrt.31) | copy-start | bytes 24580
  193.1 36.1 %copy-start.48 = (f32[2048]{0:T(1024)}, f32[2048]{0:T(1024)S(1)}, u32[]{:S(2)}) copy-start(f32[2048]{0:T(1024)S(1)} %div.123) | copy-start | bytes 24580
  304.8 180.4 %reduce-scatter.2.cloned.1.call-start = ((), (), s32[]{:S(2)}) async-start(), calls=%async_computation.2 | async-start | bytes 5242880 | tf_op jit(solution)/shard_map/reduce_scatter | solution.py:259
  335.2 108.0 %copy-start.57 = (f32[343,6]{0,1:T(8,128)S(1)}, f32[343,6]{0,1:T(8,128)}, u32[]{:S(2)}) copy-start(f32[343,6]{0,1:T(8,128)} %param.30) | copy-start | bytes 24700
  335.2 108.1 %copy-start.58 = (f32[343,6]{0,1:T(8,128)S(1)}, f32[343,6]{0,1:T(8,128)}, u32[]{:S(2)}) copy-start(f32[343,6]{0,1:T(8,128)} %param.31) | copy-start | bytes 24700
  335.2 108.1 %copy-start.59 = (f32[343,6]{0,1:T(8,128)S(1)}, f32[343,6]{0,1:T(8,128)}, u32[]{:S(2)}) copy-start(f32[343,6]{0,1:T(8,128)} %param.32) | copy-start | bytes 24700
  335.2 108.7 %copy-start.60 = (f32[343,6]{0,1:T(8,128)S(1)}, f32[343,6]{0,1:T(8,128)}, u32[]{:S(2)}) copy-start(f32[343,6]{0,1:T(8,128)} %param.33) | copy-start | bytes 24700
  335.2 109.3 %copy-start.87 = (f32[1,72]{1,0:T(1,128)S(1)}, f32[1,72]{1,0:T(1,128)}, u32[]{:S(2)}) copy-start(f32[1,72]{1,0:T(1,128)} %param.26) | copy-start | bytes 868
  335.2 109.3 %copy-start.88 = (f32[1,72]{1,0:T(1,128)S(1)}, f32[1,72]{1,0:T(1,128)}, u32[]{:S(2)}) copy-start(f32[1,72]{1,0:T(1,128)} %param.27) | copy-start | bytes 868
  335.2 109.3 %copy-start.89 = (f32[1,72]{1,0:T(1,128)S(1)}, f32[1,72]{1,0:T(1,128)}, u32[]{:S(2)}) copy-start(f32[1,72]{1,0:T(1,128)} %param.28) | copy-start | bytes 868
  335.2 109.8 %copy-start.92 = (f32[1,72]{1,0:T(1,128)S(1)}, f32[1,72]{1,0:T(1,128)}, u32[]{:S(2)}) copy-start(f32[1,72]{1,0:T(1,128)} %param.29) | copy-start | bytes 868
  335.2 110.3 %copy-start.37 = (f32[1,13824]{1,0:T(1,128)S(1)}, f32[1,13824]{1,0:T(1,128)}, u32[]{:S(2)}) copy-start(f32[1,13824]{1,0:T(1,128)} %param.22) | copy-start | bytes 165892
  335.3 110.3 %copy-start.43 = (f32[1,13824]{1,0:T(1,128)S(1)}, f32[1,13824]{1,0:T(1,128)}, u32[]{:S(2)}) copy-start(f32[1,13824]{1,0:T(1,128)} %param.23) | copy-start | bytes 165892
  335.3 110.3 %copy-start.44 = (f32[1,13824]{1,0:T(1,128)S(1)}, f32[1,13824]{1,0:T(1,128)}, u32[]{:S(2)}) copy-start(f32[1,13824]{1,0:T(1,128)} %param.24) | copy-start | bytes 165892
  335.3 112.5 %copy-start.42 = (f32[1,13824]{1,0:T(1,128)S(1)}, f32[1,13824]{1,0:T(1,128)}, u32[]{:S(2)}) copy-start(f32[1,13824]{1,0:T(1,128)} %param.25) | copy-start | bytes 165892
  443.9 43.7 %copy-start.45 = (f32[343,6]{0,1:T(8,128)}, f32[343,6]{0,1:T(8,128)S(1)}, u32[]{:S(2)}) copy-start(f32[343,6]{0,1:T(8,128)S(1)} %get-tuple-element.103) | copy-start | bytes 24700
  445.1 42.5 %copy-start.90 = (f32[1,72]{1,0:T(1,128)}, f32[1,72]{1,0:T(1,128)S(1)}, u32[]{:S(2)}) copy-start(f32[1,72]{1,0:T(1,128)S(1)} %get-tuple-element.108) | copy-start | bytes 868
  447.8 39.8 %copy-start.38 = (f32[1,13824]{1,0:T(1,128)}, f32[1,13824]{1,0:T(1,128)S(1)}, u32[]{:S(2)}) copy-start(f32[1,13824]{1,0:T(1,128)S(1)} %get-tuple-element.113) | copy-start | bytes 165892
  (76 other events, 284.7 us)
Sparse Core Ops, SparseCore 0:
  9.6 31.3 all-gather.3
  304.9 133.7 all-reduce.2
  441.2 43.9 reduce-scatter.1
where the time goes:
time: 506 us; the launch traced here: 496 us
  waiting for transfers between devices  141 us (28%)
  blocking collectives  122 us (24%)
  local copies, waits for them, and re-layouts  93.7 us (19%)
  matrix products  81.9 us (16%)
  other arithmetic  38.3 us (8%)
  between operations  19.1 us (4%)
    psum x1, waiting for transfers between devices, on_device(): lax.psum((grad_matrices, grad_vectors, grad_table), ('slab', 'skip'))  103 us
    all_gather x1, blocking collectives, on_device(): lax.all_gather(vec_master.astype(jnp.bfloat16), ('slab', 'skip'), axis=0,...  43 us
    all_gather x1, blocking collectives, on_device(): lax.all_gather(mat_master.astype(jnp.bfloat16), ('slab', 'skip'), axis=0,...  41.6 us
    psum x1, blocking collectives, on_device(): lax.psum((grad_matrices, grad_vectors, grad_table), ('slab', 'skip'))  37.2 us
    reduce_scatter x1, waiting for transfers between devices, on_device(): lax.psum_scatter(slab_grad.reshape(-1, C).astype(jnp.bfloat16), 'skip', s...  36.7 us
    unnamed x201, local copies, waits for them, and re-layouts  18.6 us
    dot_general x1, matrix products, on_device(): jnp.dot(hidden_norm, w_up, preferred_element_type=jnp.float32) + bias_up  15.4 us
  transfers between devices with their start and end apart: 3, of which 2 were waited for; matrix products, arithmetic and copies ran while one was open for 10% of the time, Pallas kernels for 0%

commit v1 on v0

v1 whole, which is shorter than its diff:
```python
import functools
import math
import jax
import jax.numpy as jnp
from jax import lax
from jax.experimental import pallas as pl
from jax.experimental.pallas import tpu as pltpu
from jax.sharding import PartitionSpec as P

C = 192
HEADS = 6
HEAD_DIM = 32
HIDDEN_SIZE = 768
WS = 4
DEPTH = 16
STEP = 10
WTOK = 64
REL = 343

EPS = 1e-05
MASK_FILL = -1000000000.0
CLIP = 1.0
BETA_ONE = 0.9
BETA_TWO = 0.999
RATE = 0.3
MATRIX_DECAY = 0.05
ADAM_EPS = 1e-08
EMA_RATE = 0.9

BF = jnp.bfloat16
F32 = jnp.float32
GROUP = 256
GWIN = GROUP // WTOK
T = 1024
GROUPS = T // GROUP
WIN = T // WTOK
QSCALE = HEAD_DIM ** (-0.5)
SHAPES = ((C, C), (C, 2 * C), (C, C), (C, HIDDEN_SIZE), (HIDDEN_SIZE, C))
VLEN = (C, C, C, C, C, C, C, HIDDEN_SIZE, C)
VOFF = tuple(sum(VLEN[:n]) for n in range(len(VLEN)))
VEC = sum(VLEN)
MAT = sum(r * c for r, c in SHAPES)
ROWS = 32
OUTER = 4
INNER = ROWS // OUTER
BLOCK = (16, 896)
BLOCK_TILES = BLOCK[1] // 128
VEC_TILE = MAT // ROWS // 128
SIDE_TILE = VEC_TILE + 1
TABLE_LANES = 8 * 384 // ROWS


def mm(a, b):
    return jnp.dot(a, b, preferred_element_type=F32)


def mm_nt(a, b):
    return lax.dot_general(a, b, (((1,), (1,)), ((), ())), preferred_element_type=F32)


def iota(shape, dim):
    return lax.broadcasted_iota(jnp.int32, shape, dim)


def kept(value):
    return pltpu.with_memory_space_constraint(value, pltpu.HBM)


def both(column):
    return jnp.concatenate([column, column], axis=1)


def place(slot):
    span = 2 * WS - 1
    return ((slot >> 4) * span + ((slot >> 2) & 3)) * span + (slot & 3)


def splits(value):
    high = value.astype(BF)
    rest = value - high.astype(F32)
    middle = rest.astype(BF)
    return high, middle, (rest - middle.astype(F32)).astype(BF)


def normed(value):
    center = value - jnp.sum(value, axis=0, keepdims=True) * (1.0 / C)
    scale = lax.rsqrt(jnp.sum(center * center, axis=0, keepdims=True) * (1.0 / C) + EPS)
    return center * scale, scale


def normed_back(grad_hat, hat, scale):
    mean_grad = jnp.sum(grad_hat, axis=0, keepdims=True) * (1.0 / C)
    mean_both = jnp.sum(grad_hat * hat, axis=0, keepdims=True) * (1.0 / C)
    return scale * (grad_hat - mean_grad - hat * mean_both)


def fold(value):
    return sum(value[:, n : n + 128] for n in range(0, value.shape[1], 128))


def gelu_parts(u):
    t = pl.reciprocal(1.0 + (0.3275911 * 0.5**0.5) * jnp.abs(u), approx=True)
    bell = jnp.exp2((-0.5 * math.log2(math.e)) * (u * u))
    series = 0.5 * 1.061405429
    for factor in (-1.453152027, 1.421413741, -0.284496736, 0.254829592):
        series = series * t + 0.5 * factor
    tail = series * t * bell
    cdf = jnp.where(u >= 0.0, 1.0 - tail, tail)
    return u * cdf, cdf + ((0.5 / math.pi) ** 0.5 * u) * bell


def early_kernel(skip_count, windows, chosen, table, after, bias_s, ranks, tab_s, big, count_s):
    del after
    tab_s[...] = jnp.zeros_like(tab_s)
    tab_s[0:HEADS, 0:REL] = table[...]
    hot = (iota((256, 128), 0) == place(iota((256, 128), 1) & 63)).astype(BF)
    total = None
    for part in splits(tab_s[...]):
        part = part.astype(F32)
        for j in range(WTOK):
            turn = (place(j) - place(WTOK - 1)) % 384
            rolled = pltpu.roll(part, turn, 1) if turn else part
            big[0, 8 * j : 8 * j + 8, :] = rolled[:, 0:128]
            big[1, 8 * j : 8 * j + 8, :] = rolled[:, 128:256]
        product = mm(big[0].astype(BF), hot[0:128]) + mm(big[1].astype(BF), hot[128:256])
        total = product if total is None else total + product
    big[0] = total
    for h in range(HEADS):
        bias_s[h] = big[0, pl.ds(h, WTOK, stride=8), :]
    for e in range(skip_count):
        count_s[e] = 0

    def note(w, rank_row):
        owner = lax.div(chosen[w], windows)
        rank = count_s[owner]
        count_s[owner] = rank + 1
        return jnp.where(iota((1, 128), 1) == w, rank, rank_row)

    ranks[...] = lax.fori_loop(0, windows, note, jnp.zeros((1, 128), jnp.int32))


def layer_kernel(
    skip_count,
    windows,
    piece_count,
    chosen,
    extents,
    here,
    ranks,
    dec_all,
    cot_all,
    bias_s,
    *refs,
):
    step = pl.program_id(0)
    packs, refs = refs[:OUTER], refs[OUTER:]
    pieces, refs = refs[:piece_count], refs[piece_count:]
    layer_out, grad_dec, everyone, *refs = refs
    grad_picks, refs = refs[:skip_count], refs[skip_count:]
    grad_packs, refs = refs[:OUTER], refs[OUTER:]
    (
        pick_s,
        big,
        vcol,
        wq,
        wqt,
        wkv,
        wkvt,
        wo,
        wot,
        w1,
        w1t,
        w2,
        w2t,
        xn_s,
        sn_s,
        hn_s,
        o_s,
        gl_s,
        du_s,
        q_s,
        qbd_s,
        kst_s,
        vst_s,
        kcat_s,
        vcat_s,
        pf_s,
        pb_s,
        ds_s,
        da_s,
        do_s,
        dm_s,
        u_s,
        ga_s,
        gh_s,
        gs_s,
        dq_s,
        dkv_s,
        n1_s,
        n2_s,
        n3_s,
        x1_s,
        gds_s,
        aq,
        akv,
        ao,
        a1,
        a2,
        ln_s,
        slab,
        slab_sem,
        dec_s,
        cot_s,
        token_sem,
        pack_s,
        pack_sem,
    ) = refs
    dec, cot = dec_s.at[step], cot_s.at[step]
    stage, block_s = u_s, ga_s
    my_skip, mix = here[0], here[1]
    lane = iota((1, 128), 1)
    left = lane < WTOK

    def tile_of(number):
        j, n = divmod(number, BLOCK_TILES)
        return n, pl.ds(j, ROWS, stride=BLOCK[0]), slice(None)


    def token_copies(n):
        lanes = slice(T * n, T * n + T)
        return [
            pltpu.make_async_copy(dec_all.at[:, lanes], dec_s.at[n], token_sem.at[2 * n]),
            pltpu.make_async_copy(cot_all.at[:, lanes], cot_s.at[n], token_sem.at[2 * n + 1]),
        ]

    for n in range(1, windows // WIN):

        @pl.when(step == n)
        def _(n=n):
            for copy in token_copies(n):
                copy.wait()

    @pl.when(step == 0)
    def _():
        copies = token_copies(0) + [
            pltpu.make_async_copy(
                piece, slab.at[:, n * piece.shape[1] : (n + 1) * piece.shape[1]], slab_sem.at[n]
            )
            for n, piece in enumerate(pieces)
        ]
        pack_copies = [
            pltpu.make_async_copy(packs[n], pack_s.at[n], pack_sem.at[n]) for n in range(OUTER)
        ]
        for copy in pack_copies + copies + [copy for n in range(1, windows // WIN) for copy in token_copies(n)]:
            copy.start()
        for ref in (gds_s, aq, akv, ao, a1, a2, ln_s):
            ref[...] = jnp.zeros_like(ref)
        for ref, rows in ((xn_s, C), (sn_s, C), (hn_s, C), (o_s, C), (gl_s, HIDDEN_SIZE)):
            ref[rows : rows + 16, :] = jnp.ones((16, T), BF)
        for copy in pack_copies:
            copy.wait()
        for outer in range(OUTER):
            for inner in range(INNER):
                k = inner * OUTER + lax.bitwise_xor(my_skip, outer)
                rows = pl.ds(pl.multiple_of(k * BLOCK[0], BLOCK[0]), BLOCK[0])
                for n in range(BLOCK_TILES):
                    block_s[n, rows, :] = pack_s[outer, inner, :, 128 * n : 128 * n + 128].astype(
                        F32
                    )
        offset = 0
        for (rows, cols), plain, turned in zip(
            SHAPES, (wq, wkv, wo, w1, w2), (wqt, wkvt, wot, w1t, w2t)
        ):
            per = rows // ROWS
            tiles = -(-cols // 128)
            for a in range(per):
                first, shift = divmod(offset + a * cols, 128)
                for n in range(tiles):
                    piece = block_s[tile_of(first + n)]
                    if shift and n + 1 < tiles:
                        after = block_s[tile_of(first + n + 1)]
                        piece = jnp.concatenate([piece[:, shift:], after[:, :shift]], axis=1)
                    elif shift:
                        piece = pltpu.roll(piece, 128 - shift, 1)
                    stage[n, pl.ds(a, ROWS, stride=per), :] = piece
            for n in range(tiles):
                width = min(128, cols - 128 * n)
                value = stage[n, 0:rows, :].astype(BF)
                plain[:, 128 * n : 128 * n + width] = value[:, 0:width]
                turned[128 * n : 128 * n + width, :] = jnp.transpose(value)[0:width]
            offset += per * cols
        side = block_s[tile_of(VEC_TILE)]
        per = VEC // ROWS
        vec = jnp.concatenate([side[k : k + 1, 0:per] for k in range(ROWS)], axis=1)
        vcol[...] = jnp.transpose(jnp.broadcast_to(vec, (128, VEC)))
        side = block_s[tile_of(SIDE_TILE)]
        everyone[...] = side.astype(jnp.int32)
        for copy in copies:
            copy.wait()

    def column(number, first=0, last=None):
        start = VOFF[number]
        return vcol[start + first : start + (VLEN[number] if last is None else last), :]

    chunks = [slice(128 * c, 128 * c + 128) for c in range(T // 128)]
    tiles = [slice(GROUP * g, GROUP * g + GROUP) for g in range(GROUPS)]
    layers, valid = [], []
    for c in range(len(chunks)):
        deep = [
            jnp.clip(extents[0] - WS * (chosen[step * WIN + 2 * c + w] & 3), 0, WS) for w in (0, 1)
        ]
        layers.append(jnp.where(left, deep[0], deep[1]))
        valid.append(jnp.where((lane & 63) >> 4 < layers[c], 1.0, 0.0))

    scale_one, scale_two, scale_three = {}, {}, {}

    def stacks(rows, g, stack_ref, cat_ref):
        turned = pltpu.roll(rows, WTOK, 1)
        first, second = rows[:, 0:128], rows[:, 128:256]
        mixed, middle = turned[:, 0:128], turned[:, 128:256]
        at_left = (first, middle, second, mixed)
        at_right = (mixed, first, middle, second)
        for h in range(0, HEADS, 2):
            n = g * HEADS + h
            at = slice(HEAD_DIM * h, HEAD_DIM * h + HEAD_DIM)
            after = slice(HEAD_DIM * h + HEAD_DIM, HEAD_DIM * h + 2 * HEAD_DIM)
            pieces = []
            for w in range(GWIN):
                to = slice(HEAD_DIM * w, HEAD_DIM * w + HEAD_DIM)
                stack_ref[n, to, :] = at_left[w][at, 0:WTOK]
                stack_ref[n + 1, to, :] = at_left[w][after, 0:WTOK]
                pieces.append(jnp.where(left, at_left[w][at], at_right[w][after]))
            pair = jnp.transpose(jnp.concatenate(pieces, axis=0))
            cat_ref[n] = pair[0:WTOK]
            cat_ref[n + 1] = pair[WTOK:]

    window_mask = [
        (iota((HEAD_DIM, GROUP), 1) >> 6 == w).astype(F32).astype(BF) for w in range(GWIN)
    ]

    def spread(rows):
        return jnp.concatenate([rows * mask for mask in window_mask], axis=0)

    def own(stacked, probs):
        parts = []
        for n in range(GWIN // 2):
            cut = mm(
                stacked[2 * HEAD_DIM * n : 2 * HEAD_DIM * (n + 1)],
                probs[:, 128 * n : 128 * n + 128],
            )
            parts.append(jnp.where(left, cut[0:HEAD_DIM], cut[HEAD_DIM:]))
        return jnp.concatenate(parts, axis=1)

    def unstack(product):
        parts = []
        for n in range(GWIN // 2):
            cut = product[2 * HEAD_DIM * n : 2 * HEAD_DIM * (n + 1)]
            parts.append(jnp.where(left, cut[0:HEAD_DIM], cut[HEAD_DIM:]))
        return jnp.concatenate(parts, axis=1)

    def filled(g):
        return jnp.concatenate(
            [
                jnp.concatenate(
                    [
                        jnp.broadcast_to(jnp.where(layers[c] > d, 0.0, MASK_FILL), (WS * WS, 128))
                        for d in range(WS)
                    ],
                    axis=0,
                )
                for c in (2 * g, 2 * g + 1)
            ],
            axis=1,
        )

    def place_of(n):
        g, h = divmod(n, HEADS)
        return slice(HEAD_DIM * h, HEAD_DIM * h + HEAD_DIM), tiles[g]

    def softmax(n, scores, fill):
        scores = scores + both(bias_s[n % HEADS]) + fill
        powers = jnp.exp(scores - jnp.max(scores, axis=0, keepdims=True))
        probs = powers * pl.reciprocal(jnp.sum(powers, axis=0, keepdims=True), approx=True)
        pf_s[n] = probs
        pb_s[n] = probs.astype(BF)

    def softmax_back(n, grad_probs):
        probs = pf_s[n]
        grad_scores = (
            probs * (grad_probs - jnp.sum(probs * grad_probs, axis=0, keepdims=True))
        ).astype(BF)
        gds_s[n % HEADS] += fold(grad_scores.astype(F32))
        ds_s[n] = grad_scores

    def forward(g):
        lanes = tiles[g]
        for c in (2 * g, 2 * g + 1):
            cut = chunks[c]
            hat, scale_one[c] = normed(dec[:, cut].astype(F32))
            n1_s[:, cut] = hat
            xn_s[0:C, cut] = (hat * column(0) + column(1)).astype(BF)
            yield 130
            halves = []
            for w in (0, 1):
                a = chosen[step * WIN + 2 * c + w]
                at = lax.bitwise_xor(a, mix * windows) >> 1
                part = slab[:, pl.ds(pl.multiple_of(at * 128, 128), 128)]
                halves.append(pltpu.roll(part, ((a + w) & 1) * WTOK, 1))
            hat, scale_two[c] = normed(jnp.where(left, halves[0], halves[1]).astype(F32))
            n2_s[:, cut] = hat
            sn_s[0:C, cut] = (hat * column(0) + column(1)).astype(BF)
            yield 160
        query = mm(wqt[...], xn_s[0:C, lanes])
        pair = mm(wkvt[...], sn_s[0:C, lanes])
        q_s[:, lanes] = ((query + both(column(2))) * QSCALE).astype(BF)
        for c in (2 * g, 2 * g + 1):
            dm_s[:, chunks[c]] = (cot[:, chunks[c]].astype(F32) * valid[c]).astype(BF)
        yield 250
        first = g * HEADS
        for n in range(first, first + HEADS):
            qbd_s[n] = spread(q_s[place_of(n)])
        stacks(pair[0:C].astype(BF), g, kst_s, kcat_s)
        yield 250
        stacks((pair[C:] + both(column(3))).astype(BF), g, vst_s, vcat_s)
        yield 250
        fill = filled(g)
        scores = {}
        for n in range(first, first + HEADS + 2):
            if n < first + HEADS:
                scores[n] = mm(kcat_s[n], qbd_s[n])
            if n >= first + 2:
                o_s[place_of(n - 2)] = own(vst_s[n - 2], pb_s[n - 2]).astype(BF)
            if first + 1 <= n <= first + HEADS:
                softmax(n - 1, scores.pop(n - 1), fill)
            yield 180
        product = mm(w2[...], dm_s[:, lanes])
        ga_s[2 * g] = product[:, 0:128]
        ga_s[2 * g + 1] = product[:, 128:256]
        yield 300
        x1_s[:, lanes] = mm(wot[...], o_s[0:C, lanes])
        yield 150
        for c in (2 * g, 2 * g + 1):
            cut = chunks[c]
            middle = dec[:, cut].astype(F32) + x1_s[:, cut] + column(4)
            x1_s[:, cut] = middle
            hat, scale_three[c] = normed(middle)
            n3_s[:, cut] = hat
            hn_s[0:C, cut] = (hat * column(5) + column(6)).astype(BF)
            yield 150

    def feed(g):
        lanes = tiles[g]
        product = mm(w1t[...], hn_s[0:C, lanes])
        u_s[2 * g] = product[:, 0:128]
        u_s[2 * g + 1] = product[:, 128:256]
        yield 300
        piece = 32
        for start in range(0, HIDDEN_SIZE, piece):
            rows = slice(start, start + piece)
            for c in (2 * g, 2 * g + 1):
                active, slope = gelu_parts(u_s[c, rows, :] + column(7, start, start + piece))
                gl_s[rows, chunks[c]] = active.astype(BF)
                du_s[rows, chunks[c]] = (ga_s[c, rows, :] * slope).astype(BF)
            yield 35 * piece // 16
        gh_s[:, lanes] = mm(w1[...], du_s[:, lanes])
        yield 450
        mlp = mm(w2t[...], gl_s[0:HIDDEN_SIZE, lanes]) + both(column(8))
        layer_out[:, lanes] = (
            jnp.concatenate([valid[2 * g], valid[2 * g + 1]], axis=1) * (x1_s[:, lanes] + mlp)
        ).astype(BF)
        yield 500
        for c in (2 * g, 2 * g + 1):
            cut = chunks[c]
            grad, hat = gh_s[:, cut], n3_s[:, cut]
            ln_s[2] += grad * hat
            ln_s[3] += grad
            back = normed_back(grad * column(5), hat, scale_three[c])
            grad_middle = cot[:, cut].astype(F32) * valid[c] + back
            x1_s[:, cut] = grad_middle
            da_s[:, cut] = grad_middle.astype(BF)
            yield 170
        do_s[:, lanes] = mm(wo[...], da_s[:, lanes]).astype(BF)
        yield 150

    def backward(g):
        lanes = tiles[g]
        first = g * HEADS
        spreads, grads = {}, {}
        for n in range(first, first + HEADS + 2):
            if n < first + HEADS:
                at, _ = place_of(n)
                spreads[n] = spread(do_s[at, lanes])
                grads[n] = mm(vcat_s[n], spreads[n])
                twice = jnp.concatenate([pb_s[n], pb_s[n]], axis=0)
                dkv_s[at.start + C : at.stop + C, lanes] = unstack(
                    mm_nt(spreads.pop(n), twice)
                ).astype(BF)
            if n >= first + 2:
                at, _ = place_of(n - 2)
                dq_s[at, lanes] = own(kst_s[n - 2], ds_s[n - 2]).astype(BF)
                twice = jnp.concatenate([ds_s[n - 2], ds_s[n - 2]], axis=0)
                dkv_s[at, lanes] = unstack(mm_nt(qbd_s[n - 2], twice)).astype(BF)
            if first + 1 <= n <= first + HEADS:
                softmax_back(n - 1, grads.pop(n - 1))
            yield 340
        gh_s[:, lanes] = mm(wq[...], dq_s[:, lanes])
        yield 150
        gs_s[:, lanes] = mm(wkv[...], dkv_s[:, lanes])
        yield 300
        for c in (2 * g, 2 * g + 1):
            cut = chunks[c]
            grad, hat = gh_s[:, cut] * QSCALE, n1_s[:, cut]
            ln_s[0] += grad * hat
            ln_s[1] += grad
            grad_dec[:, cut] = x1_s[:, cut] + normed_back(grad * column(0), hat, scale_one[c])
            yield 170
            grad, hat = gs_s[:, cut], n2_s[:, cut]
            ln_s[0] += grad * hat
            ln_s[1] += grad
            back = normed_back(grad * column(0), hat, scale_two[c]).astype(BF)
            for w in (0, 1):
                a = chosen[step * WIN + 2 * c + w]
                rank = ranks[0, step * WIN + 2 * c + w]
                owner = lax.bitwise_xor(lax.div(a, windows), mix)
                half = pltpu.roll(back, ((rank + w) & 1) * WTOK, 1)
                at = pl.ds(pl.multiple_of((rank >> 1) * 128, 128), 128)
                pick_s[owner, :, at] = jnp.where(
                    lane >> 6 == (rank & 1), half, pick_s[owner, :, at]
                )
            yield 250

    def add(ref, product):
        ref[0] += product[:, 0:128]
        ref[1, :, 0 : C - 128] += product[:, 128:]

    def early_sums():
        add(a2, mm_nt(gl_s[...], dm_s[...]))
        yield 1200
        a1[...] += mm_nt(du_s[...], hn_s[...])
        yield 1200
        add(ao, mm_nt(o_s[...], da_s[...]))
        yield 400

    costs = {forward: 3500, feed: 3450, backward: 4000, early_sums: 2800}

    def interleaved(parts):
        running = [[part(*args), 0, costs[part]] for part, *args in parts]
        while running:
            now = min(running, key=lambda entry: entry[1] / entry[2])
            try:
                now[1] += next(now[0])
            except StopIteration:
                running.remove(now)

    for slot in range(GROUPS + 2):
        parts = [
            (part, slot - lag)
            for lag, part in enumerate((forward, feed, backward))
            if 0 <= slot - lag < GROUPS
        ]
        if slot == GROUPS + 1:
            parts.append((early_sums,))
        interleaved(parts)
    add(aq, mm_nt(xn_s[...], dq_s[...]))
    akv[...] += mm_nt(dkv_s[...], sn_s[...])

    @pl.when(step == pl.num_programs(0) - 1)
    def _():
        offset = 0
        sums = {1: [], 3: []}
        for number, ((rows, cols), ref) in enumerate(zip(SHAPES, (aq, akv, ao, a1, a2))):
            per = rows // ROWS
            tiles = -(-cols // 128)
            source = ref
            if number in sums:
                source = stage
                for n in range(tiles):
                    turned = jnp.transpose(ref[128 * n : 128 * n + 128, :])
                    sums[number].append(turned[rows : rows + 1])
                    stage[n, 0:rows, :] = turned[0:rows]
            joined = 2 if cols % 128 else 1
            for a in range(0, per, joined):
                value = jnp.concatenate(
                    [
                        jnp.concatenate(
                            [source[n, pl.ds(b, ROWS, stride=per), :] for n in range(tiles)], axis=1
                        )[:, 0:cols]
                        for b in range(a, a + joined)
                    ],
                    axis=1,
                )
                if number == 0:
                    value = value * QSCALE
                for n in range(joined * cols // 128):
                    block_s[tile_of((offset + a * cols) // 128 + n)] = value[
                        :, 128 * n : 128 * n + 128
                    ]
            offset += per * cols
        rows = [jnp.sum(jnp.transpose(ln_s[n]), axis=0, keepdims=True) for n in range(4)]
        def last_row(ref, at):
            return jnp.concatenate(
                [ref[0, at : at + 1, :], ref[1, at : at + 1, 0 : C - 128]], axis=1
            )

        flat = jnp.concatenate(
            [
                rows[0],
                rows[1],
                last_row(aq, C) * QSCALE,
                jnp.concatenate(sums[1], axis=1)[:, C:],
                last_row(ao, C),
                rows[2],
                rows[3],
                *sums[3],
                last_row(a2, HIDDEN_SIZE),
            ],
            axis=1,
        )
        big[0] = jnp.zeros((8 * WTOK, 128), F32)
        for h in range(HEADS):
            big[0, pl.ds(h, WTOK, stride=8), :] = gds_s[h]
        hot = (iota((128, 256), 1) == place(iota((128, 256), 0) & 63)).astype(BF)
        total = sum(mm(part, hot) for part in splits(big[0]))
        big[0] = total[:, 0:128]
        big[1] = total[:, 128:256]
        result = jnp.zeros((8, 384), F32)
        for j in range(WTOK):
            row = jnp.concatenate(
                [
                    big[0, 8 * j : 8 * j + 8, :],
                    big[1, 8 * j : 8 * j + 8, :],
                    jnp.zeros((8, 128), F32),
                ],
                axis=1,
            )
            turn = (place(WTOK - 1) - place(j)) % 384
            result = result + (pltpu.roll(row, turn, 1) if turn else row)
        per = VEC // ROWS
        block_s[tile_of(VEC_TILE)] = jnp.concatenate(
            [
                jnp.concatenate([flat[:, per * k : per * k + per] for k in range(ROWS)], axis=0),
                jnp.zeros((ROWS, 128 - per), F32),
            ],
            axis=1,
        )
        count = TABLE_LANES
        block_s[tile_of(SIDE_TILE)] = jnp.concatenate(
            [
                jnp.concatenate([result[:, count * n : count * n + count] for n in range(4)], axis=0),
                jnp.zeros((ROWS, 128 - count), F32),
            ],
            axis=1,
        )
        for number in range(SIDE_TILE + 1, BLOCK[0] * BLOCK_TILES):
            block_s[tile_of(number)] = jnp.zeros((ROWS, 128), F32)
        for outer in range(OUTER):
            for inner in range(INNER):
                k = inner * OUTER + lax.bitwise_xor(my_skip, outer)
                rows = pl.ds(pl.multiple_of(k * BLOCK[0], BLOCK[0]), BLOCK[0])
                for n in range(BLOCK_TILES):
                    grad_packs[outer][inner, :, 128 * n : 128 * n + 128] = block_s[
                        n, rows, :
                    ].astype(BF)
        for n in range(skip_count):
            grad_picks[n][...] = pick_s[n]


def layer_call(skip_count, chosen, extents, here, ranks, dec, cot, bias, packs, pieces):
    tokens = dec.shape[1]
    windows = tokens // WTOK
    steps = tokens // T
    share = tokens // skip_count
    block = pl.BlockSpec((C, T), lambda i: (0, i))
    smem = pl.BlockSpec(memory_space=pltpu.SMEM)
    hbm = pl.BlockSpec(memory_space=pltpu.HBM)

    def whole(shape):
        return pl.BlockSpec(shape, lambda i: (0,) * len(shape))

    scratch = [
        ((skip_count, C, share), BF),
        ((2, 8 * WTOK, 128), F32),
        ((VEC, 128), F32),
        ((C, C), BF),
        ((C, C), BF),
        ((C, 2 * C), BF),
        ((2 * C, C), BF),
        ((C, C), BF),
        ((C, C), BF),
        ((C, HIDDEN_SIZE), BF),
        ((HIDDEN_SIZE, C), BF),
        ((HIDDEN_SIZE, C), BF),
        ((C, HIDDEN_SIZE), BF),
        ((C + 16, T), BF),
        ((C + 16, T), BF),
        ((C + 16, T), BF),
        ((C + 16, T), BF),
        ((HIDDEN_SIZE + 16, T), BF),
        ((HIDDEN_SIZE, T), BF),
        ((C, T), BF),
        ((GROUPS * HEADS, GWIN * HEAD_DIM, GROUP), BF),
        ((GROUPS * HEADS, GWIN * HEAD_DIM, WTOK), BF),
        ((GROUPS * HEADS, GWIN * HEAD_DIM, WTOK), BF),
        ((GROUPS * HEADS, WTOK, GWIN * HEAD_DIM), BF),
        ((GROUPS * HEADS, WTOK, GWIN * HEAD_DIM), BF),
        ((GROUPS * HEADS, WTOK, GROUP), F32),
        ((GROUPS * HEADS, WTOK, GROUP), BF),
        ((GROUPS * HEADS, WTOK, GROUP), BF),
        ((C, T), BF),
        ((C, T), BF),
        ((C, T), BF),
        ((T // 128, HIDDEN_SIZE, 128), F32),
        ((T // 128, HIDDEN_SIZE, 128), F32),
        ((C, T), F32),
        ((C, T), F32),
        ((C, T), BF),
        ((2 * C, T), BF),
        ((C, T), F32),
        ((C, T), F32),
        ((C, T), F32),
        ((C, T), F32),
        ((HEADS, WTOK, 128), F32),
        ((2, C + 16, 128), F32),
        ((2 * C, C + 16), F32),
        ((2, C + 16, 128), F32),
        ((HIDDEN_SIZE, C + 16), F32),
        ((2, HIDDEN_SIZE + 16, 128), F32),
        ((4, C, 128), F32),
    ]
    flops = 2 * tokens * (3 * 442368 + 12 * WTOK * C)
    return pl.pallas_call(
        functools.partial(layer_kernel, skip_count, windows, len(pieces)),
        grid=(steps,),
        in_specs=[smem, smem, smem, smem, hbm, hbm, whole(bias.shape)]
        + [pl.BlockSpec(memory_space=pl.ANY)] * (OUTER + len(pieces)),
        out_specs=[block, block, whole((ROWS, 128))]
        + [whole((C, share))] * skip_count
        + [whole((INNER, *BLOCK))] * OUTER,
        out_shape=[
            jax.ShapeDtypeStruct((C, tokens), BF),
            jax.ShapeDtypeStruct((C, tokens), F32),
            jax.ShapeDtypeStruct((ROWS, 128), jnp.int32),
        ]
        + [jax.ShapeDtypeStruct((C, share), BF)] * skip_count
        + [jax.ShapeDtypeStruct((INNER, *BLOCK), BF)] * OUTER,
        scratch_shapes=[pltpu.VMEM(shape, kind) for shape, kind in scratch]
        + [
            pltpu.VMEM((C, skip_count * tokens), BF),
            pltpu.SemaphoreType.DMA((len(pieces),)),
            pltpu.VMEM((steps, C, T), BF),
            pltpu.VMEM((steps, C, T), BF),
            pltpu.SemaphoreType.DMA((2 * steps,)),
            pltpu.VMEM((OUTER, INNER, *BLOCK), BF),
            pltpu.SemaphoreType.DMA((OUTER,)),
        ],
        compiler_params=pltpu.CompilerParams(
            dimension_semantics=("arbitrary",), vmem_limit_bytes=42 * 1024 * 1024
        ),
        cost_estimate=pl.CostEstimate(
            flops=flops, bytes_accessed=8_000_000, transcendentals=tokens * 1200
        ),
        name="layer",
    )(
        kept(chosen),
        extents,
        here,
        ranks,
        kept(dec),
        kept(cot),
        bias,
        *packs,
        kept(pieces[0]),
        *[pltpu.with_memory_space_constraint(piece, pltpu.VMEM) for piece in pieces[1:]],
    )


def pack_kernel(mat, vec, chosen, out):
    flat = jnp.concatenate(
        [
            mat[...],
            vec[...],
            jnp.zeros((1, 128 - vec.shape[1]), F32),
            chosen[...].astype(F32),
            jnp.zeros((1, BLOCK[0] * BLOCK[1] - 128 * SIDE_TILE - chosen.shape[1]), F32),
        ],
        axis=1,
    )
    block = jnp.concatenate(
        [flat[:, BLOCK[1] * j : BLOCK[1] * (j + 1)] for j in range(BLOCK[0])], axis=0
    ).astype(BF)
    for n in range(INNER):
        out[n] = block


def skip_sum_kernel(*refs):
    blocks, out = refs[:-1], refs[-1]
    for n in range(INNER):
        out[n] = sum(block[n].astype(F32) for block in blocks).astype(BF)


def split_kernel(here, *refs):
    blocks, (keep, send) = refs[:-2], refs[-2:]
    for n in range(INNER // 2):
        for odd, out in enumerate((keep, send)):
            at = lax.bitwise_xor(here[3], 2 * n + odd)
            out[n] = sum(block[at].astype(F32) for block in blocks).astype(out.dtype)


def halve_kernel(kept, came, keep, send):
    for n in range(kept.shape[0] // 2):
        keep[n] = kept[2 * n] + came[2 * n].astype(F32)
        send[n] = (kept[2 * n + 1] + came[2 * n + 1].astype(F32)).astype(BF)


def slab_sum_kernel(kept, came, mat, vec, tail):
    total = kept[0] + came[0].astype(F32)
    squares = jnp.sum(jnp.sum(total * total, axis=1, keepdims=True), axis=0, keepdims=True)
    flat = jnp.concatenate([total[j : j + 1, :] for j in range(BLOCK[0])], axis=1)
    mat[...] = flat[:, 0 : mat.shape[1]]
    vec[...] = flat[:, 128 * VEC_TILE : 128 * VEC_TILE + vec.shape[1]]
    side = flat[:, 128 * SIDE_TILE : 128 * SIDE_TILE + 128]
    side = jnp.where(iota((1, 128), 1) == TABLE_LANES, squares, side)
    tail[...] = jnp.broadcast_to(side, tail.shape)


def return_kernel(windows, row, here, everyone, after, *refs):
    del after
    received, (out, gathered, source) = refs[:-3], refs[-3:]
    skip_count = len(received)
    per = windows // skip_count
    mix = here[1]
    for d in range(skip_count):
        gathered[d] = received[d][...]
        s = lax.bitwise_xor(mix, d)

        def note(w, rank):
            a = everyone[here[3] * row + s, w]
            mine = lax.div(a, windows) == here[2]

            @pl.when(mine)
            def _():
                source[lax.rem(a, windows)] = d * per + rank

            return rank + mine.astype(jnp.int32)

        lax.fori_loop(0, windows, note, 0)
    left = iota((1, 128), 1) < WTOK
    for n in range(windows // 2):
        halves = []
        for w in (0, 1):
            place_in = source[2 * n + w]
            d, rank = lax.div(place_in, per), lax.rem(place_in, per)
            lanes = pl.ds(pl.multiple_of((rank >> 1) * 128, 128), 128)
            block = gathered[d, :, lanes].astype(F32)
            halves.append(pltpu.roll(block, ((rank + w) & 1) * WTOK, 1))
        out[:, 128 * n : 128 * n + 128] = jnp.where(left, halves[0], halves[1])


VMEM = pl.BlockSpec(memory_space=pltpu.VMEM)
SMEM = pl.BlockSpec(memory_space=pltpu.SMEM)


def small_call(kernel, name, in_specs, outs, operands, scratch=(), moved=1_000_000):
    return pl.pallas_call(
        kernel,
        in_specs=in_specs,
        out_specs=[VMEM] * len(outs),
        out_shape=outs,
        scratch_shapes=scratch,
        compiler_params=pltpu.CompilerParams(vmem_limit_bytes=16 * 1024 * 1024),
        cost_estimate=pl.CostEstimate(flops=moved, bytes_accessed=moved, transcendentals=0),
        name=name,
    )(*operands)


def repack(packed, count):
    pieces, offset = [], 0
    for rows, cols in SHAPES:
        width = rows * cols // packed.shape[0]
        pieces.append(packed[:, offset : offset + width].reshape(count, -1))
        offset += width
    return jnp.concatenate(pieces, axis=1)


def padded(value, width):
    return jnp.pad(value, ((0, 0), (0, width - value.shape[1])))


def adamw_update(master, first, second, average, grad, factor, decay):
    clipped = grad * factor
    first_new = BETA_ONE * first + (1.0 - BETA_ONE) * clipped
    second_new = BETA_TWO * second + (1.0 - BETA_TWO) * clipped * clipped
    first_hat = first_new / (1.0 - BETA_ONE**STEP)
    second_hat = second_new / (1.0 - BETA_TWO**STEP)
    master_new = master - RATE * (first_hat / (jnp.sqrt(second_hat) + ADAM_EPS) + decay * master)
    average_new = EMA_RATE * average + (1.0 - EMA_RATE) * master_new
    return (clipped, master_new, first_new, second_new, average_new, master_new.astype(BF))


def update_kernel(mat_share, vec_share, tail, *refs):
    mats, vecs, tables = refs[0:4], refs[4:8], refs[8:12]
    norm_out, outs = refs[12], refs[13:]
    squares = jnp.sum(tail[:, TABLE_LANES : TABLE_LANES + 1], axis=0, keepdims=True)
    norm = jnp.sqrt(squares)
    norm_out[...] = norm
    factor = CLIP / jnp.maximum(norm, CLIP)
    table = jnp.concatenate([tail[8 * q : 8 * q + 8, 0:TABLE_LANES] for q in range(4)], axis=1)
    work = (
        (mats, mat_share[...], MATRIX_DECAY),
        (vecs, vec_share[...], 0.0),
        (tables, table[0:HEADS, 0:REL], 0.0),
    )
    for n, (group, grad, decay) in enumerate(work):
        results = adamw_update(*[ref[...] for ref in group], grad, factor, decay)
        for ref, value in zip(outs[6 * n : 6 * n + 6], results):
            ref[...] = value


def on_device(
    decoder_tokens,
    skip_tokens,
    cotangent,
    extents,
    assignment,
    mat_master,
    mat_first,
    mat_second,
    mat_average,
    vec_master,
    vec_first,
    vec_second,
    vec_average,
    table_master,
    table_first,
    table_second,
    table_average,
):
    skip_count = lax.axis_size("skip")
    slab_count = lax.axis_size("slab")
    device_count = skip_count * slab_count
    windows = assignment.shape[1]
    mat_width, vec_width = mat_master.shape[1], vec_master.shape[1]
    me = lax.axis_index("skip")
    plain = (skip_count, slab_count) == (OUTER, INNER)

    def swap(value, axis, distance):
        count = lax.axis_size(axis)
        return lax.ppermute(value, axis, [(n, n ^ distance) for n in range(count)])

    if plain:
        here = jnp.stack([me, me, me, lax.axis_index("slab")])
        (block,) = small_call(
            pack_kernel,
            "pack",
            [VMEM] * 3,
            [jax.ShapeDtypeStruct((INNER, *BLOCK), BF)],
            (kept(mat_master), kept(vec_master), kept(assignment)),
            moved=100_000,
        )
        own = lax.all_to_all(block, "slab", split_axis=0, concat_axis=0)
        across = swap(skip_tokens, "skip", 2)
        near = swap(skip_tokens, "skip", 1)
        packs_across = swap(own, "skip", 2)
        packs_across, across = lax.optimization_barrier((packs_across, across))
        packs = [own, swap(own, "skip", 1), packs_across, swap(packs_across, "skip", 1)]
        pieces = [skip_tokens, near, across, swap(across, "skip", 1)]
    else:
        zero = jnp.zeros_like(me)
        here = jnp.stack([zero, zero, me, zero])
        low = jnp.concatenate([mat_master, vec_master], axis=1).astype(BF)
        low = lax.all_gather(low, ("slab", "skip"), axis=0, tiled=True)
        vec = padded(low[:, mat_width:].reshape(ROWS, -1), 128)
        low = padded(
            jnp.concatenate([repack(low, ROWS), vec], axis=1), BLOCK[0] * BLOCK[1]
        ).reshape(INNER, OUTER, *BLOCK)
        packs = [low[:, n] for n in range(OUTER)]
        pieces = [lax.all_gather(skip_tokens, "skip", axis=0, tiled=True)]

    bias, ranks = pl.pallas_call(
        functools.partial(early_kernel, skip_count, windows),
        in_specs=[SMEM, VMEM, pl.BlockSpec(memory_space=pl.ANY)],
        out_specs=[VMEM, VMEM],
        out_shape=[
            jax.ShapeDtypeStruct((HEADS, WTOK, 128), F32),
            jax.ShapeDtypeStruct((1, 128), jnp.int32),
        ],
        scratch_shapes=[
            pltpu.VMEM((8, 384), F32),
            pltpu.VMEM((2, 8 * WTOK, 128), F32),
            pltpu.SMEM((skip_count,), jnp.int32),
        ],
        compiler_params=pltpu.CompilerParams(vmem_limit_bytes=16 * 1024 * 1024),
        cost_estimate=pl.CostEstimate(flops=100_000_000, bytes_accessed=1_000_000, transcendentals=0),
        name="early",
    )(kept(assignment[0]), kept(table_master.T), packs[0])
    layer_out, grad_decoder, everyone, *grads = layer_call(
        skip_count,
        assignment[0],
        extents,
        here,
        ranks,
        decoder_tokens.T,
        cotangent.T,
        bias,
        packs,
        [piece.T for piece in pieces],
    )
    grad_picks, grad_packs = grads[:skip_count], grads[skip_count:]

    def returned_call(here, everyone, after, received):
        (grad_skip,) = small_call(
            functools.partial(return_kernel, windows, OUTER),
            "returned",
            [SMEM, SMEM] + [VMEM] * (1 + skip_count),
            [jax.ShapeDtypeStruct((C, windows * WTOK), F32)],
            (here, everyone, after, *received),
            [
                pltpu.VMEM((skip_count, *received[0].shape), BF),
                pltpu.SMEM((windows,), jnp.int32),
            ],
            3_000_000,
        )
        return grad_skip

    shares = [
        jax.ShapeDtypeStruct((1, mat_width), F32),
        jax.ShapeDtypeStruct((1, vec_width), F32),
    ]
    if plain:
        far = swap(grad_packs[3], "skip", 1)
        near = swap(grad_packs[1], "skip", 1)
        (far,) = small_call(
            skip_sum_kernel,
            "core_sum",
            [VMEM] * 2,
            [jax.ShapeDtypeStruct((INNER, *BLOCK), BF)],
            (grad_packs[2], far),
        )
        keep, send = small_call(
            split_kernel,
            "skip_sum",
            [SMEM] + [VMEM] * 3,
            [
                jax.ShapeDtypeStruct((INNER // 2, *BLOCK), F32),
                jax.ShapeDtypeStruct((INNER // 2, *BLOCK), BF),
            ],
            (here, grad_packs[0], near, swap(far, "skip", 2)),
        )
        send, grad_picks = lax.optimization_barrier((send, grad_picks))
        received = [grad_picks[0]] + [swap(grad_picks[d], "skip", d) for d in range(1, OUTER)]
        for distance in (1, 2):
            half = keep.shape[0] // 2
            keep, send = small_call(
                halve_kernel,
                "slab_half",
                [VMEM] * 2,
                [
                    jax.ShapeDtypeStruct((half, *BLOCK), F32),
                    jax.ShapeDtypeStruct((half, *BLOCK), BF),
                ],
                (keep, swap(send, "slab", distance)),
                moved=300_000,
            )
        came, received = lax.optimization_barrier((swap(send, "slab", 4), received))
        mat_share, vec_share, tail = small_call(
            slab_sum_kernel,
            "slab_sum",
            [VMEM] * 2,
            shares + [jax.ShapeDtypeStruct((ROWS, 128), F32)],
            (keep, came),
            moved=300_000,
        )
        grad_skip = returned_call(here, everyone, vec_share, received)
        tail = lax.all_to_all(tail, ("slab", "skip"), split_axis=0, concat_axis=0, tiled=True)
        tail, grad_skip = lax.optimization_barrier((tail, grad_skip))
    else:
        received = list(
            lax.all_to_all(jnp.stack(grad_picks), "skip", split_axis=0, concat_axis=0)
        )
        everyone = lax.all_gather(assignment, "skip", axis=0, tiled=True)
        rows = jnp.stack(grad_packs, axis=1).reshape(ROWS, -1)
        start, side = 128 * VEC_TILE, 128 * SIDE_TILE
        rows = jnp.concatenate(
            [
                repack(rows, device_count),
                rows[:, start : start + VEC // ROWS].reshape(device_count, -1),
                rows[:, side : side + TABLE_LANES].reshape(device_count, -1),
            ],
            axis=1,
        )
        share = lax.psum_scatter(
            rows.astype(F32), ("slab", "skip"), scatter_dimension=0, tiled=True
        )
        mat_share = share[:, :mat_width]
        vec_share = share[:, mat_width : mat_width + vec_width]
        table = lax.all_gather(
            share[:, mat_width + vec_width :], ("slab", "skip"), axis=0, tiled=True
        )
        squares = lax.psum(jnp.sum(share * share), ("slab", "skip")) * (1.0 / ROWS)
        tail = jnp.concatenate(
            [table.reshape(ROWS, TABLE_LANES), jnp.full((ROWS, 128 - TABLE_LANES), squares)],
            axis=1,
        )

    if not plain:
        grad_skip = returned_call(here, everyone, vec_share, received)
    groups = (
        (mat_master, mat_first, mat_second, mat_average),
        (vec_master, vec_first, vec_second, vec_average),
        (table_master.T, table_first.T, table_second.T, table_average.T),
    )
    kinds = [jax.ShapeDtypeStruct((1, 1), F32)]
    for group in groups:
        kinds += [jax.ShapeDtypeStruct(group[0].shape, F32)] * 5
        kinds += [jax.ShapeDtypeStruct(group[0].shape, BF)]
    outs = small_call(
        update_kernel,
        "update",
        [VMEM] * 15,
        kinds,
        (mat_share, vec_share, tail, *groups[0], *groups[1], *groups[2]),
    )
    return (
        layer_out.T,
        grad_decoder.T,
        grad_skip.T,
        outs[0].reshape(()),
        *outs[1:13],
        *[value.T for value in outs[13:]],
    )


def solution(mesh):
    split = P(("slab", "skip"), None)
    return jax.shard_map(
        on_device,
        mesh=mesh,
        in_specs=(split, split, split, P("slab"), P("slab", "skip"))
        + (split,) * 8
        + (P(),) * 4,
        out_specs=(split, split, split, P()) + (split,) * 12 + (P(),) * 6,
        check_vma=False,
    )
```

time: 506 us -> 104 us (0.21); the launches traced: 496 us -> 104 us
  waiting for transfers between devices: 141 us -> 22.9 us
  blocking collectives: 122 us -> 13.8 us
  local copies, waits for them, and re-layouts: 93.7 us -> 2.08 us
  matrix products: 81.9 us -> 0 us
  Pallas kernels: 0 us -> 42.6 us
  other arithmetic: 38.3 us -> 0.08 us
  starting transfers between devices: 0.12 us -> 21.1 us
  between operations: 19.1 us -> 1.56 us
    psum x1 -> x0, waiting for transfers between devices: 103 us -> none  [on_device(): lax.psum((grad_matrices, grad_vectors, grad_table), ('slab', 'skip'))]
    all_gather x2 -> x0, blocking collectives: 84.6 us -> none  [the longest x1 43 us: on_device(): lax.all_gather(vec_master.astype(jnp.bfloat16), ('slab', 'skip'), axis=0,...]
    dot_general x23 -> x0, matrix products: 81.9 us -> none  [the longest x1 15.4 us: on_device(): jnp.dot(hidden_norm, w_up, preferred_element_type=jnp.float32) + bias_up]
    pallas_call x0 -> x10, Pallas kernels: none -> 42.6 us  [the longest x1 33.2 us: layer_call(): pl.pallas_call(functools.partial(layer_kernel, skip_count, windows, len(p...]
    psum x1 -> x0, blocking collectives: 37.2 us -> none  [on_device(): lax.psum((grad_matrices, grad_vectors, grad_table), ('slab', 'skip'))]
    reduce_scatter x1 -> x0, waiting for transfers between devices: 36.7 us -> none  [on_device(): lax.psum_scatter(slab_grad.reshape(-1, C).astype(jnp.bfloat16), 'skip', s...]
    reshape x21 -> x0, local copies, waits for them, and re-layouts: 31.6 us -> none  [the longest x5 8.67 us: on_device(): grad_part.reshape(device_count, -1)]
    ppermute x0 -> x15, waiting for transfers between devices: none -> 20.3 us  [swap(): return lax.ppermute(value, axis, [(n, n ^ distance) for n in range(count)])]
  transfers between devices with their start and end apart: 3 -> 16, of which waited for: 2 -> 8; matrix products, arithmetic and copies ran while one was open for 10% -> 0% of each run, Pallas kernels for 0% -> 7%
where the time goes in v1:
time: 104 us
  Pallas kernels  42.6 us (41%)
  waiting for transfers between devices  22.9 us (22%)
  starting transfers between devices  21.1 us (20%)
  blocking collectives  13.8 us (13%)
  local copies, waits for them, and re-layouts  2.08 us (2%)
  between operations  1.56 us (2%)
    pallas_call x1, Pallas kernels, layer_call(): pl.pallas_call(functools.partial(layer_kernel, skip_count, windows, len(p...  33.2 us
    ppermute x15, waiting for transfers between devices, swap(): return lax.ppermute(value, axis, [(n, n ^ distance) for n in range(count)])  20.3 us
    ppermute x15, starting transfers between devices, swap(): return lax.ppermute(value, axis, [(n, n ^ distance) for n in range(count)])  14.9 us
    all_to_all x1, blocking collectives, on_device(): own = lax.all_to_all(block, 'slab', split_axis=0, concat_axis=0)  13.8 us
    pallas_call x8, Pallas kernels, small_call(): pl.pallas_call(kernel, in_specs=in_specs, out_specs=[VMEM] * len(outs), o...  7.75 us
    all_to_all x1, starting transfers between devices, on_device(): lax.all_to_all(tail, ('slab', 'skip'), split_axis=0, concat_axis=0, tiled...  6.26 us
    all_to_all x1, waiting for transfers between devices, on_device(): lax.all_to_all(tail, ('slab', 'skip'), split_axis=0, concat_axis=0, tiled...  2.56 us
    unnamed x28, local copies, waits for them, and re-layouts  2.08 us
  transfers between devices with their start and end apart: 16, of which 8 were waited for; matrix products, arithmetic and copies ran while one was open for 0% of the time, Pallas kernels for 7%

profile of v1, /device:TPU:0, one launch (start us, length us, event | category | flops | bytes accessed | tf_op | source)
XLA Modules:
  0.0 104.1 jit_solution(6843298129486902092)
XLA Ops:
  0.7 3.0 %collective-permute-start.2 = (bf16[2048,192]{0,1:T(8,128)(2,1)}, bf16[2048,192]{0,1:T(8,128)(2,1)S(1)}, u32[]{:S(2)}, u32[]{:S(2)}) collective-permute-start(bf16[2048,192]{0,1:T(8,128)(2,1)} %param.18), channel_id=1, source_target_pairs={{0,2},{1,3},{2,0},{3,1},{4,6},{5,7},{6,4},{7,5},{8,10},{9,11},{10,... | collective-permute-start | bytes 2359304 | tf_op jit(solution)/shard_map/ppermute | solution.py:948
  3.7 0.9 pack.1
  4.6 13.8 %all_to_all.17.after.refs_0_ = bf16[8,16,896]{2,1,0:T(8,128)(2,1)S(1)} all-to-all(bf16[8,16,896]{2,1,0:T(8,128)(2,1)S(1)} %pack.1), channel_id=1, replica_groups=mesh['slab'=8,'skip'=4] {'slab'}, dimensions={0} | all-to-all | bytes 458752 | tf_op jit(solution)/shard_map/all_to_all | solution.py:960
  18.8 7.5 %collective-permute-done.1.refs_2_ = bf16[8,16,896]{2,1,0:T(8,128)(2,1)S(1)} collective-permute-done((bf16[8,16,896]{2,1,0:T(8,128)(2,1)S(1)}, bf16[8,16,896]{2,1,0:T(8,128)(2,1)S(1)}, u32[]{:S(2)}, u32[]{:S(2)}) %collective-permute-start.1) | collective-permute-done | bytes 229408 | tf_op jit(solution)/shard_map/ppermute | solution.py:948
  27.6 1.7 %early.1 = (f32[6,64,128]{2,1,0:T(8,128)S(1)}, s32[1,128]{1,0:T(1,128)S(1)}) custom-call(s32[32]{0:T(128)} %bitcast.37, f32[6,343]{1,0:T(8,128)} %bitcast.28, bf16[8,16,896]{2,1,0:T(8,128)(2,1)S(1)} %all_to_all.17.after.refs_0_), custom_call_target="tpu_custom_call" | custom-call | flops 100000000 | bytes 1000000 | tf_op jit(solution)/shard_map/early/pallas_call | solution.py:979
  29.3 0.9 copy-done.12
  30.2 1.1 %copy-done.13 = bf16[2048,192]{0,1:T(8,128)(2,1)S(1)} copy-done((bf16[2048,192]{0,1:T(8,128)(2,1)S(1)}, bf16[2048,192]{0,1:T(8,128)(2,1)}, u32[]{:S(2)}) %copy-start.13) | copy-done | bytes 786456
  31.3 33.2 %layer.1 = (bf16[192,2048]{1,0:T(8,128)(2,1)}, f32[192,2048]{1,0:T(8,128)}, s32[32,128]{1,0:T(8,128)S(1)}, bf16[192,512]{1,0:T(8,128)(2,1)S(1)}, bf16[192,512]{1...) custom-call(s32[32]{0:T(128)} %bitcast.38, ...), custom_call_target="tpu_custom_call" | custom-call | flops 6039797760 | bytes 8000000 | tf_op jit(solution)/shard_map/layer/pallas_call | solution.py:731
  65.2 1.0 collective-permute-done.7.refs_1_
  66.3 1.8 %collective-permute-start.8 = (bf16[8,16,896]{2,1,0:T(8,128)(2,1)S(1)}, bf16[8,16,896]{2,1,0:T(8,128)(2,1)S(1)}, u32[]{:S(2)}, u32[]{:S(2)}) collective-permute-start(bf16[8,16,896]{2,1,0:T(8,128)(2,1)S(1)} %core_sum.1), channel_id=1, source_target_pairs={{0,2},{1,3},{2,0},{3,1},{4,6},{5,7},{6,4},{7,5},{8,10},{9,11},{10,... | collective-permute-start | bytes 688136 | tf_op jit(solution)/shard_map/ppermute | solution.py:948
  68.1 6.1 %collective-permute-done.8.refs_2_ = bf16[8,16,896]{2,1,0:T(8,128)(2,1)S(1)} collective-permute-done((bf16[8,16,896]{2,1,0:T(8,128)(2,1)S(1)}, bf16[8,16,896]{2,1,0:T(8,128)(2,1)S(1)}, u32[]{:S(2)}, u32[]{:S(2)}) %collective-permute-start.8) | collective-permute-done | bytes 229408 | tf_op jit(solution)/shard_map/ppermute | solution.py:948
  75.0 1.8 %collective-permute-start.9 = (bf16[4,16,896]{2,1,0:T(8,128)(2,1)S(1)}, bf16[4,16,896]{2,1,0:T(8,128)(2,1)S(1)}, u32[]{:S(2)}, u32[]{:S(2)}) collective-permute-start(bf16[4,16,896]{2,1,0:T(8,128)(2,1)S(1)} %get-tuple-element.93), channel_id=1, source_target_pairs={{0,4},{4,0},{8,12},{12,8},{16,20},{20,16},{24,28},{28,24},{1,5},{5... | collective-permute-start | bytes 344072 | tf_op jit(solution)/shard_map/ppermute | solution.py:948
  76.8 1.5 %collective-permute-start.13 = (bf16[192,512]{1,0:T(8,128)(2,1)S(1)}, bf16[192,512]{1,0:T(8,128)(2,1)S(1)}, u32[]{:S(2)}, u32[]{:S(2)}) collective-permute-start(bf16[192,512]{1,0:T(8,128)(2,1)S(1)} %get-tuple-element.100), channel_id=1, source_target_pairs={{0,2},{1,3},{2,0},{3,1},{4,6},{5,7},{6,4},{7,5},{8,10},{9,11},{10,... | collective-permute-start | bytes 589832 | tf_op jit(solution)/shard_map/ppermute | solution.py:948
  78.6 1.2 %collective-permute-done.9.came = bf16[4,16,896]{2,1,0:T(8,128)(2,1)S(1)} collective-permute-done((bf16[4,16,896]{2,1,0:T(8,128)(2,1)S(1)}, bf16[4,16,896]{2,1,0:T(8,128)(2,1)S(1)}, u32[]{:S(2)}, u32[]{:S(2)}) %collective-permute-start.9) | collective-permute-done | bytes 114720 | tf_op jit(solution)/shard_map/ppermute | solution.py:948
  79.9 1.9 %collective-permute-start.10 = (bf16[2,16,896]{2,1,0:T(8,128)(2,1)S(1)}, bf16[2,16,896]{2,1,0:T(8,128)(2,1)S(1)}, u32[]{:S(2)}, u32[]{:S(2)}) collective-permute-start(bf16[2,16,896]{2,1,0:T(8,128)(2,1)S(1)} %get-tuple-element.95), channel_id=1, source_target_pairs={{0,8},{4,12},{8,0},{12,4},{16,24},{20,28},{24,16},{28,20},{1,9},{5... | collective-permute-start | bytes 172040 | tf_op jit(solution)/shard_map/ppermute | solution.py:948
  81.8 2.4 %collective-permute-done.10.came = bf16[2,16,896]{2,1,0:T(8,128)(2,1)S(1)} collective-permute-done((bf16[2,16,896]{2,1,0:T(8,128)(2,1)S(1)}, bf16[2,16,896]{2,1,0:T(8,128)(2,1)S(1)}, u32[]{:S(2)}, u32[]{:S(2)}) %collective-permute-start.10) | collective-permute-done | bytes 57376 | tf_op jit(solution)/shard_map/ppermute | solution.py:948
  84.2 2.9 %collective-permute-start.11 = (bf16[1,16,896]{2,1,0:T(8,128)(2,1)S(1)}, bf16[1,16,896]{2,1,0:T(8,128)(2,1)S(1)}, u32[]{:S(2)}, u32[]{:S(2)}) collective-permute-start(bf16[1,16,896]{2,1,0:T(8,128)(2,1)S(1)} %get-tuple-element.97), channel_id=1, source_target_pairs={{0,16},{4,20},{8,24},{12,28},{16,0},{20,4},{24,8},{28,12},{1,17},{... | collective-permute-start | bytes 86024 | tf_op jit(solution)/shard_map/ppermute | solution.py:948
  87.0 0.9 collective-permute-done.14.refs_3_
  87.9 1.1 %collective-permute-done.11.came = bf16[1,16,896]{2,1,0:T(8,128)(2,1)S(1)} collective-permute-done((bf16[1,16,896]{2,1,0:T(8,128)(2,1)S(1)}, bf16[1,16,896]{2,1,0:T(8,128)(2,1)S(1)}, u32[]{:S(2)}, u32[]{:S(2)}) %collective-permute-start.11) | collective-permute-done | bytes 28704 | tf_op jit(solution)/shard_map/ppermute | solution.py:948
  89.0 0.7 slab_sum.1
  89.7 6.3 %all-to-all-start.1 = ((f32[32,1,128]{2,1,0:T(1,128)}), f32[32,1,128]{2,1,0:T(1,128)S(1)}, u32[]{:S(2)}, u32[]{:S(2)}) async-start(f32[32,1,128]{2,1,0:T(1,128)} %bitcast.13), calls=%async_computation.1 | async-start | bytes 32768 | tf_op jit(solution)/shard_map/all_to_all | solution.py:1074
  96.0 4.5 %returned.1 = f32[192,2048]{1,0:T(8,128)} custom-call(s32[4]{0:T(128)S(1)} %pad_add_fusion.here, s32[32,128]{1,0:T(8,128)S(1)} %get-tuple-element.104.everyone, f32[1,72]{1,0:T(1,128)S(1)} %get-tuple-element.105.after.vec_share, bf16[192,512]{1,0:T(8,128)(2,1)S(1)} %get-tuple-element.106.refs_0_, bf16[192,512]{1,0:T(8,128)(2,1)S(1)} %collective-permute-done.12.refs_1_, ...), custom_call_target="tpu_custom_call" | custom-call | flops 3000000 | bytes 3000000 | tf_op jit(solution)/shard_map/returned/pallas_call | solution.py:864
  100.5 2.6 %all-to-all-done.1 = f32[32,1,128]{2,1,0:T(1,128)S(1)} async-done(((f32[32,1,128]{2,1,0:T(1,128)}), f32[32,1,128]{2,1,0:T(1,128)S(1)}, u32[]{:S(2)}, u32[]{:S(2)}) %all-to-all-start.1) | async-done | bytes 16416 | tf_op jit(solution)/shard_map/all_to_all | solution.py:1074
  103.1 0.9 update.1
  (48 shorter events, 2.9 us)
Async XLA Ops:
  0.7 25.7 %collective-permute-start.2 = (bf16[2048,192]{0,1:T(8,128)(2,1)}, bf16[2048,192]{0,1:T(8,128)(2,1)S(1)}, u32[]{:S(2)}, u32[]{:S(2)}) collective-permute-start(bf16[2048,192]{0,1:T(8,128)(2,1)} %param.18), channel_id=1, source_target_pairs={{0,2},{1,3},{2,0},{3,1},{4,6},{5,7},{6,4},{7,5},{8,10},{9,11},{10,... | collective-permute-start | bytes 2359304 | tf_op jit(solution)/shard_map/ppermute | solution.py:948
  18.3 8.0 %collective-permute-start.1 = (bf16[8,16,896]{2,1,0:T(8,128)(2,1)S(1)}, bf16[8,16,896]{2,1,0:T(8,128)(2,1)S(1)}, u32[]{:S(2)}, u32[]{:S(2)}) collective-permute-start(bf16[8,16,896]{2,1,0:T(8,128)(2,1)S(1)} %all_to_all.17.after.refs_0_), channel_id=1, source_target_pairs={{0,2},{1,3},{2,0},{3,1},{4,6},{5,7},{6,4},{7,5},{8,10},{9,11},{10,... | collective-permute-start | bytes 688136 | tf_op jit(solution)/shard_map/ppermute | solution.py:948
  18.8 10.5 %collective-permute-start.4 = (bf16[2048,192]{0,1:T(8,128)(2,1)}, bf16[2048,192]{0,1:T(8,128)(2,1)S(1)}, u32[]{:S(2)}, u32[]{:S(2)}) collective-permute-start(bf16[2048,192]{0,1:T(8,128)(2,1)} %param.18), channel_id=1, source_target_pairs={{0,1},{1,0},{2,3},{3,2},{4,5},{5,4},{6,7},{7,6},{8,9},{9,8},{10,11... | collective-permute-start | bytes 2359304 | tf_op jit(solution)/shard_map/ppermute | solution.py:948
  26.4 2.9 %collective-permute-start.5 = (bf16[2048,192]{0,1:T(8,128)(2,1)S(1)}, bf16[2048,192]{0,1:T(8,128)(2,1)S(1)}, u32[]{:S(2)}, u32[]{:S(2)}) collective-permute-start(bf16[2048,192]{0,1:T(8,128)(2,1)S(1)} %collective-permute-done.2), channel_id=1, source_target_pairs={{0,1},{1,0},{2,3},{3,2},{4,5},{5,4},{6,7},{7,6},{8,9},{9,8},{10,11... | collective-permute-start | bytes 2359304 | tf_op jit(solution)/shard_map/ppermute | solution.py:948
  26.4 2.9 %collective-permute-start = (bf16[8,16,896]{2,1,0:T(8,128)(2,1)S(1)}, bf16[8,16,896]{2,1,0:T(8,128)(2,1)S(1)}, u32[]{:S(2)}, u32[]{:S(2)}) collective-permute-start(bf16[8,16,896]{2,1,0:T(8,128)(2,1)S(1)} %all_to_all.17.after.refs_0_), channel_id=1, source_target_pairs={{0,1},{1,0},{2,3},{3,2},{4,5},{5,4},{6,7},{7,6},{8,9},{9,8},{10,11... | collective-permute-start | bytes 688136 | tf_op jit(solution)/shard_map/ppermute | solution.py:948
  26.9 2.4 %collective-permute-start.3 = (bf16[8,16,896]{2,1,0:T(8,128)(2,1)S(1)}, bf16[8,16,896]{2,1,0:T(8,128)(2,1)S(1)}, u32[]{:S(2)}, u32[]{:S(2)}) collective-permute-start(bf16[8,16,896]{2,1,0:T(8,128)(2,1)S(1)} %collective-permute-done.1.refs_2_), channel_id=1, source_target_pairs={{0,1},{1,0},{2,3},{3,2},{4,5},{5,4},{6,7},{7,6},{8,9},{9,8},{10,11... | collective-permute-start | bytes 688136 | tf_op jit(solution)/shard_map/ppermute | solution.py:948
  64.5 1.7 %collective-permute-start.7 = (bf16[8,16,896]{2,1,0:T(8,128)(2,1)S(1)}, bf16[8,16,896]{2,1,0:T(8,128)(2,1)S(1)}, u32[]{:S(2)}, u32[]{:S(2)}) collective-permute-start(bf16[8,16,896]{2,1,0:T(8,128)(2,1)S(1)} %get-tuple-element.86), channel_id=1, source_target_pairs={{0,1},{1,0},{2,3},{3,2},{4,5},{5,4},{6,7},{7,6},{8,9},{9,8},{10,11... | collective-permute-start | bytes 688136 | tf_op jit(solution)/shard_map/ppermute | solution.py:948
  65.1 3.0 %collective-permute-start.6 = (bf16[8,16,896]{2,1,0:T(8,128)(2,1)S(1)}, bf16[8,16,896]{2,1,0:T(8,128)(2,1)S(1)}, u32[]{:S(2)}, u32[]{:S(2)}) collective-permute-start(bf16[8,16,896]{2,1,0:T(8,128)(2,1)S(1)} %get-tuple-element.84), channel_id=1, source_target_pairs={{0,1},{1,0},{2,3},{3,2},{4,5},{5,4},{6,7},{7,6},{8,9},{9,8},{10,11... | collective-permute-start | bytes 688136 | tf_op jit(solution)/shard_map/ppermute | solution.py:948
  66.3 8.0 %collective-permute-start.8 = (bf16[8,16,896]{2,1,0:T(8,128)(2,1)S(1)}, bf16[8,16,896]{2,1,0:T(8,128)(2,1)S(1)}, u32[]{:S(2)}, u32[]{:S(2)}) collective-permute-start(bf16[8,16,896]{2,1,0:T(8,128)(2,1)S(1)} %core_sum.1), channel_id=1, source_target_pairs={{0,2},{1,3},{2,0},{3,1},{4,6},{5,7},{6,4},{7,5},{8,10},{9,11},{10,... | collective-permute-start | bytes 688136 | tf_op jit(solution)/shard_map/ppermute | solution.py:948
  74.9 28.2 %copy-start = (f32[1,13824]{1,0:T(1,128)S(1)}, f32[1,13824]{1,0:T(1,128)}, u32[]{:S(2)}) copy-start(f32[1,13824]{1,0:T(1,128)} %refs_0_.1) | copy-start | bytes 165892
  74.9 28.2 %copy-start.1 = (f32[1,13824]{1,0:T(1,128)S(1)}, f32[1,13824]{1,0:T(1,128)}, u32[]{:S(2)}) copy-start(f32[1,13824]{1,0:T(1,128)} %refs_1_.1) | copy-start | bytes 165892
  74.9 28.2 %copy-start.2 = (f32[1,13824]{1,0:T(1,128)S(1)}, f32[1,13824]{1,0:T(1,128)}, u32[]{:S(2)}) copy-start(f32[1,13824]{1,0:T(1,128)} %refs_2_.1) | copy-start | bytes 165892
  74.9 28.2 %copy-start.3 = (f32[1,13824]{1,0:T(1,128)S(1)}, f32[1,13824]{1,0:T(1,128)}, u32[]{:S(2)}) copy-start(f32[1,13824]{1,0:T(1,128)} %refs_3_.1) | copy-start | bytes 165892
  74.9 28.2 %copy-start.4 = (f32[343,6]{0,1:T(8,128)S(1)}, f32[343,6]{0,1:T(8,128)}, u32[]{:S(2)}) copy-start(f32[343,6]{0,1:T(8,128)} %param.30) | copy-start | bytes 24700
  74.9 28.2 %copy-start.5 = (f32[343,6]{0,1:T(8,128)S(1)}, f32[343,6]{0,1:T(8,128)}, u32[]{:S(2)}) copy-start(f32[343,6]{0,1:T(8,128)} %param.31) | copy-start | bytes 24700
  74.9 28.2 %copy-start.6 = (f32[343,6]{0,1:T(8,128)S(1)}, f32[343,6]{0,1:T(8,128)}, u32[]{:S(2)}) copy-start(f32[343,6]{0,1:T(8,128)} %param.32) | copy-start | bytes 24700
  75.0 28.1 %copy-start.7 = (f32[343,6]{0,1:T(8,128)S(1)}, f32[343,6]{0,1:T(8,128)}, u32[]{:S(2)}) copy-start(f32[343,6]{0,1:T(8,128)} %param.33) | copy-start | bytes 24700
  75.0 4.9 %collective-permute-start.9 = (bf16[4,16,896]{2,1,0:T(8,128)(2,1)S(1)}, bf16[4,16,896]{2,1,0:T(8,128)(2,1)S(1)}, u32[]{:S(2)}, u32[]{:S(2)}) collective-permute-start(bf16[4,16,896]{2,1,0:T(8,128)(2,1)S(1)} %get-tuple-element.93), channel_id=1, source_target_pairs={{0,4},{4,0},{8,12},{12,8},{16,20},{20,16},{24,28},{28,24},{1,5},{5... | collective-permute-start | bytes 344072 | tf_op jit(solution)/shard_map/ppermute | solution.py:948
  76.8 10.2 %collective-permute-start.12 = (bf16[192,512]{1,0:T(8,128)(2,1)S(1)}, bf16[192,512]{1,0:T(8,128)(2,1)S(1)}, u32[]{:S(2)}, u32[]{:S(2)}) collective-permute-start(bf16[192,512]{1,0:T(8,128)(2,1)S(1)} %get-tuple-element.99), channel_id=1, source_target_pairs={{0,1},{1,0},{2,3},{3,2},{4,5},{5,4},{6,7},{7,6},{8,9},{9,8},{10,11... | collective-permute-start | bytes 589832 | tf_op jit(solution)/shard_map/ppermute | solution.py:948
  76.8 10.2 %collective-permute-start.13 = (bf16[192,512]{1,0:T(8,128)(2,1)S(1)}, bf16[192,512]{1,0:T(8,128)(2,1)S(1)}, u32[]{:S(2)}, u32[]{:S(2)}) collective-permute-start(bf16[192,512]{1,0:T(8,128)(2,1)S(1)} %get-tuple-element.100), channel_id=1, source_target_pairs={{0,2},{1,3},{2,0},{3,1},{4,6},{5,7},{6,4},{7,5},{8,10},{9,11},{10,... | collective-permute-start | bytes 589832 | tf_op jit(solution)/shard_map/ppermute | solution.py:948
  78.3 9.6 %collective-permute-start.14 = (bf16[192,512]{1,0:T(8,128)(2,1)S(1)}, bf16[192,512]{1,0:T(8,128)(2,1)S(1)}, u32[]{:S(2)}, u32[]{:S(2)}) collective-permute-start(bf16[192,512]{1,0:T(8,128)(2,1)S(1)} %get-tuple-element.101), channel_id=1, source_target_pairs={{0,3},{1,2},{2,1},{3,0},{4,7},{5,6},{6,5},{7,4},{8,11},{9,10},{10,... | collective-permute-start | bytes 589832 | tf_op jit(solution)/shard_map/ppermute | solution.py:948
  79.9 4.2 %collective-permute-start.10 = (bf16[2,16,896]{2,1,0:T(8,128)(2,1)S(1)}, bf16[2,16,896]{2,1,0:T(8,128)(2,1)S(1)}, u32[]{:S(2)}, u32[]{:S(2)}) collective-permute-start(bf16[2,16,896]{2,1,0:T(8,128)(2,1)S(1)} %get-tuple-element.95), channel_id=1, source_target_pairs={{0,8},{4,12},{8,0},{12,4},{16,24},{20,28},{24,16},{28,20},{1,9},{5... | collective-permute-start | bytes 172040 | tf_op jit(solution)/shard_map/ppermute | solution.py:948
  84.2 4.8 %collective-permute-start.11 = (bf16[1,16,896]{2,1,0:T(8,128)(2,1)S(1)}, bf16[1,16,896]{2,1,0:T(8,128)(2,1)S(1)}, u32[]{:S(2)}, u32[]{:S(2)}) collective-permute-start(bf16[1,16,896]{2,1,0:T(8,128)(2,1)S(1)} %get-tuple-element.97), channel_id=1, source_target_pairs={{0,16},{4,20},{8,24},{12,28},{16,0},{20,4},{24,8},{28,12},{1,17},{... | collective-permute-start | bytes 86024 | tf_op jit(solution)/shard_map/ppermute | solution.py:948
  89.7 13.3 %all-to-all-start.1 = ((f32[32,1,128]{2,1,0:T(1,128)}), f32[32,1,128]{2,1,0:T(1,128)S(1)}, u32[]{:S(2)}, u32[]{:S(2)}) async-start(f32[32,1,128]{2,1,0:T(1,128)} %bitcast.13), calls=%async_computation.1 | async-start | bytes 32768 | tf_op jit(solution)/shard_map/all_to_all | solution.py:1074
  (6 other events, 114.6 us)

commit v2 on v1

--- a/solution.py
+++ b/solution.py
@@ -770,7 +770,8 @@
         bias,
         *packs,
         kept(pieces[0]),
-        *[pltpu.with_memory_space_constraint(piece, pltpu.VMEM) for piece in pieces[1:]],
+        *pieces[1:3],
+        *[kept(piece) for piece in pieces[3:]],
     )
 
 

time: 104 us -> 102 us (0.981)
  local copies, waits for them, and re-layouts: 2.08 us -> 0.08 us
    unnamed x28 -> x24, local copies, waits for them, and re-layouts: 2.08 us -> 0.08 us
  transfers between devices with their start and end apart: 16 -> 16, of which waited for: 8 -> 9; matrix products, arithmetic and copies ran while one was open for 0% -> 0% of each run, Pallas kernels for 7% -> 7%
where the time goes in v2:
time: 102 us
  Pallas kernels  42.5 us (42%)
  waiting for transfers between devices  22.9 us (22%)
  starting transfers between devices  21.1 us (21%)
  blocking collectives  13.8 us (14%)
  between operations  1.55 us (2%)
    pallas_call x1, Pallas kernels, layer_call(): pl.pallas_call(functools.partial(layer_kernel, skip_count, windows, len(p...  33.1 us
    ppermute x15, waiting for transfers between devices, swap(): return lax.ppermute(value, axis, [(n, n ^ distance) for n in range(count)])  20.3 us
    ppermute x15, starting transfers between devices, swap(): return lax.ppermute(value, axis, [(n, n ^ distance) for n in range(count)])  14.9 us
    all_to_all x1, blocking collectives, on_device(): own = lax.all_to_all(block, 'slab', split_axis=0, concat_axis=0)  13.8 us
    pallas_call x8, Pallas kernels, small_call(): pl.pallas_call(kernel, in_specs=in_specs, out_specs=[VMEM] * len(outs), o...  7.76 us
    all_to_all x1, starting transfers between devices, on_device(): lax.all_to_all(tail, ('slab', 'skip'), split_axis=0, concat_axis=0, tiled...  6.27 us
    all_to_all x1, waiting for transfers between devices, on_device(): lax.all_to_all(tail, ('slab', 'skip'), split_axis=0, concat_axis=0, tiled...  2.56 us
  transfers between devices with their start and end apart: 16, of which 9 were waited for; matrix products, arithmetic and copies ran while one was open for 0% of the time, Pallas kernels for 7%

profile of v2, /device:TPU:0, one launch (start us, length us, event | category | flops | bytes accessed | tf_op | source)
XLA Modules:
  0.0 102.1 jit_solution(12791755829839544170)
XLA Ops:
  0.7 3.0 %collective-permute-start.2 = (bf16[2048,192]{0,1:T(8,128)(2,1)}, bf16[2048,192]{0,1:T(8,128)(2,1)S(1)}, u32[]{:S(2)}, u32[]{:S(2)}) collective-permute-start(bf16[2048,192]{0,1:T(8,128)(2,1)} %param.18), channel_id=1, source_target_pairs={{0,2},{1,3},{2,0},{3,1},{4,6},{5,7},{6,4},{7,5},{8,10},{9,11},{10,... | collective-permute-start | bytes 2359304 | tf_op jit(solution)/shard_map/ppermute | solution.py:949
  3.7 0.9 pack.1
  4.6 13.8 %all_to_all.17.after.refs_0_ = bf16[8,16,896]{2,1,0:T(8,128)(2,1)S(1)} all-to-all(bf16[8,16,896]{2,1,0:T(8,128)(2,1)S(1)} %pack.1), channel_id=1, replica_groups=mesh['slab'=8,'skip'=4] {'slab'}, dimensions={0} | all-to-all | bytes 458752 | tf_op jit(solution)/shard_map/all_to_all | solution.py:961
  18.8 7.5 %collective-permute-done.1.refs_2_ = bf16[8,16,896]{2,1,0:T(8,128)(2,1)S(1)} collective-permute-done((bf16[8,16,896]{2,1,0:T(8,128)(2,1)S(1)}, bf16[8,16,896]{2,1,0:T(8,128)(2,1)S(1)}, u32[]{:S(2)}, u32[]{:S(2)}) %collective-permute-start.1) | collective-permute-done | bytes 229408 | tf_op jit(solution)/shard_map/ppermute | solution.py:949
  26.4 0.5 collective-permute-start
  27.6 1.7 %early.1 = (f32[6,64,128]{2,1,0:T(8,128)S(1)}, s32[1,128]{1,0:T(1,128)S(1)}) custom-call(s32[32]{0:T(128)} %bitcast.36, f32[6,343]{1,0:T(8,128)} %bitcast.28, bf16[8,16,896]{2,1,0:T(8,128)(2,1)S(1)} %all_to_all.17.after.refs_0_), custom_call_target="tpu_custom_call" | custom-call | flops 100000000 | bytes 1000000 | tf_op jit(solution)/shard_map/early/pallas_call | solution.py:980
  29.4 33.1 %layer.1 = (bf16[192,2048]{1,0:T(8,128)(2,1)}, f32[192,2048]{1,0:T(8,128)}, s32[32,128]{1,0:T(8,128)S(1)}, bf16[192,512]{1,0:T(8,128)(2,1)S(1)}, bf16[192,512]{1...) custom-call(s32[32]{0:T(128)} %bitcast.37, ...), custom_call_target="tpu_custom_call" | custom-call | flops 6039797760 | bytes 8000000 | tf_op jit(solution)/shard_map/layer/pallas_call | solution.py:731
  63.2 1.0 %collective-permute-done.7.refs_1_ = bf16[8,16,896]{2,1,0:T(8,128)(2,1)S(1)} collective-permute-done((bf16[8,16,896]{2,1,0:T(8,128)(2,1)S(1)}, bf16[8,16,896]{2,1,0:T(8,128)(2,1)S(1)}, u32[]{:S(2)}, u32[]{:S(2)}) %collective-permute-start.7) | collective-permute-done | bytes 229408 | tf_op jit(solution)/shard_map/ppermute | solution.py:949
  64.3 1.8 %collective-permute-start.8 = (bf16[8,16,896]{2,1,0:T(8,128)(2,1)S(1)}, bf16[8,16,896]{2,1,0:T(8,128)(2,1)S(1)}, u32[]{:S(2)}, u32[]{:S(2)}) collective-permute-start(bf16[8,16,896]{2,1,0:T(8,128)(2,1)S(1)} %core_sum.1), channel_id=1, source_target_pairs={{0,2},{1,3},{2,0},{3,1},{4,6},{5,7},{6,4},{7,5},{8,10},{9,11},{10,... | collective-permute-start | bytes 688136 | tf_op jit(solution)/shard_map/ppermute | solution.py:949
  66.1 6.1 %collective-permute-done.8.refs_2_ = bf16[8,16,896]{2,1,0:T(8,128)(2,1)S(1)} collective-permute-done((bf16[8,16,896]{2,1,0:T(8,128)(2,1)S(1)}, bf16[8,16,896]{2,1,0:T(8,128)(2,1)S(1)}, u32[]{:S(2)}, u32[]{:S(2)}) %collective-permute-start.8) | collective-permute-done | bytes 229408 | tf_op jit(solution)/shard_map/ppermute | solution.py:949
  72.2 0.6 skip_sum.1
  73.0 1.8 %collective-permute-start.9 = (bf16[4,16,896]{2,1,0:T(8,128)(2,1)S(1)}, bf16[4,16,896]{2,1,0:T(8,128)(2,1)S(1)}, u32[]{:S(2)}, u32[]{:S(2)}) collective-permute-start(bf16[4,16,896]{2,1,0:T(8,128)(2,1)S(1)} %get-tuple-element.93), channel_id=1, source_target_pairs={{0,4},{4,0},{8,12},{12,8},{16,20},{20,16},{24,28},{28,24},{1,5},{5... | collective-permute-start | bytes 344072 | tf_op jit(solution)/shard_map/ppermute | solution.py:949
  74.8 1.5 %collective-permute-start.13 = (bf16[192,512]{1,0:T(8,128)(2,1)S(1)}, bf16[192,512]{1,0:T(8,128)(2,1)S(1)}, u32[]{:S(2)}, u32[]{:S(2)}) collective-permute-start(bf16[192,512]{1,0:T(8,128)(2,1)S(1)} %get-tuple-element.100), channel_id=1, source_target_pairs={{0,2},{1,3},{2,0},{3,1},{4,6},{5,7},{6,4},{7,5},{8,10},{9,11},{10,... | collective-permute-start | bytes 589832 | tf_op jit(solution)/shard_map/ppermute | solution.py:949
  76.6 1.2 %collective-permute-done.9.came = bf16[4,16,896]{2,1,0:T(8,128)(2,1)S(1)} collective-permute-done((bf16[4,16,896]{2,1,0:T(8,128)(2,1)S(1)}, bf16[4,16,896]{2,1,0:T(8,128)(2,1)S(1)}, u32[]{:S(2)}, u32[]{:S(2)}) %collective-permute-start.9) | collective-permute-done | bytes 114720 | tf_op jit(solution)/shard_map/ppermute | solution.py:949
  77.9 1.9 %collective-permute-start.10 = (bf16[2,16,896]{2,1,0:T(8,128)(2,1)S(1)}, bf16[2,16,896]{2,1,0:T(8,128)(2,1)S(1)}, u32[]{:S(2)}, u32[]{:S(2)}) collective-permute-start(bf16[2,16,896]{2,1,0:T(8,128)(2,1)S(1)} %get-tuple-element.95), channel_id=1, source_target_pairs={{0,8},{4,12},{8,0},{12,4},{16,24},{20,28},{24,16},{28,20},{1,9},{5... | collective-permute-start | bytes 172040 | tf_op jit(solution)/shard_map/ppermute | solution.py:949
  79.8 2.4 %collective-permute-done.10.came = bf16[2,16,896]{2,1,0:T(8,128)(2,1)S(1)} collective-permute-done((bf16[2,16,896]{2,1,0:T(8,128)(2,1)S(1)}, bf16[2,16,896]{2,1,0:T(8,128)(2,1)S(1)}, u32[]{:S(2)}, u32[]{:S(2)}) %collective-permute-start.10) | collective-permute-done | bytes 57376 | tf_op jit(solution)/shard_map/ppermute | solution.py:949
  82.1 2.9 %collective-permute-start.11 = (bf16[1,16,896]{2,1,0:T(8,128)(2,1)S(1)}, bf16[1,16,896]{2,1,0:T(8,128)(2,1)S(1)}, u32[]{:S(2)}, u32[]{:S(2)}) collective-permute-start(bf16[1,16,896]{2,1,0:T(8,128)(2,1)S(1)} %get-tuple-element.97), channel_id=1, source_target_pairs={{0,16},{4,20},{8,24},{12,28},{16,0},{20,4},{24,8},{28,12},{1,17},{... | collective-permute-start | bytes 86024 | tf_op jit(solution)/shard_map/ppermute | solution.py:949
  85.0 0.9 collective-permute-done.14.refs_3_
  85.9 1.1 %collective-permute-done.11.came = bf16[1,16,896]{2,1,0:T(8,128)(2,1)S(1)} collective-permute-done((bf16[1,16,896]{2,1,0:T(8,128)(2,1)S(1)}, bf16[1,16,896]{2,1,0:T(8,128)(2,1)S(1)}, u32[]{:S(2)}, u32[]{:S(2)}) %collective-permute-start.11) | collective-permute-done | bytes 28704 | tf_op jit(solution)/shard_map/ppermute | solution.py:949
  87.0 0.7 slab_sum.1
  87.7 6.3 %all-to-all-start.1 = ((f32[32,1,128]{2,1,0:T(1,128)}), f32[32,1,128]{2,1,0:T(1,128)S(1)}, u32[]{:S(2)}, u32[]{:S(2)}) async-start(f32[32,1,128]{2,1,0:T(1,128)} %bitcast.13), calls=%async_computation.1 | async-start | bytes 32768 | tf_op jit(solution)/shard_map/all_to_all | solution.py:1075
  94.0 4.5 %returned.1 = f32[192,2048]{1,0:T(8,128)} custom-call(s32[4]{0:T(128)S(1)} %pad_add_fusion.here, s32[32,128]{1,0:T(8,128)S(1)} %get-tuple-element.104.everyone, f32[1,72]{1,0:T(1,128)S(1)} %get-tuple-element.105.after.vec_share, bf16[192,512]{1,0:T(8,128)(2,1)S(1)} %get-tuple-element.106.refs_0_, bf16[192,512]{1,0:T(8,128)(2,1)S(1)} %collective-permute-done.12.refs_1_, ...), custom_call_target="tpu_custom_call" | custom-call | flops 3000000 | bytes 3000000 | tf_op jit(solution)/shard_map/returned/pallas_call | solution.py:865
  98.5 2.6 %all-to-all-done.1 = f32[32,1,128]{2,1,0:T(1,128)S(1)} async-done(((f32[32,1,128]{2,1,0:T(1,128)}), f32[32,1,128]{2,1,0:T(1,128)S(1)}, u32[]{:S(2)}, u32[]{:S(2)}) %all-to-all-start.1) | async-done | bytes 16416 | tf_op jit(solution)/shard_map/all_to_all | solution.py:1075
  101.1 0.9 update.1
  (44 shorter events, 1.8 us)
Async XLA Ops:
  0.7 25.7 %collective-permute-start.2 = (bf16[2048,192]{0,1:T(8,128)(2,1)}, bf16[2048,192]{0,1:T(8,128)(2,1)S(1)}, u32[]{:S(2)}, u32[]{:S(2)}) collective-permute-start(bf16[2048,192]{0,1:T(8,128)(2,1)} %param.18), channel_id=1, source_target_pairs={{0,2},{1,3},{2,0},{3,1},{4,6},{5,7},{6,4},{7,5},{8,10},{9,11},{10,... | collective-permute-start | bytes 2359304 | tf_op jit(solution)/shard_map/ppermute | solution.py:949
  18.3 8.0 %collective-permute-start.1 = (bf16[8,16,896]{2,1,0:T(8,128)(2,1)S(1)}, bf16[8,16,896]{2,1,0:T(8,128)(2,1)S(1)}, u32[]{:S(2)}, u32[]{:S(2)}) collective-permute-start(bf16[8,16,896]{2,1,0:T(8,128)(2,1)S(1)} %all_to_all.17.after.refs_0_), channel_id=1, source_target_pairs={{0,2},{1,3},{2,0},{3,1},{4,6},{5,7},{6,4},{7,5},{8,10},{9,11},{10,... | collective-permute-start | bytes 688136 | tf_op jit(solution)/shard_map/ppermute | solution.py:949
  18.8 10.5 %collective-permute-start.4 = (bf16[2048,192]{0,1:T(8,128)(2,1)}, bf16[2048,192]{0,1:T(8,128)(2,1)S(1)}, u32[]{:S(2)}, u32[]{:S(2)}) collective-permute-start(bf16[2048,192]{0,1:T(8,128)(2,1)} %param.18), channel_id=1, source_target_pairs={{0,1},{1,0},{2,3},{3,2},{4,5},{5,4},{6,7},{7,6},{8,9},{9,8},{10,11... | collective-permute-start | bytes 2359304 | tf_op jit(solution)/shard_map/ppermute | solution.py:949
  26.4 3.1 %collective-permute-start.5 = (bf16[2048,192]{0,1:T(8,128)(2,1)S(1)}, bf16[2048,192]{0,1:T(8,128)(2,1)}, u32[]{:S(2)}, u32[]{:S(2)}) collective-permute-start(bf16[2048,192]{0,1:T(8,128)(2,1)S(1)} %collective-permute-done.2), channel_id=1, source_target_pairs={{0,1},{1,0},{2,3},{3,2},{4,5},{5,4},{6,7},{7,6},{8,9},{9,8},{10,11... | collective-permute-start | bytes 2359304 | tf_op jit(solution)/shard_map/ppermute | solution.py:949
  26.4 2.9 %collective-permute-start = (bf16[8,16,896]{2,1,0:T(8,128)(2,1)S(1)}, bf16[8,16,896]{2,1,0:T(8,128)(2,1)S(1)}, u32[]{:S(2)}, u32[]{:S(2)}) collective-permute-start(bf16[8,16,896]{2,1,0:T(8,128)(2,1)S(1)} %all_to_all.17.after.refs_0_), channel_id=1, source_target_pairs={{0,1},{1,0},{2,3},{3,2},{4,5},{5,4},{6,7},{7,6},{8,9},{9,8},{10,11... | collective-permute-start | bytes 688136 | tf_op jit(solution)/shard_map/ppermute | solution.py:949
  26.9 2.4 %collective-permute-start.3 = (bf16[8,16,896]{2,1,0:T(8,128)(2,1)S(1)}, bf16[8,16,896]{2,1,0:T(8,128)(2,1)S(1)}, u32[]{:S(2)}, u32[]{:S(2)}) collective-permute-start(bf16[8,16,896]{2,1,0:T(8,128)(2,1)S(1)} %collective-permute-done.1.refs_2_), channel_id=1, source_target_pairs={{0,1},{1,0},{2,3},{3,2},{4,5},{5,4},{6,7},{7,6},{8,9},{9,8},{10,11... | collective-permute-start | bytes 688136 | tf_op jit(solution)/shard_map/ppermute | solution.py:949
  62.6 1.6 %collective-permute-start.7 = (bf16[8,16,896]{2,1,0:T(8,128)(2,1)S(1)}, bf16[8,16,896]{2,1,0:T(8,128)(2,1)S(1)}, u32[]{:S(2)}, u32[]{:S(2)}) collective-permute-start(bf16[8,16,896]{2,1,0:T(8,128)(2,1)S(1)} %get-tuple-element.86), channel_id=1, source_target_pairs={{0,1},{1,0},{2,3},{3,2},{4,5},{5,4},{6,7},{7,6},{8,9},{9,8},{10,11... | collective-permute-start | bytes 688136 | tf_op jit(solution)/shard_map/ppermute | solution.py:949
  63.1 3.0 %collective-permute-start.6 = (bf16[8,16,896]{2,1,0:T(8,128)(2,1)S(1)}, bf16[8,16,896]{2,1,0:T(8,128)(2,1)S(1)}, u32[]{:S(2)}, u32[]{:S(2)}) collective-permute-start(bf16[8,16,896]{2,1,0:T(8,128)(2,1)S(1)} %get-tuple-element.84), channel_id=1, source_target_pairs={{0,1},{1,0},{2,3},{3,2},{4,5},{5,4},{6,7},{7,6},{8,9},{9,8},{10,11... | collective-permute-start | bytes 688136 | tf_op jit(solution)/shard_map/ppermute | solution.py:949
  64.3 7.9 %collective-permute-start.8 = (bf16[8,16,896]{2,1,0:T(8,128)(2,1)S(1)}, bf16[8,16,896]{2,1,0:T(8,128)(2,1)S(1)}, u32[]{:S(2)}, u32[]{:S(2)}) collective-permute-start(bf16[8,16,896]{2,1,0:T(8,128)(2,1)S(1)} %core_sum.1), channel_id=1, source_target_pairs={{0,2},{1,3},{2,0},{3,1},{4,6},{5,7},{6,4},{7,5},{8,10},{9,11},{10,... | collective-permute-start | bytes 688136 | tf_op jit(solution)/shard_map/ppermute | solution.py:949
  72.8 28.2 %copy-start = (f32[1,13824]{1,0:T(1,128)S(1)}, f32[1,13824]{1,0:T(1,128)}, u32[]{:S(2)}) copy-start(f32[1,13824]{1,0:T(1,128)} %refs_0_.1) | copy-start | bytes 165892
  72.9 28.2 %copy-start.1 = (f32[1,13824]{1,0:T(1,128)S(1)}, f32[1,13824]{1,0:T(1,128)}, u32[]{:S(2)}) copy-start(f32[1,13824]{1,0:T(1,128)} %refs_1_.1) | copy-start | bytes 165892
  72.9 28.2 %copy-start.2 = (f32[1,13824]{1,0:T(1,128)S(1)}, f32[1,13824]{1,0:T(1,128)}, u32[]{:S(2)}) copy-start(f32[1,13824]{1,0:T(1,128)} %refs_2_.1) | copy-start | bytes 165892
  72.9 28.2 %copy-start.3 = (f32[1,13824]{1,0:T(1,128)S(1)}, f32[1,13824]{1,0:T(1,128)}, u32[]{:S(2)}) copy-start(f32[1,13824]{1,0:T(1,128)} %refs_3_.1) | copy-start | bytes 165892
  72.9 28.2 %copy-start.4 = (f32[343,6]{0,1:T(8,128)S(1)}, f32[343,6]{0,1:T(8,128)}, u32[]{:S(2)}) copy-start(f32[343,6]{0,1:T(8,128)} %param.30) | copy-start | bytes 24700
  72.9 28.2 %copy-start.5 = (f32[343,6]{0,1:T(8,128)S(1)}, f32[343,6]{0,1:T(8,128)}, u32[]{:S(2)}) copy-start(f32[343,6]{0,1:T(8,128)} %param.31) | copy-start | bytes 24700
  72.9 28.2 %copy-start.6 = (f32[343,6]{0,1:T(8,128)S(1)}, f32[343,6]{0,1:T(8,128)}, u32[]{:S(2)}) copy-start(f32[343,6]{0,1:T(8,128)} %param.32) | copy-start | bytes 24700
  72.9 28.2 %copy-start.7 = (f32[343,6]{0,1:T(8,128)S(1)}, f32[343,6]{0,1:T(8,128)}, u32[]{:S(2)}) copy-start(f32[343,6]{0,1:T(8,128)} %param.33) | copy-start | bytes 24700
  73.0 4.9 %collective-permute-start.9 = (bf16[4,16,896]{2,1,0:T(8,128)(2,1)S(1)}, bf16[4,16,896]{2,1,0:T(8,128)(2,1)S(1)}, u32[]{:S(2)}, u32[]{:S(2)}) collective-permute-start(bf16[4,16,896]{2,1,0:T(8,128)(2,1)S(1)} %get-tuple-element.93), channel_id=1, source_target_pairs={{0,4},{4,0},{8,12},{12,8},{16,20},{20,16},{24,28},{28,24},{1,5},{5... | collective-permute-start | bytes 344072 | tf_op jit(solution)/shard_map/ppermute | solution.py:949
  74.8 10.3 %collective-permute-start.12 = (bf16[192,512]{1,0:T(8,128)(2,1)S(1)}, bf16[192,512]{1,0:T(8,128)(2,1)S(1)}, u32[]{:S(2)}, u32[]{:S(2)}) collective-permute-start(bf16[192,512]{1,0:T(8,128)(2,1)S(1)} %get-tuple-element.99), channel_id=1, source_target_pairs={{0,1},{1,0},{2,3},{3,2},{4,5},{5,4},{6,7},{7,6},{8,9},{9,8},{10,11... | collective-permute-start | bytes 589832 | tf_op jit(solution)/shard_map/ppermute | solution.py:949
  74.8 10.3 %collective-permute-start.13 = (bf16[192,512]{1,0:T(8,128)(2,1)S(1)}, bf16[192,512]{1,0:T(8,128)(2,1)S(1)}, u32[]{:S(2)}, u32[]{:S(2)}) collective-permute-start(bf16[192,512]{1,0:T(8,128)(2,1)S(1)} %get-tuple-element.100), channel_id=1, source_target_pairs={{0,2},{1,3},{2,0},{3,1},{4,6},{5,7},{6,4},{7,5},{8,10},{9,11},{10,... | collective-permute-start | bytes 589832 | tf_op jit(solution)/shard_map/ppermute | solution.py:949
  76.3 9.6 %collective-permute-start.14 = (bf16[192,512]{1,0:T(8,128)(2,1)S(1)}, bf16[192,512]{1,0:T(8,128)(2,1)S(1)}, u32[]{:S(2)}, u32[]{:S(2)}) collective-permute-start(bf16[192,512]{1,0:T(8,128)(2,1)S(1)} %get-tuple-element.101), channel_id=1, source_target_pairs={{0,3},{1,2},{2,1},{3,0},{4,7},{5,6},{6,5},{7,4},{8,11},{9,10},{10,... | collective-permute-start | bytes 589832 | tf_op jit(solution)/shard_map/ppermute | solution.py:949
  77.9 4.2 %collective-permute-start.10 = (bf16[2,16,896]{2,1,0:T(8,128)(2,1)S(1)}, bf16[2,16,896]{2,1,0:T(8,128)(2,1)S(1)}, u32[]{:S(2)}, u32[]{:S(2)}) collective-permute-start(bf16[2,16,896]{2,1,0:T(8,128)(2,1)S(1)} %get-tuple-element.95), channel_id=1, source_target_pairs={{0,8},{4,12},{8,0},{12,4},{16,24},{20,28},{24,16},{28,20},{1,9},{5... | collective-permute-start | bytes 172040 | tf_op jit(solution)/shard_map/ppermute | solution.py:949
  82.1 4.8 %collective-permute-start.11 = (bf16[1,16,896]{2,1,0:T(8,128)(2,1)S(1)}, bf16[1,16,896]{2,1,0:T(8,128)(2,1)S(1)}, u32[]{:S(2)}, u32[]{:S(2)}) collective-permute-start(bf16[1,16,896]{2,1,0:T(8,128)(2,1)S(1)} %get-tuple-element.97), channel_id=1, source_target_pairs={{0,16},{4,20},{8,24},{12,28},{16,0},{20,4},{24,8},{28,12},{1,17},{... | collective-permute-start | bytes 86024 | tf_op jit(solution)/shard_map/ppermute | solution.py:949
  87.7 13.4 %all-to-all-start.1 = ((f32[32,1,128]{2,1,0:T(1,128)}), f32[32,1,128]{2,1,0:T(1,128)S(1)}, u32[]{:S(2)}, u32[]{:S(2)}) async-start(f32[32,1,128]{2,1,0:T(1,128)} %bitcast.13), calls=%async_computation.1 | async-start | bytes 32768 | tf_op jit(solution)/shard_map/all_to_all | solution.py:1075
  (4 other events, 112.6 us)

commit v3 on v2

--- a/solution.py
+++ b/solution.py
@@ -33,6 +33,8 @@
 GWIN = GROUP // WTOK
 T = 1024
 GROUPS = T // GROUP
+WIDE = 512
+PARTS = T // WIDE
 WIN = T // WTOK
 QSCALE = HEAD_DIM ** (-0.5)
 SHAPES = ((C, C), (C, 2 * C), (C, C), (C, HIDDEN_SIZE), (HIDDEN_SIZE, C))
@@ -66,8 +68,8 @@
     return pltpu.with_memory_space_constraint(value, pltpu.HBM)
 
 
-def both(column):
-    return jnp.concatenate([column, column], axis=1)
+def both(column, width=256):
+    return jnp.concatenate([column] * (width // 128), axis=1)
 
 
 def place(slot):
@@ -304,6 +306,9 @@
 
     chunks = [slice(128 * c, 128 * c + 128) for c in range(T // 128)]
     tiles = [slice(GROUP * g, GROUP * g + GROUP) for g in range(GROUPS)]
+    wides = [slice(WIDE * g, WIDE * g + WIDE) for g in range(PARTS)]
+    per_wide = WIDE // 128
+    groups_wide = WIDE // GROUP
     layers, valid = [], []
     for c in range(len(chunks)):
         deep = [
@@ -393,8 +398,8 @@
         ds_s[n] = grad_scores
 
     def forward(g):
-        lanes = tiles[g]
-        for c in (2 * g, 2 * g + 1):
+        lanes = wides[g]
+        for c in range(per_wide * g, per_wide * (g + 1)):
             cut = chunks[c]
             hat, scale_one[c] = normed(dec[:, cut].astype(F32))
             n1_s[:, cut] = hat
@@ -412,34 +417,39 @@
             yield 160
         query = mm(wqt[...], xn_s[0:C, lanes])
         pair = mm(wkvt[...], sn_s[0:C, lanes])
-        q_s[:, lanes] = ((query + both(column(2))) * QSCALE).astype(BF)
-        for c in (2 * g, 2 * g + 1):
+        q_s[:, lanes] = ((query + both(column(2), WIDE)) * QSCALE).astype(BF)
+        for c in range(per_wide * g, per_wide * (g + 1)):
             dm_s[:, chunks[c]] = (cot[:, chunks[c]].astype(F32) * valid[c]).astype(BF)
         yield 250
-        first = g * HEADS
-        for n in range(first, first + HEADS):
+        first, units = g * groups_wide * HEADS, groups_wide * HEADS
+        for n in range(first, first + units):
             qbd_s[n] = spread(q_s[place_of(n)])
-        stacks(pair[0:C].astype(BF), g, kst_s, kcat_s)
-        yield 250
-        stacks((pair[C:] + both(column(3))).astype(BF), g, vst_s, vcat_s)
-        yield 250
-        fill = filled(g)
+        keys = pair[0:C].astype(BF)
+        values = (pair[C:] + both(column(3), WIDE)).astype(BF)
+        for k in range(groups_wide):
+            cut = slice(GROUP * k, GROUP * k + GROUP)
+            stacks(keys[:, cut], groups_wide * g + k, kst_s, kcat_s)
+            yield 250
+            stacks(values[:, cut], groups_wide * g + k, vst_s, vcat_s)
+            yield 250
         scores = {}
-        for n in range(first, first + HEADS + 2):
-            if n < first + HEADS:
+        for n in range(first, first + units + 2):
+            if n < first + units:
                 scores[n] = mm(kcat_s[n], qbd_s[n])
             if n >= first + 2:
                 o_s[place_of(n - 2)] = own(vst_s[n - 2], pb_s[n - 2]).astype(BF)
-            if first + 1 <= n <= first + HEADS:
+            if first + 1 <= n <= first + units:
+                if (n - 1) % HEADS == 0:
+                    fill = filled((n - 1) // HEADS)
                 softmax(n - 1, scores.pop(n - 1), fill)
             yield 180
         product = mm(w2[...], dm_s[:, lanes])
-        ga_s[2 * g] = product[:, 0:128]
-        ga_s[2 * g + 1] = product[:, 128:256]
+        for c in range(per_wide):
+            ga_s[per_wide * g + c] = product[:, 128 * c : 128 * c + 128]
         yield 300
         x1_s[:, lanes] = mm(wot[...], o_s[0:C, lanes])
         yield 150
-        for c in (2 * g, 2 * g + 1):
+        for c in range(per_wide * g, per_wide * (g + 1)):
             cut = chunks[c]
             middle = dec[:, cut].astype(F32) + x1_s[:, cut] + column(4)
             x1_s[:, cut] = middle
@@ -449,27 +459,27 @@
             yield 150
 
     def feed(g):
-        lanes = tiles[g]
+        lanes = wides[g]
         product = mm(w1t[...], hn_s[0:C, lanes])
-        u_s[2 * g] = product[:, 0:128]
-        u_s[2 * g + 1] = product[:, 128:256]
+        for c in range(per_wide):
+            u_s[per_wide * g + c] = product[:, 128 * c : 128 * c + 128]
         yield 300
         piece = 32
         for start in range(0, HIDDEN_SIZE, piece):
             rows = slice(start, start + piece)
-            for c in (2 * g, 2 * g + 1):
+            for c in range(per_wide * g, per_wide * (g + 1)):
                 active, slope = gelu_parts(u_s[c, rows, :] + column(7, start, start + piece))
                 gl_s[rows, chunks[c]] = active.astype(BF)
                 du_s[rows, chunks[c]] = (ga_s[c, rows, :] * slope).astype(BF)
             yield 35 * piece // 16
         gh_s[:, lanes] = mm(w1[...], du_s[:, lanes])
         yield 450
-        mlp = mm(w2t[...], gl_s[0:HIDDEN_SIZE, lanes]) + both(column(8))
+        mlp = mm(w2t[...], gl_s[0:HIDDEN_SIZE, lanes]) + both(column(8), WIDE)
         layer_out[:, lanes] = (
-            jnp.concatenate([valid[2 * g], valid[2 * g + 1]], axis=1) * (x1_s[:, lanes] + mlp)
+            jnp.concatenate(valid[per_wide * g : per_wide * (g + 1)], axis=1) * (x1_s[:, lanes] + mlp)
         ).astype(BF)
         yield 500
-        for c in (2 * g, 2 * g + 1):
+        for c in range(per_wide * g, per_wide * (g + 1)):
             cut = chunks[c]
             grad, hat = gh_s[:, cut], n3_s[:, cut]
             ln_s[2] += grad * hat
@@ -483,11 +493,12 @@
         yield 150
 
     def backward(g):
-        lanes = tiles[g]
-        first = g * HEADS
+        lanes = wides[g]
+        first, units = g * groups_wide * HEADS, groups_wide * HEADS
         spreads, grads = {}, {}
-        for n in range(first, first + HEADS + 2):
-            if n < first + HEADS:
+        for n in range(first, first + units + 2):
+            if n < first + units:
+                lanes = place_of(n)[1]
                 at, _ = place_of(n)
                 spreads[n] = spread(do_s[at, lanes])
                 grads[n] = mm(vcat_s[n], spreads[n])
@@ -496,18 +507,19 @@
                     mm_nt(spreads.pop(n), twice)
                 ).astype(BF)
             if n >= first + 2:
-                at, _ = place_of(n - 2)
+                at, lanes = place_of(n - 2)
                 dq_s[at, lanes] = own(kst_s[n - 2], ds_s[n - 2]).astype(BF)
                 twice = jnp.concatenate([ds_s[n - 2], ds_s[n - 2]], axis=0)
                 dkv_s[at, lanes] = unstack(mm_nt(qbd_s[n - 2], twice)).astype(BF)
-            if first + 1 <= n <= first + HEADS:
+            if first + 1 <= n <= first + units:
                 softmax_back(n - 1, grads.pop(n - 1))
             yield 340
+        lanes = wides[g]
         gh_s[:, lanes] = mm(wq[...], dq_s[:, lanes])
         yield 150
         gs_s[:, lanes] = mm(wkv[...], dkv_s[:, lanes])
         yield 300
-        for c in (2 * g, 2 * g + 1):
+        for c in range(per_wide * g, per_wide * (g + 1)):
             cut = chunks[c]
             grad, hat = gh_s[:, cut] * QSCALE, n1_s[:, cut]
             ln_s[0] += grad * hat
@@ -530,13 +542,14 @@
             yield 250
 
     def add(ref, product):
-        ref[0] += product[:, 0:128]
-        ref[1, :, 0 : C - 128] += product[:, 128:]
+        for n in range(ref.shape[0]):
+            width = min(128, product.shape[1] - 128 * n)
+            ref[n, :, 0:width] += product[:, 128 * n : 128 * n + width]
 
     def early_sums():
         add(a2, mm_nt(gl_s[...], dm_s[...]))
         yield 1200
-        a1[...] += mm_nt(du_s[...], hn_s[...])
+        add(a1, mm_nt(hn_s[...], du_s[...]))
         yield 1200
         add(ao, mm_nt(o_s[...], da_s[...]))
         yield 400
@@ -552,38 +565,30 @@
             except StopIteration:
                 running.remove(now)
 
-    for slot in range(GROUPS + 2):
+    for slot in range(PARTS + 2):
         parts = [
             (part, slot - lag)
             for lag, part in enumerate((forward, feed, backward))
-            if 0 <= slot - lag < GROUPS
+            if 0 <= slot - lag < PARTS
         ]
-        if slot == GROUPS + 1:
+        if slot == PARTS + 1:
             parts.append((early_sums,))
         interleaved(parts)
     add(aq, mm_nt(xn_s[...], dq_s[...]))
-    akv[...] += mm_nt(dkv_s[...], sn_s[...])
+    add(akv, mm_nt(sn_s[...], dkv_s[...]))
 
     @pl.when(step == pl.num_programs(0) - 1)
     def _():
         offset = 0
-        sums = {1: [], 3: []}
         for number, ((rows, cols), ref) in enumerate(zip(SHAPES, (aq, akv, ao, a1, a2))):
             per = rows // ROWS
             tiles = -(-cols // 128)
-            source = ref
-            if number in sums:
-                source = stage
-                for n in range(tiles):
-                    turned = jnp.transpose(ref[128 * n : 128 * n + 128, :])
-                    sums[number].append(turned[rows : rows + 1])
-                    stage[n, 0:rows, :] = turned[0:rows]
             joined = 2 if cols % 128 else 1
             for a in range(0, per, joined):
                 value = jnp.concatenate(
                     [
                         jnp.concatenate(
-                            [source[n, pl.ds(b, ROWS, stride=per), :] for n in range(tiles)], axis=1
+                            [ref[n, pl.ds(b, ROWS, stride=per), :] for n in range(tiles)], axis=1
                         )[:, 0:cols]
                         for b in range(a, a + joined)
                     ],
@@ -598,21 +603,20 @@
             offset += per * cols
         rows = [jnp.sum(jnp.transpose(ln_s[n]), axis=0, keepdims=True) for n in range(4)]
         def last_row(ref, at):
-            return jnp.concatenate(
-                [ref[0, at : at + 1, :], ref[1, at : at + 1, 0 : C - 128]], axis=1
-            )
+            row = [ref[n, at : at + 1, :] for n in range(ref.shape[0])]
+            return jnp.concatenate(row, axis=1)
 
         flat = jnp.concatenate(
             [
                 rows[0],
                 rows[1],
-                last_row(aq, C) * QSCALE,
-                jnp.concatenate(sums[1], axis=1)[:, C:],
-                last_row(ao, C),
+                last_row(aq, C)[:, 0:C] * QSCALE,
+                last_row(akv, C)[:, C:],
+                last_row(ao, C)[:, 0:C],
                 rows[2],
                 rows[3],
-                *sums[3],
-                last_row(a2, HIDDEN_SIZE),
+                last_row(a1, C),
+                last_row(a2, HIDDEN_SIZE)[:, 0:C],
             ],
             axis=1,
         )
@@ -721,9 +725,9 @@
         ((C, T), F32),
         ((HEADS, WTOK, 128), F32),
         ((2, C + 16, 128), F32),
-        ((2 * C, C + 16), F32),
+        ((3, C + 16, 128), F32),
         ((2, C + 16, 128), F32),
-        ((HIDDEN_SIZE, C + 16), F32),
+        ((6, C + 16, 128), F32),
         ((2, HIDDEN_SIZE + 16, 128), F32),
         ((4, C, 128), F32),
     ]
@@ -948,6 +952,25 @@
         count = lax.axis_size(axis)
         return lax.ppermute(value, axis, [(n, n ^ distance) for n in range(count)])
 
+    def early_call(after):
+        return pl.pallas_call(
+            functools.partial(early_kernel, skip_count, windows),
+            in_specs=[SMEM, VMEM, pl.BlockSpec(memory_space=pl.ANY)],
+            out_specs=[VMEM, VMEM],
+            out_shape=[
+                jax.ShapeDtypeStruct((HEADS, WTOK, 128), F32),
+                jax.ShapeDtypeStruct((1, 128), jnp.int32),
+            ],
+            scratch_shapes=[
+                pltpu.VMEM((8, 384), F32),
+                pltpu.VMEM((2, 8 * WTOK, 128), F32),
+                pltpu.SMEM((skip_count,), jnp.int32),
+            ],
+            compiler_params=pltpu.CompilerParams(vmem_limit_bytes=16 * 1024 * 1024),
+            cost_estimate=pl.CostEstimate(flops=100_000_000, bytes_accessed=1_000_000, transcendentals=0),
+            name="early",
+        )(kept(assignment[0]), kept(table_master.T), after)
+
     if plain:
         here = jnp.stack([me, me, me, lax.axis_index("slab")])
         (block,) = small_call(
@@ -962,7 +985,10 @@
         across = swap(skip_tokens, "skip", 2)
         near = swap(skip_tokens, "skip", 1)
         packs_across = swap(own, "skip", 2)
-        packs_across, across = lax.optimization_barrier((packs_across, across))
+        bias, ranks = early_call(own)
+        packs_across, across, bias, ranks = lax.optimization_barrier(
+            (packs_across, across, bias, ranks)
+        )
         packs = [own, swap(own, "skip", 1), packs_across, swap(packs_across, "skip", 1)]
         pieces = [skip_tokens, near, across, swap(across, "skip", 1)]
     else:
@@ -976,24 +1002,8 @@
         ).reshape(INNER, OUTER, *BLOCK)
         packs = [low[:, n] for n in range(OUTER)]
         pieces = [lax.all_gather(skip_tokens, "skip", axis=0, tiled=True)]
-
-    bias, ranks = pl.pallas_call(
-        functools.partial(early_kernel, skip_count, windows),
-        in_specs=[SMEM, VMEM, pl.BlockSpec(memory_space=pl.ANY)],
-        out_specs=[VMEM, VMEM],
-        out_shape=[
-            jax.ShapeDtypeStruct((HEADS, WTOK, 128), F32),
-            jax.ShapeDtypeStruct((1, 128), jnp.int32),
-        ],
-        scratch_shapes=[
-            pltpu.VMEM((8, 384), F32),
-            pltpu.VMEM((2, 8 * WTOK, 128), F32),
-            pltpu.SMEM((skip_count,), jnp.int32),
-        ],
-        compiler_params=pltpu.CompilerParams(vmem_limit_bytes=16 * 1024 * 1024),
-        cost_estimate=pl.CostEstimate(flops=100_000_000, bytes_accessed=1_000_000, transcendentals=0),
-        name="early",
-    )(kept(assignment[0]), kept(table_master.T), packs[0])
+        bias, ranks = early_call(packs[0])
+
     layer_out, grad_decoder, everyone, *grads = layer_call(
         skip_count,
         assignment[0],

time: 102 us -> 98.7 us (0.968)
  Pallas kernels: 42.5 us -> 39.1 us
    pallas_call x1, Pallas kernels: 33.1 us -> 29.7 us  [layer_call(): pl.pallas_call(functools.partial(layer_kernel, skip_count, windows, len(p...]
  transfers between devices with their start and end apart: 16 -> 16, of which waited for: 9 -> 11; matrix products, arithmetic and copies ran while one was open for 0% -> 0% of each run, Pallas kernels for 7% -> 7%
where the time goes in v3:
time: 98.7 us; the launch traced here: 98.4 us
  Pallas kernels  39.1 us (40%)
  waiting for transfers between devices  22.7 us (23%)
  starting transfers between devices  21.2 us (21%)
  blocking collectives  13.8 us (14%)
  between operations  1.53 us (2%)
    pallas_call x1, Pallas kernels, layer_call(): pl.pallas_call(functools.partial(layer_kernel, skip_count, windows, len(p...  29.7 us
    ppermute x15, waiting for transfers between devices, swap(): return lax.ppermute(value, axis, [(n, n ^ distance) for n in range(count)])  20.1 us
    ppermute x15, starting transfers between devices, swap(): return lax.ppermute(value, axis, [(n, n ^ distance) for n in range(count)])  14.8 us
    all_to_all x1, blocking collectives, on_device(): own = lax.all_to_all(block, 'slab', split_axis=0, concat_axis=0)  13.8 us
    pallas_call x8, Pallas kernels, small_call(): pl.pallas_call(kernel, in_specs=in_specs, out_specs=[VMEM] * len(outs), o...  7.76 us
    all_to_all x1, starting transfers between devices, on_device(): lax.all_to_all(tail, ('slab', 'skip'), split_axis=0, concat_axis=0, tiled...  6.38 us
    all_to_all x1, waiting for transfers between devices, on_device(): lax.all_to_all(tail, ('slab', 'skip'), split_axis=0, concat_axis=0, tiled...  2.56 us
  transfers between devices with their start and end apart: 16, of which 11 were waited for; matrix products, arithmetic and copies ran while one was open for 0% of the time, Pallas kernels for 7%

profile of v3, /device:TPU:0, one launch (start us, length us, event | category | flops | bytes accessed | tf_op | source)
XLA Modules:
  0.0 98.4 jit_solution(12590070293497506764)
XLA Ops:
  0.7 3.0 %collective-permute-start.1 = (bf16[2048,192]{0,1:T(8,128)(2,1)}, bf16[2048,192]{0,1:T(8,128)(2,1)S(1)}, u32[]{:S(2)}, u32[]{:S(2)}) collective-permute-start(bf16[2048,192]{0,1:T(8,128)(2,1)} %param.18), channel_id=1, source_target_pairs={{0,2},{1,3},{2,0},{3,1},{4,6},{5,7},{6,4},{7,5},{8,10},{9,11},{10,... | collective-permute-start | bytes 2359304 | tf_op jit(solution)/shard_map/ppermute | solution.py:953
  3.7 0.9 pack.1
  4.6 13.8 %all_to_all.17.after.refs_0_ = bf16[8,16,896]{2,1,0:T(8,128)(2,1)S(1)} all-to-all(bf16[8,16,896]{2,1,0:T(8,128)(2,1)S(1)} %pack.1), channel_id=1, replica_groups=mesh['slab'=8,'skip'=4] {'slab'}, dimensions={0} | all-to-all | bytes 458752 | tf_op jit(solution)/shard_map/all_to_all | solution.py:984
  18.8 1.7 %early.1 = (f32[6,64,128]{2,1,0:T(8,128)S(1)}, s32[1,128]{1,0:T(1,128)S(1)}) custom-call(s32[32]{0:T(128)} %bitcast.36, f32[6,343]{1,0:T(8,128)} %bitcast.28, bf16[8,16,896]{2,1,0:T(8,128)(2,1)S(1)} %all_to_all.17.after.refs_0_), custom_call_target="tpu_custom_call" | custom-call | flops 100000000 | bytes 1000000 | tf_op jit(solution)/shard_map/early/pallas_call | solution.py:956
  20.5 5.9 %collective-permute-done.refs_2_ = bf16[8,16,896]{2,1,0:T(8,128)(2,1)S(1)} collective-permute-done((bf16[8,16,896]{2,1,0:T(8,128)(2,1)S(1)}, bf16[8,16,896]{2,1,0:T(8,128)(2,1)S(1)}, u32[]{:S(2)}, u32[]{:S(2)}) %collective-permute-start) | collective-permute-done | bytes 229408 | tf_op jit(solution)/shard_map/ppermute | solution.py:953
  27.6 1.0 %collective-permute-done.2.refs_1_ = bf16[8,16,896]{2,1,0:T(8,128)(2,1)S(1)} collective-permute-done((bf16[8,16,896]{2,1,0:T(8,128)(2,1)S(1)}, bf16[8,16,896]{2,1,0:T(8,128)(2,1)S(1)}, u32[]{:S(2)}, u32[]{:S(2)}) %collective-permute-start.2) | collective-permute-done | bytes 229408 | tf_op jit(solution)/shard_map/ppermute | solution.py:953
  29.4 29.7 %layer.1 = (bf16[192,2048]{1,0:T(8,128)(2,1)}, f32[192,2048]{1,0:T(8,128)}, s32[32,128]{1,0:T(8,128)S(1)}, bf16[192,512]{1,0:T(8,128)(2,1)S(1)}, bf16[192,512]{1...) custom-call(s32[32]{0:T(128)} %bitcast.37, ...), custom_call_target="tpu_custom_call" | custom-call | flops 6039797760 | bytes 8000000 | tf_op jit(solution)/shard_map/layer/pallas_call | solution.py:735
  59.7 1.0 collective-permute-done.7.refs_1_
  60.7 1.8 %collective-permute-start.8 = (bf16[8,16,896]{2,1,0:T(8,128)(2,1)S(1)}, bf16[8,16,896]{2,1,0:T(8,128)(2,1)S(1)}, u32[]{:S(2)}, u32[]{:S(2)}) collective-permute-start(bf16[8,16,896]{2,1,0:T(8,128)(2,1)S(1)} %core_sum.1), channel_id=1, source_target_pairs={{0,2},{1,3},{2,0},{3,1},{4,6},{5,7},{6,4},{7,5},{8,10},{9,11},{10,... | collective-permute-start | bytes 688136 | tf_op jit(solution)/shard_map/ppermute | solution.py:953
  62.5 5.9 %collective-permute-done.8.refs_2_ = bf16[8,16,896]{2,1,0:T(8,128)(2,1)S(1)} collective-permute-done((bf16[8,16,896]{2,1,0:T(8,128)(2,1)S(1)}, bf16[8,16,896]{2,1,0:T(8,128)(2,1)S(1)}, u32[]{:S(2)}, u32[]{:S(2)}) %collective-permute-start.8) | collective-permute-done | bytes 229408 | tf_op jit(solution)/shard_map/ppermute | solution.py:953
  68.4 0.6 skip_sum.1
  69.2 1.8 %collective-permute-start.9 = (bf16[4,16,896]{2,1,0:T(8,128)(2,1)S(1)}, bf16[4,16,896]{2,1,0:T(8,128)(2,1)S(1)}, u32[]{:S(2)}, u32[]{:S(2)}) collective-permute-start(bf16[4,16,896]{2,1,0:T(8,128)(2,1)S(1)} %get-tuple-element.97), channel_id=1, source_target_pairs={{0,4},{4,0},{8,12},{12,8},{16,20},{20,16},{24,28},{28,24},{1,5},{5... | collective-permute-start | bytes 344072 | tf_op jit(solution)/shard_map/ppermute | solution.py:953
  71.0 1.5 %collective-permute-start.13 = (bf16[192,512]{1,0:T(8,128)(2,1)S(1)}, bf16[192,512]{1,0:T(8,128)(2,1)S(1)}, u32[]{:S(2)}, u32[]{:S(2)}) collective-permute-start(bf16[192,512]{1,0:T(8,128)(2,1)S(1)} %get-tuple-element.104), channel_id=1, source_target_pairs={{0,2},{1,3},{2,0},{3,1},{4,6},{5,7},{6,4},{7,5},{8,10},{9,11},{10,... | collective-permute-start | bytes 589832 | tf_op jit(solution)/shard_map/ppermute | solution.py:953
  72.9 1.2 %collective-permute-done.9.came = bf16[4,16,896]{2,1,0:T(8,128)(2,1)S(1)} collective-permute-done((bf16[4,16,896]{2,1,0:T(8,128)(2,1)S(1)}, bf16[4,16,896]{2,1,0:T(8,128)(2,1)S(1)}, u32[]{:S(2)}, u32[]{:S(2)}) %collective-permute-start.9) | collective-permute-done | bytes 114720 | tf_op jit(solution)/shard_map/ppermute | solution.py:953
  74.1 1.9 %collective-permute-start.10 = (bf16[2,16,896]{2,1,0:T(8,128)(2,1)S(1)}, bf16[2,16,896]{2,1,0:T(8,128)(2,1)S(1)}, u32[]{:S(2)}, u32[]{:S(2)}) collective-permute-start(bf16[2,16,896]{2,1,0:T(8,128)(2,1)S(1)} %get-tuple-element.99), channel_id=1, source_target_pairs={{0,8},{4,12},{8,0},{12,4},{16,24},{20,28},{24,16},{28,20},{1,9},{5... | collective-permute-start | bytes 172040 | tf_op jit(solution)/shard_map/ppermute | solution.py:953
  76.0 2.4 %collective-permute-done.10.came = bf16[2,16,896]{2,1,0:T(8,128)(2,1)S(1)} collective-permute-done((bf16[2,16,896]{2,1,0:T(8,128)(2,1)S(1)}, bf16[2,16,896]{2,1,0:T(8,128)(2,1)S(1)}, u32[]{:S(2)}, u32[]{:S(2)}) %collective-permute-start.10) | collective-permute-done | bytes 57376 | tf_op jit(solution)/shard_map/ppermute | solution.py:953
  78.4 2.9 %collective-permute-start.11 = (bf16[1,16,896]{2,1,0:T(8,128)(2,1)S(1)}, bf16[1,16,896]{2,1,0:T(8,128)(2,1)S(1)}, u32[]{:S(2)}, u32[]{:S(2)}) collective-permute-start(bf16[1,16,896]{2,1,0:T(8,128)(2,1)S(1)} %get-tuple-element.101), channel_id=1, source_target_pairs={{0,16},{4,20},{8,24},{12,28},{16,0},{20,4},{24,8},{28,12},{1,17},{... | collective-permute-start | bytes 86024 | tf_op jit(solution)/shard_map/ppermute | solution.py:953
  81.2 0.9 collective-permute-done.14.refs_3_
  82.1 1.1 %collective-permute-done.11.came = bf16[1,16,896]{2,1,0:T(8,128)(2,1)S(1)} collective-permute-done((bf16[1,16,896]{2,1,0:T(8,128)(2,1)S(1)}, bf16[1,16,896]{2,1,0:T(8,128)(2,1)S(1)}, u32[]{:S(2)}, u32[]{:S(2)}) %collective-permute-start.11) | collective-permute-done | bytes 28704 | tf_op jit(solution)/shard_map/ppermute | solution.py:953
  83.2 0.7 slab_sum.1
  83.9 6.4 %all-to-all-start.1 = ((f32[32,1,128]{2,1,0:T(1,128)}), f32[32,1,128]{2,1,0:T(1,128)S(1)}, u32[]{:S(2)}, u32[]{:S(2)}) async-start(f32[32,1,128]{2,1,0:T(1,128)} %bitcast.13), calls=%async_computation.1 | async-start | bytes 32768 | tf_op jit(solution)/shard_map/all_to_all | solution.py:1085
  90.3 4.5 %returned.1 = f32[192,2048]{1,0:T(8,128)} custom-call(s32[4]{0:T(128)S(1)} %pad_add_fusion.here, s32[32,128]{1,0:T(8,128)S(1)} %get-tuple-element.108.everyone, f32[1,72]{1,0:T(1,128)S(1)} %get-tuple-element.109.after.vec_share, bf16[192,512]{1,0:T(8,128)(2,1)S(1)} %get-tuple-element.110.refs_0_, bf16[192,512]{1,0:T(8,128)(2,1)S(1)} %collective-permute-done.12.refs_1_, ...), custom_call_target="tpu_custom_call" | custom-call | flops 3000000 | bytes 3000000 | tf_op jit(solution)/shard_map/returned/pallas_call | solution.py:869
  94.8 2.6 %all-to-all-done.1 = f32[32,1,128]{2,1,0:T(1,128)S(1)} async-done(((f32[32,1,128]{2,1,0:T(1,128)}), f32[32,1,128]{2,1,0:T(1,128)S(1)}, u32[]{:S(2)}, u32[]{:S(2)}) %all-to-all-start.1) | async-done | bytes 16416 | tf_op jit(solution)/shard_map/all_to_all | solution.py:1085
  97.5 0.9 update.1
  (44 shorter events, 3.0 us)
Async XLA Ops:
  0.7 25.7 %collective-permute-start.1 = (bf16[2048,192]{0,1:T(8,128)(2,1)}, bf16[2048,192]{0,1:T(8,128)(2,1)S(1)}, u32[]{:S(2)}, u32[]{:S(2)}) collective-permute-start(bf16[2048,192]{0,1:T(8,128)(2,1)} %param.18), channel_id=1, source_target_pairs={{0,2},{1,3},{2,0},{3,1},{4,6},{5,7},{6,4},{7,5},{8,10},{9,11},{10,... | collective-permute-start | bytes 2359304 | tf_op jit(solution)/shard_map/ppermute | solution.py:953
  18.3 8.0 %collective-permute-start = (bf16[8,16,896]{2,1,0:T(8,128)(2,1)S(1)}, bf16[8,16,896]{2,1,0:T(8,128)(2,1)S(1)}, u32[]{:S(2)}, u32[]{:S(2)}) collective-permute-start(bf16[8,16,896]{2,1,0:T(8,128)(2,1)S(1)} %all_to_all.17.after.refs_0_), channel_id=1, source_target_pairs={{0,2},{1,3},{2,0},{3,1},{4,6},{5,7},{6,4},{7,5},{8,10},{9,11},{10,... | collective-permute-start | bytes 688136 | tf_op jit(solution)/shard_map/ppermute | solution.py:953
  18.8 9.8 %collective-permute-start.4 = (bf16[2048,192]{0,1:T(8,128)(2,1)}, bf16[2048,192]{0,1:T(8,128)(2,1)S(1)}, u32[]{:S(2)}, u32[]{:S(2)}) collective-permute-start(bf16[2048,192]{0,1:T(8,128)(2,1)} %param.18), channel_id=1, source_target_pairs={{0,1},{1,0},{2,3},{3,2},{4,5},{5,4},{6,7},{7,6},{8,9},{9,8},{10,11... | collective-permute-start | bytes 2359304 | tf_op jit(solution)/shard_map/ppermute | solution.py:953
  26.4 3.1 %collective-permute-start.5 = (bf16[2048,192]{0,1:T(8,128)(2,1)S(1)}, bf16[2048,192]{0,1:T(8,128)(2,1)}, u32[]{:S(2)}, u32[]{:S(2)}) collective-permute-start(bf16[2048,192]{0,1:T(8,128)(2,1)S(1)} %collective-permute-done.1), channel_id=1, source_target_pairs={{0,1},{1,0},{2,3},{3,2},{4,5},{5,4},{6,7},{7,6},{8,9},{9,8},{10,11... | collective-permute-start | bytes 2359304 | tf_op jit(solution)/shard_map/ppermute | solution.py:953
  26.4 2.2 %collective-permute-start.2 = (bf16[8,16,896]{2,1,0:T(8,128)(2,1)S(1)}, bf16[8,16,896]{2,1,0:T(8,128)(2,1)S(1)}, u32[]{:S(2)}, u32[]{:S(2)}) collective-permute-start(bf16[8,16,896]{2,1,0:T(8,128)(2,1)S(1)} %all_to_all.17.after.refs_0_), channel_id=1, source_target_pairs={{0,1},{1,0},{2,3},{3,2},{4,5},{5,4},{6,7},{7,6},{8,9},{9,8},{10,11... | collective-permute-start | bytes 688136 | tf_op jit(solution)/shard_map/ppermute | solution.py:953
  26.9 2.1 %collective-permute-start.3 = (bf16[8,16,896]{2,1,0:T(8,128)(2,1)S(1)}, bf16[8,16,896]{2,1,0:T(8,128)(2,1)S(1)}, u32[]{:S(2)}, u32[]{:S(2)}) collective-permute-start(bf16[8,16,896]{2,1,0:T(8,128)(2,1)S(1)} %collective-permute-done.refs_2_), channel_id=1, source_target_pairs={{0,1},{1,0},{2,3},{3,2},{4,5},{5,4},{6,7},{7,6},{8,9},{9,8},{10,11... | collective-permute-start | bytes 688136 | tf_op jit(solution)/shard_map/ppermute | solution.py:953
  59.1 1.6 %collective-permute-start.7 = (bf16[8,16,896]{2,1,0:T(8,128)(2,1)S(1)}, bf16[8,16,896]{2,1,0:T(8,128)(2,1)S(1)}, u32[]{:S(2)}, u32[]{:S(2)}) collective-permute-start(bf16[8,16,896]{2,1,0:T(8,128)(2,1)S(1)} %get-tuple-element.90), channel_id=1, source_target_pairs={{0,1},{1,0},{2,3},{3,2},{4,5},{5,4},{6,7},{7,6},{8,9},{9,8},{10,11... | collective-permute-start | bytes 688136 | tf_op jit(solution)/shard_map/ppermute | solution.py:953
  59.3 3.2 %collective-permute-start.6 = (bf16[8,16,896]{2,1,0:T(8,128)(2,1)S(1)}, bf16[8,16,896]{2,1,0:T(8,128)(2,1)S(1)}, u32[]{:S(2)}, u32[]{:S(2)}) collective-permute-start(bf16[8,16,896]{2,1,0:T(8,128)(2,1)S(1)} %get-tuple-element.88), channel_id=1, source_target_pairs={{0,1},{1,0},{2,3},{3,2},{4,5},{5,4},{6,7},{7,6},{8,9},{9,8},{10,11... | collective-permute-start | bytes 688136 | tf_op jit(solution)/shard_map/ppermute | solution.py:953
  60.7 7.7 %collective-permute-start.8 = (bf16[8,16,896]{2,1,0:T(8,128)(2,1)S(1)}, bf16[8,16,896]{2,1,0:T(8,128)(2,1)S(1)}, u32[]{:S(2)}, u32[]{:S(2)}) collective-permute-start(bf16[8,16,896]{2,1,0:T(8,128)(2,1)S(1)} %core_sum.1), channel_id=1, source_target_pairs={{0,2},{1,3},{2,0},{3,1},{4,6},{5,7},{6,4},{7,5},{8,10},{9,11},{10,... | collective-permute-start | bytes 688136 | tf_op jit(solution)/shard_map/ppermute | solution.py:953
  69.1 28.3 %copy-start = (f32[1,13824]{1,0:T(1,128)S(1)}, f32[1,13824]{1,0:T(1,128)}, u32[]{:S(2)}) copy-start(f32[1,13824]{1,0:T(1,128)} %refs_0_.1) | copy-start | bytes 165892
  69.1 28.3 %copy-start.1 = (f32[1,13824]{1,0:T(1,128)S(1)}, f32[1,13824]{1,0:T(1,128)}, u32[]{:S(2)}) copy-start(f32[1,13824]{1,0:T(1,128)} %refs_1_.1) | copy-start | bytes 165892
  69.1 28.3 %copy-start.2 = (f32[1,13824]{1,0:T(1,128)S(1)}, f32[1,13824]{1,0:T(1,128)}, u32[]{:S(2)}) copy-start(f32[1,13824]{1,0:T(1,128)} %refs_2_.1) | copy-start | bytes 165892
  69.1 28.3 %copy-start.3 = (f32[1,13824]{1,0:T(1,128)S(1)}, f32[1,13824]{1,0:T(1,128)}, u32[]{:S(2)}) copy-start(f32[1,13824]{1,0:T(1,128)} %refs_3_.1) | copy-start | bytes 165892
  69.1 28.3 %copy-start.4 = (f32[343,6]{0,1:T(8,128)S(1)}, f32[343,6]{0,1:T(8,128)}, u32[]{:S(2)}) copy-start(f32[343,6]{0,1:T(8,128)} %param.30) | copy-start | bytes 24700
  69.1 28.3 %copy-start.5 = (f32[343,6]{0,1:T(8,128)S(1)}, f32[343,6]{0,1:T(8,128)}, u32[]{:S(2)}) copy-start(f32[343,6]{0,1:T(8,128)} %param.31) | copy-start | bytes 24700
  69.1 28.3 %copy-start.6 = (f32[343,6]{0,1:T(8,128)S(1)}, f32[343,6]{0,1:T(8,128)}, u32[]{:S(2)}) copy-start(f32[343,6]{0,1:T(8,128)} %param.32) | copy-start | bytes 24700
  69.2 28.3 %copy-start.7 = (f32[343,6]{0,1:T(8,128)S(1)}, f32[343,6]{0,1:T(8,128)}, u32[]{:S(2)}) copy-start(f32[343,6]{0,1:T(8,128)} %param.33) | copy-start | bytes 24700
  69.2 4.9 %collective-permute-start.9 = (bf16[4,16,896]{2,1,0:T(8,128)(2,1)S(1)}, bf16[4,16,896]{2,1,0:T(8,128)(2,1)S(1)}, u32[]{:S(2)}, u32[]{:S(2)}) collective-permute-start(bf16[4,16,896]{2,1,0:T(8,128)(2,1)S(1)} %get-tuple-element.97), channel_id=1, source_target_pairs={{0,4},{4,0},{8,12},{12,8},{16,20},{20,16},{24,28},{28,24},{1,5},{5... | collective-permute-start | bytes 344072 | tf_op jit(solution)/shard_map/ppermute | solution.py:953
  71.0 10.2 %collective-permute-start.12 = (bf16[192,512]{1,0:T(8,128)(2,1)S(1)}, bf16[192,512]{1,0:T(8,128)(2,1)S(1)}, u32[]{:S(2)}, u32[]{:S(2)}) collective-permute-start(bf16[192,512]{1,0:T(8,128)(2,1)S(1)} %get-tuple-element.103), channel_id=1, source_target_pairs={{0,1},{1,0},{2,3},{3,2},{4,5},{5,4},{6,7},{7,6},{8,9},{9,8},{10,11... | collective-permute-start | bytes 589832 | tf_op jit(solution)/shard_map/ppermute | solution.py:953
  71.0 10.2 %collective-permute-start.13 = (bf16[192,512]{1,0:T(8,128)(2,1)S(1)}, bf16[192,512]{1,0:T(8,128)(2,1)S(1)}, u32[]{:S(2)}, u32[]{:S(2)}) collective-permute-start(bf16[192,512]{1,0:T(8,128)(2,1)S(1)} %get-tuple-element.104), channel_id=1, source_target_pairs={{0,2},{1,3},{2,0},{3,1},{4,6},{5,7},{6,4},{7,5},{8,10},{9,11},{10,... | collective-permute-start | bytes 589832 | tf_op jit(solution)/shard_map/ppermute | solution.py:953
  72.5 9.6 %collective-permute-start.14 = (bf16[192,512]{1,0:T(8,128)(2,1)S(1)}, bf16[192,512]{1,0:T(8,128)(2,1)S(1)}, u32[]{:S(2)}, u32[]{:S(2)}) collective-permute-start(bf16[192,512]{1,0:T(8,128)(2,1)S(1)} %get-tuple-element.105), channel_id=1, source_target_pairs={{0,3},{1,2},{2,1},{3,0},{4,7},{5,6},{6,5},{7,4},{8,11},{9,10},{10,... | collective-permute-start | bytes 589832 | tf_op jit(solution)/shard_map/ppermute | solution.py:953
  74.1 4.2 %collective-permute-start.10 = (bf16[2,16,896]{2,1,0:T(8,128)(2,1)S(1)}, bf16[2,16,896]{2,1,0:T(8,128)(2,1)S(1)}, u32[]{:S(2)}, u32[]{:S(2)}) collective-permute-start(bf16[2,16,896]{2,1,0:T(8,128)(2,1)S(1)} %get-tuple-element.99), channel_id=1, source_target_pairs={{0,8},{4,12},{8,0},{12,4},{16,24},{20,28},{24,16},{28,20},{1,9},{5... | collective-permute-start | bytes 172040 | tf_op jit(solution)/shard_map/ppermute | solution.py:953
  78.4 4.8 %collective-permute-start.11 = (bf16[1,16,896]{2,1,0:T(8,128)(2,1)S(1)}, bf16[1,16,896]{2,1,0:T(8,128)(2,1)S(1)}, u32[]{:S(2)}, u32[]{:S(2)}) collective-permute-start(bf16[1,16,896]{2,1,0:T(8,128)(2,1)S(1)} %get-tuple-element.101), channel_id=1, source_target_pairs={{0,16},{4,20},{8,24},{12,28},{16,0},{20,4},{24,8},{28,12},{1,17},{... | collective-permute-start | bytes 86024 | tf_op jit(solution)/shard_map/ppermute | solution.py:953
  83.9 13.5 %all-to-all-start.1 = ((f32[32,1,128]{2,1,0:T(1,128)}), f32[32,1,128]{2,1,0:T(1,128)S(1)}, u32[]{:S(2)}, u32[]{:S(2)}) async-start(f32[32,1,128]{2,1,0:T(1,128)} %bitcast.13), calls=%async_computation.1 | async-start | bytes 32768 | tf_op jit(solution)/shard_map/all_to_all | solution.py:1085
  (4 other events, 113.0 us)

commit v4 on v3

--- a/solution.py
+++ b/solution.py
@@ -33,7 +33,7 @@
 GWIN = GROUP // WTOK
 T = 1024
 GROUPS = T // GROUP
-WIDE = 512
+WIDE = 1024
 PARTS = T // WIDE
 WIN = T // WTOK
 QSCALE = HEAD_DIM ** (-0.5)
@@ -357,11 +357,10 @@
         return jnp.concatenate(parts, axis=1)
 
     def unstack(product):
-        parts = []
-        for n in range(GWIN // 2):
-            cut = product[2 * HEAD_DIM * n : 2 * HEAD_DIM * (n + 1)]
-            parts.append(jnp.where(left, cut[0:HEAD_DIM], cut[HEAD_DIM:]))
-        return jnp.concatenate(parts, axis=1)
+        low = product.astype(BF)
+        return jnp.concatenate(
+            [low[HEAD_DIM * w : HEAD_DIM * w + HEAD_DIM] for w in range(GWIN)], axis=1
+        )
 
     def filled(g):
         return jnp.concatenate(
@@ -482,8 +481,7 @@
         for c in range(per_wide * g, per_wide * (g + 1)):
             cut = chunks[c]
             grad, hat = gh_s[:, cut], n3_s[:, cut]
-            ln_s[2] += grad * hat
-            ln_s[3] += grad
+            ln_s[1] += grad * hat
             back = normed_back(grad * column(5), hat, scale_three[c])
             grad_middle = cot[:, cut].astype(F32) * valid[c] + back
             x1_s[:, cut] = grad_middle
@@ -502,15 +500,13 @@
                 at, _ = place_of(n)
                 spreads[n] = spread(do_s[at, lanes])
                 grads[n] = mm(vcat_s[n], spreads[n])
-                twice = jnp.concatenate([pb_s[n], pb_s[n]], axis=0)
                 dkv_s[at.start + C : at.stop + C, lanes] = unstack(
-                    mm_nt(spreads.pop(n), twice)
-                ).astype(BF)
+                    mm_nt(spreads.pop(n), pb_s[n])
+                )
             if n >= first + 2:
                 at, lanes = place_of(n - 2)
                 dq_s[at, lanes] = own(kst_s[n - 2], ds_s[n - 2]).astype(BF)
-                twice = jnp.concatenate([ds_s[n - 2], ds_s[n - 2]], axis=0)
-                dkv_s[at, lanes] = unstack(mm_nt(qbd_s[n - 2], twice)).astype(BF)
+                dkv_s[at, lanes] = unstack(mm_nt(qbd_s[n - 2], ds_s[n - 2]))
             if first + 1 <= n <= first + units:
                 softmax_back(n - 1, grads.pop(n - 1))
             yield 340
@@ -523,12 +519,10 @@
             cut = chunks[c]
             grad, hat = gh_s[:, cut] * QSCALE, n1_s[:, cut]
             ln_s[0] += grad * hat
-            ln_s[1] += grad
             grad_dec[:, cut] = x1_s[:, cut] + normed_back(grad * column(0), hat, scale_one[c])
             yield 170
             grad, hat = gs_s[:, cut], n2_s[:, cut]
             ln_s[0] += grad * hat
-            ln_s[1] += grad
             back = normed_back(grad * column(0), hat, scale_two[c]).astype(BF)
             for w in (0, 1):
                 a = chosen[step * WIN + 2 * c + w]
@@ -601,20 +595,26 @@
                         :, 128 * n : 128 * n + 128
                     ]
             offset += per * cols
-        rows = [jnp.sum(jnp.transpose(ln_s[n]), axis=0, keepdims=True) for n in range(4)]
+        rows = [jnp.sum(jnp.transpose(ln_s[n]), axis=0, keepdims=True) for n in range(2)]
         def last_row(ref, at):
             row = [ref[n, at : at + 1, :] for n in range(ref.shape[0])]
             return jnp.concatenate(row, axis=1)
 
+        def through(row, weight):
+            row = jnp.broadcast_to(row, (16, row.shape[1]))
+            return sum(mm_nt(part, weight[...]) for part in splits(row))[0:1]
+
+        query_row = last_row(aq, C)[:, 0:C]
+        pair_row, upper_row = last_row(akv, C), last_row(a1, C)
         flat = jnp.concatenate(
             [
                 rows[0],
-                rows[1],
+                through(query_row, wq) * QSCALE + through(pair_row, wkv),
                 last_row(aq, C)[:, 0:C] * QSCALE,
                 last_row(akv, C)[:, C:],
                 last_row(ao, C)[:, 0:C],
-                rows[2],
-                rows[3],
+                rows[1],
+                through(upper_row, w1),
                 last_row(a1, C),
                 last_row(a2, HIDDEN_SIZE)[:, 0:C],
             ],
@@ -729,7 +729,7 @@
         ((2, C + 16, 128), F32),
         ((6, C + 16, 128), F32),
         ((2, HIDDEN_SIZE + 16, 128), F32),
-        ((4, C, 128), F32),
+        ((2, C, 128), F32),
     ]
     flops = 2 * tokens * (3 * 442368 + 12 * WTOK * C)
     return pl.pallas_call(
@@ -758,7 +758,7 @@
             pltpu.SemaphoreType.DMA((OUTER,)),
         ],
         compiler_params=pltpu.CompilerParams(
-            dimension_semantics=("arbitrary",), vmem_limit_bytes=42 * 1024 * 1024
+            dimension_semantics=("arbitrary",), vmem_limit_bytes=50 * 1024 * 1024
         ),
         cost_estimate=pl.CostEstimate(
             flops=flops, bytes_accessed=8_000_000, transcendentals=tokens * 1200

time: 98.7 us -> 98.8 us (level)
  transfers between devices with their start and end apart: 16 -> 16, of which waited for: 11 -> 10; matrix products, arithmetic and copies ran while one was open for 0% -> 0% of each run, Pallas kernels for 7% -> 7%
where the time goes in v4:
time: 98.8 us; the launch traced here: 98.5 us
  Pallas kernels  39.3 us (40%)
  waiting for transfers between devices  22.5 us (23%)
  starting transfers between devices  21.3 us (22%)
  blocking collectives  13.8 us (14%)
  between operations  1.54 us (2%)
    pallas_call x1, Pallas kernels, layer_call(): pl.pallas_call(functools.partial(layer_kernel, skip_count, windows, len(p...  29.8 us
    ppermute x15, waiting for transfers between devices, swap(): return lax.ppermute(value, axis, [(n, n ^ distance) for n in range(count)])  19.9 us
    ppermute x15, starting transfers between devices, swap(): return lax.ppermute(value, axis, [(n, n ^ distance) for n in range(count)])  14.9 us
    all_to_all x1, blocking collectives, on_device(): own = lax.all_to_all(block, 'slab', split_axis=0, concat_axis=0)  13.8 us
    pallas_call x8, Pallas kernels, small_call(): pl.pallas_call(kernel, in_specs=in_specs, out_specs=[VMEM] * len(outs), o...  7.76 us
    all_to_all x1, starting transfers between devices, on_device(): lax.all_to_all(tail, ('slab', 'skip'), split_axis=0, concat_axis=0, tiled...  6.38 us
    all_to_all x1, waiting for transfers between devices, on_device(): lax.all_to_all(tail, ('slab', 'skip'), split_axis=0, concat_axis=0, tiled...  2.56 us
  transfers between devices with their start and end apart: 16, of which 10 were waited for; matrix products, arithmetic and copies ran while one was open for 0% of the time, Pallas kernels for 7%

profile of v4, /device:TPU:0, one launch (start us, length us, event | category | flops | bytes accessed | tf_op | source)
XLA Modules:
  0.0 98.5 jit_solution(3187582661617258777)
XLA Ops:
  0.7 3.0 %collective-permute-start.1 = (bf16[2048,192]{0,1:T(8,128)(2,1)}, bf16[2048,192]{0,1:T(8,128)(2,1)S(1)}, u32[]{:S(2)}, u32[]{:S(2)}) collective-permute-start(bf16[2048,192]{0,1:T(8,128)(2,1)} %param.18), channel_id=1, source_target_pairs={{0,2},{1,3},{2,0},{3,1},{4,6},{5,7},{6,4},{7,5},{8,10},{9,11},{10,... | collective-permute-start | bytes 2359304 | tf_op jit(solution)/shard_map/ppermute | solution.py:953
  3.7 0.9 pack.1
  4.6 13.8 %all_to_all.17.after.refs_0_ = bf16[8,16,896]{2,1,0:T(8,128)(2,1)S(1)} all-to-all(bf16[8,16,896]{2,1,0:T(8,128)(2,1)S(1)} %pack.1), channel_id=1, replica_groups=mesh['slab'=8,'skip'=4] {'slab'}, dimensions={0} | all-to-all | bytes 458752 | tf_op jit(solution)/shard_map/all_to_all | solution.py:984
  18.8 1.7 %early.1 = (f32[6,64,128]{2,1,0:T(8,128)S(1)}, s32[1,128]{1,0:T(1,128)S(1)}) custom-call(s32[32]{0:T(128)} %bitcast.35, f32[6,343]{1,0:T(8,128)} %bitcast.28, bf16[8,16,896]{2,1,0:T(8,128)(2,1)S(1)} %all_to_all.17.after.refs_0_), custom_call_target="tpu_custom_call" | custom-call | flops 100000000 | bytes 1000000 | tf_op jit(solution)/shard_map/early/pallas_call | solution.py:956
  20.5 5.9 %collective-permute-done.refs_2_ = bf16[8,16,896]{2,1,0:T(8,128)(2,1)S(1)} collective-permute-done((bf16[8,16,896]{2,1,0:T(8,128)(2,1)S(1)}, bf16[8,16,896]{2,1,0:T(8,128)(2,1)S(1)}, u32[]{:S(2)}, u32[]{:S(2)}) %collective-permute-start) | collective-permute-done | bytes 229408 | tf_op jit(solution)/shard_map/ppermute | solution.py:953
  27.7 1.2 %collective-permute-done.2.refs_1_ = bf16[8,16,896]{2,1,0:T(8,128)(2,1)S(1)} collective-permute-done((bf16[8,16,896]{2,1,0:T(8,128)(2,1)S(1)}, bf16[8,16,896]{2,1,0:T(8,128)(2,1)S(1)}, u32[]{:S(2)}, u32[]{:S(2)}) %collective-permute-start.2) | collective-permute-done | bytes 229408 | tf_op jit(solution)/shard_map/ppermute | solution.py:953
  29.3 29.8 %layer.1 = (bf16[192,2048]{1,0:T(8,128)(2,1)}, f32[192,2048]{1,0:T(8,128)}, s32[32,128]{1,0:T(8,128)S(1)}, bf16[192,512]{1,0:T(8,128)(2,1)S(1)}, bf16[192,512]{1...) custom-call(s32[32]{0:T(128)} %bitcast.36, ...), custom_call_target="tpu_custom_call" | custom-call | flops 6039797760 | bytes 8000000 | tf_op jit(solution)/shard_map/layer/pallas_call | solution.py:735
  59.7 1.0 collective-permute-done.7.refs_1_
  60.8 1.8 %collective-permute-start.8 = (bf16[8,16,896]{2,1,0:T(8,128)(2,1)S(1)}, bf16[8,16,896]{2,1,0:T(8,128)(2,1)S(1)}, u32[]{:S(2)}, u32[]{:S(2)}) collective-permute-start(bf16[8,16,896]{2,1,0:T(8,128)(2,1)S(1)} %core_sum.1), channel_id=1, source_target_pairs={{0,2},{1,3},{2,0},{3,1},{4,6},{5,7},{6,4},{7,5},{8,10},{9,11},{10,... | collective-permute-start | bytes 688136 | tf_op jit(solution)/shard_map/ppermute | solution.py:953
  62.6 5.9 %collective-permute-done.8.refs_2_ = bf16[8,16,896]{2,1,0:T(8,128)(2,1)S(1)} collective-permute-done((bf16[8,16,896]{2,1,0:T(8,128)(2,1)S(1)}, bf16[8,16,896]{2,1,0:T(8,128)(2,1)S(1)}, u32[]{:S(2)}, u32[]{:S(2)}) %collective-permute-start.8) | collective-permute-done | bytes 229408 | tf_op jit(solution)/shard_map/ppermute | solution.py:953
  68.5 0.6 skip_sum.1
  69.3 1.8 %collective-permute-start.9 = (bf16[4,16,896]{2,1,0:T(8,128)(2,1)S(1)}, bf16[4,16,896]{2,1,0:T(8,128)(2,1)S(1)}, u32[]{:S(2)}, u32[]{:S(2)}) collective-permute-start(bf16[4,16,896]{2,1,0:T(8,128)(2,1)S(1)} %get-tuple-element.97), channel_id=1, source_target_pairs={{0,4},{4,0},{8,12},{12,8},{16,20},{20,16},{24,28},{28,24},{1,5},{5... | collective-permute-start | bytes 344072 | tf_op jit(solution)/shard_map/ppermute | solution.py:953
  71.1 1.5 %collective-permute-start.13 = (bf16[192,512]{1,0:T(8,128)(2,1)S(1)}, bf16[192,512]{1,0:T(8,128)(2,1)S(1)}, u32[]{:S(2)}, u32[]{:S(2)}) collective-permute-start(bf16[192,512]{1,0:T(8,128)(2,1)S(1)} %get-tuple-element.104), channel_id=1, source_target_pairs={{0,2},{1,3},{2,0},{3,1},{4,6},{5,7},{6,4},{7,5},{8,10},{9,11},{10,... | collective-permute-start | bytes 589832 | tf_op jit(solution)/shard_map/ppermute | solution.py:953
  72.9 1.2 %collective-permute-done.9.came = bf16[4,16,896]{2,1,0:T(8,128)(2,1)S(1)} collective-permute-done((bf16[4,16,896]{2,1,0:T(8,128)(2,1)S(1)}, bf16[4,16,896]{2,1,0:T(8,128)(2,1)S(1)}, u32[]{:S(2)}, u32[]{:S(2)}) %collective-permute-start.9) | collective-permute-done | bytes 114720 | tf_op jit(solution)/shard_map/ppermute | solution.py:953
  74.2 1.9 %collective-permute-start.10 = (bf16[2,16,896]{2,1,0:T(8,128)(2,1)S(1)}, bf16[2,16,896]{2,1,0:T(8,128)(2,1)S(1)}, u32[]{:S(2)}, u32[]{:S(2)}) collective-permute-start(bf16[2,16,896]{2,1,0:T(8,128)(2,1)S(1)} %get-tuple-element.99), channel_id=1, source_target_pairs={{0,8},{4,12},{8,0},{12,4},{16,24},{20,28},{24,16},{28,20},{1,9},{5... | collective-permute-start | bytes 172040 | tf_op jit(solution)/shard_map/ppermute | solution.py:953
  76.0 2.4 %collective-permute-done.10.came = bf16[2,16,896]{2,1,0:T(8,128)(2,1)S(1)} collective-permute-done((bf16[2,16,896]{2,1,0:T(8,128)(2,1)S(1)}, bf16[2,16,896]{2,1,0:T(8,128)(2,1)S(1)}, u32[]{:S(2)}, u32[]{:S(2)}) %collective-permute-start.10) | collective-permute-done | bytes 57376 | tf_op jit(solution)/shard_map/ppermute | solution.py:953
  78.4 2.9 %collective-permute-start.11 = (bf16[1,16,896]{2,1,0:T(8,128)(2,1)S(1)}, bf16[1,16,896]{2,1,0:T(8,128)(2,1)S(1)}, u32[]{:S(2)}, u32[]{:S(2)}) collective-permute-start(bf16[1,16,896]{2,1,0:T(8,128)(2,1)S(1)} %get-tuple-element.101), channel_id=1, source_target_pairs={{0,16},{4,20},{8,24},{12,28},{16,0},{20,4},{24,8},{28,12},{1,17},{... | collective-permute-start | bytes 86024 | tf_op jit(solution)/shard_map/ppermute | solution.py:953
  81.3 0.9 collective-permute-done.14.refs_3_
  82.2 1.1 %collective-permute-done.11.came = bf16[1,16,896]{2,1,0:T(8,128)(2,1)S(1)} collective-permute-done((bf16[1,16,896]{2,1,0:T(8,128)(2,1)S(1)}, bf16[1,16,896]{2,1,0:T(8,128)(2,1)S(1)}, u32[]{:S(2)}, u32[]{:S(2)}) %collective-permute-start.11) | collective-permute-done | bytes 28704 | tf_op jit(solution)/shard_map/ppermute | solution.py:953
  83.3 0.7 slab_sum.1
  84.0 6.4 %all-to-all-start.1 = ((f32[32,1,128]{2,1,0:T(1,128)}), f32[32,1,128]{2,1,0:T(1,128)S(1)}, u32[]{:S(2)}, u32[]{:S(2)}) async-start(f32[32,1,128]{2,1,0:T(1,128)} %bitcast.13), calls=%async_computation.1 | async-start | bytes 32768 | tf_op jit(solution)/shard_map/all_to_all | solution.py:1085
  90.4 4.5 %returned.1 = f32[192,2048]{1,0:T(8,128)} custom-call(s32[4]{0:T(128)S(1)} %pad_add_fusion.here, s32[32,128]{1,0:T(8,128)S(1)} %get-tuple-element.108.everyone, f32[1,72]{1,0:T(1,128)S(1)} %get-tuple-element.109.after.vec_share, bf16[192,512]{1,0:T(8,128)(2,1)S(1)} %get-tuple-element.110.refs_0_, bf16[192,512]{1,0:T(8,128)(2,1)S(1)} %collective-permute-done.12.refs_1_, ...), custom_call_target="tpu_custom_call" | custom-call | flops 3000000 | bytes 3000000 | tf_op jit(solution)/shard_map/returned/pallas_call | solution.py:869
  94.9 2.6 %all-to-all-done.1 = f32[32,1,128]{2,1,0:T(1,128)S(1)} async-done(((f32[32,1,128]{2,1,0:T(1,128)}), f32[32,1,128]{2,1,0:T(1,128)S(1)}, u32[]{:S(2)}, u32[]{:S(2)}) %all-to-all-start.1) | async-done | bytes 16416 | tf_op jit(solution)/shard_map/all_to_all | solution.py:1085
  97.5 0.9 update.1
  (46 shorter events, 2.7 us)
Async XLA Ops:
  0.7 25.7 %collective-permute-start.1 = (bf16[2048,192]{0,1:T(8,128)(2,1)}, bf16[2048,192]{0,1:T(8,128)(2,1)S(1)}, u32[]{:S(2)}, u32[]{:S(2)}) collective-permute-start(bf16[2048,192]{0,1:T(8,128)(2,1)} %param.18), channel_id=1, source_target_pairs={{0,2},{1,3},{2,0},{3,1},{4,6},{5,7},{6,4},{7,5},{8,10},{9,11},{10,... | collective-permute-start | bytes 2359304 | tf_op jit(solution)/shard_map/ppermute | solution.py:953
  18.3 8.0 %collective-permute-start = (bf16[8,16,896]{2,1,0:T(8,128)(2,1)S(1)}, bf16[8,16,896]{2,1,0:T(8,128)(2,1)S(1)}, u32[]{:S(2)}, u32[]{:S(2)}) collective-permute-start(bf16[8,16,896]{2,1,0:T(8,128)(2,1)S(1)} %all_to_all.17.after.refs_0_), channel_id=1, source_target_pairs={{0,2},{1,3},{2,0},{3,1},{4,6},{5,7},{6,4},{7,5},{8,10},{9,11},{10,... | collective-permute-start | bytes 688136 | tf_op jit(solution)/shard_map/ppermute | solution.py:953
  18.8 10.1 %collective-permute-start.4 = (bf16[2048,192]{0,1:T(8,128)(2,1)}, bf16[2048,192]{0,1:T(8,128)(2,1)S(1)}, u32[]{:S(2)}, u32[]{:S(2)}) collective-permute-start(bf16[2048,192]{0,1:T(8,128)(2,1)} %param.18), channel_id=1, source_target_pairs={{0,1},{1,0},{2,3},{3,2},{4,5},{5,4},{6,7},{7,6},{8,9},{9,8},{10,11... | collective-permute-start | bytes 2359304 | tf_op jit(solution)/shard_map/ppermute | solution.py:953
  26.4 2.9 %collective-permute-start.5 = (bf16[2048,192]{0,1:T(8,128)(2,1)S(1)}, bf16[2048,192]{0,1:T(8,128)(2,1)}, u32[]{:S(2)}, u32[]{:S(2)}) collective-permute-start(bf16[2048,192]{0,1:T(8,128)(2,1)S(1)} %collective-permute-done.1), channel_id=1, source_target_pairs={{0,1},{1,0},{2,3},{3,2},{4,5},{5,4},{6,7},{7,6},{8,9},{9,8},{10,11... | collective-permute-start | bytes 2359304 | tf_op jit(solution)/shard_map/ppermute | solution.py:953
  26.4 2.5 %collective-permute-start.2 = (bf16[8,16,896]{2,1,0:T(8,128)(2,1)S(1)}, bf16[8,16,896]{2,1,0:T(8,128)(2,1)S(1)}, u32[]{:S(2)}, u32[]{:S(2)}) collective-permute-start(bf16[8,16,896]{2,1,0:T(8,128)(2,1)S(1)} %all_to_all.17.after.refs_0_), channel_id=1, source_target_pairs={{0,1},{1,0},{2,3},{3,2},{4,5},{5,4},{6,7},{7,6},{8,9},{9,8},{10,11... | collective-permute-start | bytes 688136 | tf_op jit(solution)/shard_map/ppermute | solution.py:953
  26.9 2.4 %collective-permute-start.3 = (bf16[8,16,896]{2,1,0:T(8,128)(2,1)S(1)}, bf16[8,16,896]{2,1,0:T(8,128)(2,1)S(1)}, u32[]{:S(2)}, u32[]{:S(2)}) collective-permute-start(bf16[8,16,896]{2,1,0:T(8,128)(2,1)S(1)} %collective-permute-done.refs_2_), channel_id=1, source_target_pairs={{0,1},{1,0},{2,3},{3,2},{4,5},{5,4},{6,7},{7,6},{8,9},{9,8},{10,11... | collective-permute-start | bytes 688136 | tf_op jit(solution)/shard_map/ppermute | solution.py:953
  59.2 1.6 %collective-permute-start.7 = (bf16[8,16,896]{2,1,0:T(8,128)(2,1)S(1)}, bf16[8,16,896]{2,1,0:T(8,128)(2,1)S(1)}, u32[]{:S(2)}, u32[]{:S(2)}) collective-permute-start(bf16[8,16,896]{2,1,0:T(8,128)(2,1)S(1)} %get-tuple-element.90), channel_id=1, source_target_pairs={{0,1},{1,0},{2,3},{3,2},{4,5},{5,4},{6,7},{7,6},{8,9},{9,8},{10,11... | collective-permute-start | bytes 688136 | tf_op jit(solution)/shard_map/ppermute | solution.py:953
  59.4 3.2 %collective-permute-start.6 = (bf16[8,16,896]{2,1,0:T(8,128)(2,1)S(1)}, bf16[8,16,896]{2,1,0:T(8,128)(2,1)S(1)}, u32[]{:S(2)}, u32[]{:S(2)}) collective-permute-start(bf16[8,16,896]{2,1,0:T(8,128)(2,1)S(1)} %get-tuple-element.88), channel_id=1, source_target_pairs={{0,1},{1,0},{2,3},{3,2},{4,5},{5,4},{6,7},{7,6},{8,9},{9,8},{10,11... | collective-permute-start | bytes 688136 | tf_op jit(solution)/shard_map/ppermute | solution.py:953
  60.8 7.7 %collective-permute-start.8 = (bf16[8,16,896]{2,1,0:T(8,128)(2,1)S(1)}, bf16[8,16,896]{2,1,0:T(8,128)(2,1)S(1)}, u32[]{:S(2)}, u32[]{:S(2)}) collective-permute-start(bf16[8,16,896]{2,1,0:T(8,128)(2,1)S(1)} %core_sum.1), channel_id=1, source_target_pairs={{0,2},{1,3},{2,0},{3,1},{4,6},{5,7},{6,4},{7,5},{8,10},{9,11},{10,... | collective-permute-start | bytes 688136 | tf_op jit(solution)/shard_map/ppermute | solution.py:953
  69.1 28.3 %copy-start = (f32[1,13824]{1,0:T(1,128)S(1)}, f32[1,13824]{1,0:T(1,128)}, u32[]{:S(2)}) copy-start(f32[1,13824]{1,0:T(1,128)} %refs_0_.1) | copy-start | bytes 165892
  69.1 28.3 %copy-start.1 = (f32[1,13824]{1,0:T(1,128)S(1)}, f32[1,13824]{1,0:T(1,128)}, u32[]{:S(2)}) copy-start(f32[1,13824]{1,0:T(1,128)} %refs_1_.1) | copy-start | bytes 165892
  69.2 28.3 %copy-start.2 = (f32[1,13824]{1,0:T(1,128)S(1)}, f32[1,13824]{1,0:T(1,128)}, u32[]{:S(2)}) copy-start(f32[1,13824]{1,0:T(1,128)} %refs_2_.1) | copy-start | bytes 165892
  69.2 28.3 %copy-start.3 = (f32[1,13824]{1,0:T(1,128)S(1)}, f32[1,13824]{1,0:T(1,128)}, u32[]{:S(2)}) copy-start(f32[1,13824]{1,0:T(1,128)} %refs_3_.1) | copy-start | bytes 165892
  69.2 28.3 %copy-start.4 = (f32[343,6]{0,1:T(8,128)S(1)}, f32[343,6]{0,1:T(8,128)}, u32[]{:S(2)}) copy-start(f32[343,6]{0,1:T(8,128)} %param.30) | copy-start | bytes 24700
  69.2 28.3 %copy-start.5 = (f32[343,6]{0,1:T(8,128)S(1)}, f32[343,6]{0,1:T(8,128)}, u32[]{:S(2)}) copy-start(f32[343,6]{0,1:T(8,128)} %param.31) | copy-start | bytes 24700
  69.2 28.3 %copy-start.6 = (f32[343,6]{0,1:T(8,128)S(1)}, f32[343,6]{0,1:T(8,128)}, u32[]{:S(2)}) copy-start(f32[343,6]{0,1:T(8,128)} %param.32) | copy-start | bytes 24700
  69.2 28.3 %copy-start.7 = (f32[343,6]{0,1:T(8,128)S(1)}, f32[343,6]{0,1:T(8,128)}, u32[]{:S(2)}) copy-start(f32[343,6]{0,1:T(8,128)} %param.33) | copy-start | bytes 24700
  69.3 4.9 %collective-permute-start.9 = (bf16[4,16,896]{2,1,0:T(8,128)(2,1)S(1)}, bf16[4,16,896]{2,1,0:T(8,128)(2,1)S(1)}, u32[]{:S(2)}, u32[]{:S(2)}) collective-permute-start(bf16[4,16,896]{2,1,0:T(8,128)(2,1)S(1)} %get-tuple-element.97), channel_id=1, source_target_pairs={{0,4},{4,0},{8,12},{12,8},{16,20},{20,16},{24,28},{28,24},{1,5},{5... | collective-permute-start | bytes 344072 | tf_op jit(solution)/shard_map/ppermute | solution.py:953
  71.1 10.3 %collective-permute-start.12 = (bf16[192,512]{1,0:T(8,128)(2,1)S(1)}, bf16[192,512]{1,0:T(8,128)(2,1)S(1)}, u32[]{:S(2)}, u32[]{:S(2)}) collective-permute-start(bf16[192,512]{1,0:T(8,128)(2,1)S(1)} %get-tuple-element.103), channel_id=1, source_target_pairs={{0,1},{1,0},{2,3},{3,2},{4,5},{5,4},{6,7},{7,6},{8,9},{9,8},{10,11... | collective-permute-start | bytes 589832 | tf_op jit(solution)/shard_map/ppermute | solution.py:953
  71.1 10.3 %collective-permute-start.13 = (bf16[192,512]{1,0:T(8,128)(2,1)S(1)}, bf16[192,512]{1,0:T(8,128)(2,1)S(1)}, u32[]{:S(2)}, u32[]{:S(2)}) collective-permute-start(bf16[192,512]{1,0:T(8,128)(2,1)S(1)} %get-tuple-element.104), channel_id=1, source_target_pairs={{0,2},{1,3},{2,0},{3,1},{4,6},{5,7},{6,4},{7,5},{8,10},{9,11},{10,... | collective-permute-start | bytes 589832 | tf_op jit(solution)/shard_map/ppermute | solution.py:953
  72.6 9.6 %collective-permute-start.14 = (bf16[192,512]{1,0:T(8,128)(2,1)S(1)}, bf16[192,512]{1,0:T(8,128)(2,1)S(1)}, u32[]{:S(2)}, u32[]{:S(2)}) collective-permute-start(bf16[192,512]{1,0:T(8,128)(2,1)S(1)} %get-tuple-element.105), channel_id=1, source_target_pairs={{0,3},{1,2},{2,1},{3,0},{4,7},{5,6},{6,5},{7,4},{8,11},{9,10},{10,... | collective-permute-start | bytes 589832 | tf_op jit(solution)/shard_map/ppermute | solution.py:953
  74.2 4.2 %collective-permute-start.10 = (bf16[2,16,896]{2,1,0:T(8,128)(2,1)S(1)}, bf16[2,16,896]{2,1,0:T(8,128)(2,1)S(1)}, u32[]{:S(2)}, u32[]{:S(2)}) collective-permute-start(bf16[2,16,896]{2,1,0:T(8,128)(2,1)S(1)} %get-tuple-element.99), channel_id=1, source_target_pairs={{0,8},{4,12},{8,0},{12,4},{16,24},{20,28},{24,16},{28,20},{1,9},{5... | collective-permute-start | bytes 172040 | tf_op jit(solution)/shard_map/ppermute | solution.py:953
  78.4 4.8 %collective-permute-start.11 = (bf16[1,16,896]{2,1,0:T(8,128)(2,1)S(1)}, bf16[1,16,896]{2,1,0:T(8,128)(2,1)S(1)}, u32[]{:S(2)}, u32[]{:S(2)}) collective-permute-start(bf16[1,16,896]{2,1,0:T(8,128)(2,1)S(1)} %get-tuple-element.101), channel_id=1, source_target_pairs={{0,16},{4,20},{8,24},{12,28},{16,0},{20,4},{24,8},{28,12},{1,17},{... | collective-permute-start | bytes 86024 | tf_op jit(solution)/shard_map/ppermute | solution.py:953
  84.0 13.5 %all-to-all-start.1 = ((f32[32,1,128]{2,1,0:T(1,128)}), f32[32,1,128]{2,1,0:T(1,128)S(1)}, u32[]{:S(2)}, u32[]{:S(2)}) async-start(f32[32,1,128]{2,1,0:T(1,128)} %bitcast.13), calls=%async_computation.1 | async-start | bytes 32768 | tf_op jit(solution)/shard_map/all_to_all | solution.py:1085
  (5 other events, 116.0 us)

commit v5 on v4

--- a/solution.py
+++ b/solution.py
@@ -981,6 +981,7 @@
             (kept(mat_master), kept(vec_master), kept(assignment)),
             moved=100_000,
         )
+        block, skip_tokens = lax.optimization_barrier((block, skip_tokens))
         own = lax.all_to_all(block, "slab", split_axis=0, concat_axis=0)
         across = swap(skip_tokens, "skip", 2)
         near = swap(skip_tokens, "skip", 1)

time: 98.8 us -> 99.7 us (level)
  transfers between devices with their start and end apart: 16 -> 16, of which waited for: 10 -> 10; matrix products, arithmetic and copies ran while one was open for 0% -> 0% of each run, Pallas kernels for 7% -> 6%
where the time goes in v5:
time: 99.7 us; the launch traced here: 99.3 us
  Pallas kernels  39.3 us (39%)
  waiting for transfers between devices  23.4 us (23%)
  starting transfers between devices  21.2 us (21%)
  blocking collectives  13.7 us (14%)
  between operations  1.54 us (2%)
    pallas_call x1, Pallas kernels, layer_call(): pl.pallas_call(functools.partial(layer_kernel, skip_count, windows, len(p...  29.8 us
    ppermute x15, waiting for transfers between devices, swap(): return lax.ppermute(value, axis, [(n, n ^ distance) for n in range(count)])  20.8 us
    ppermute x15, starting transfers between devices, swap(): return lax.ppermute(value, axis, [(n, n ^ distance) for n in range(count)])  14.9 us
    all_to_all x1, blocking collectives, on_device(): own = lax.all_to_all(block, 'slab', split_axis=0, concat_axis=0)  13.7 us
    pallas_call x8, Pallas kernels, small_call(): pl.pallas_call(kernel, in_specs=in_specs, out_specs=[VMEM] * len(outs), o...  7.76 us
    all_to_all x1, starting transfers between devices, on_device(): lax.all_to_all(tail, ('slab', 'skip'), split_axis=0, concat_axis=0, tiled...  6.37 us
    all_to_all x1, waiting for transfers between devices, on_device(): lax.all_to_all(tail, ('slab', 'skip'), split_axis=0, concat_axis=0, tiled...  2.56 us
  transfers between devices with their start and end apart: 16, of which 10 were waited for; matrix products, arithmetic and copies ran while one was open for 0% of the time, Pallas kernels for 6%

profile of v5, /device:TPU:0, one launch (start us, length us, event | category | flops | bytes accessed | tf_op | source)
XLA Modules:
  0.0 99.3 jit_solution(9280040259115336070)
XLA Ops:
  0.7 0.9 pack.1
  1.5 3.0 %collective-permute-start.1 = (bf16[2048,192]{0,1:T(8,128)(2,1)}, bf16[2048,192]{0,1:T(8,128)(2,1)S(1)}, u32[]{:S(2)}, u32[]{:S(2)}) collective-permute-start(bf16[2048,192]{0,1:T(8,128)(2,1)} %param.18), channel_id=1, source_target_pairs={{0,2},{1,3},{2,0},{3,1},{4,6},{5,7},{6,4},{7,5},{8,10},{9,11},{10,... | collective-permute-start | bytes 2359304 | tf_op jit(solution)/shard_map/ppermute | solution.py:953
  4.6 13.7 %all_to_all.17.after.refs_0_ = bf16[8,16,896]{2,1,0:T(8,128)(2,1)S(1)} all-to-all(bf16[8,16,896]{2,1,0:T(8,128)(2,1)S(1)} %pack.1), channel_id=1, replica_groups=mesh['slab'=8,'skip'=4] {'slab'}, dimensions={0} | all-to-all | bytes 458752 | tf_op jit(solution)/shard_map/all_to_all | solution.py:985
  18.8 1.7 %early.1 = (f32[6,64,128]{2,1,0:T(8,128)S(1)}, s32[1,128]{1,0:T(1,128)S(1)}) custom-call(s32[32]{0:T(128)} %bitcast.35, f32[6,343]{1,0:T(8,128)} %bitcast.28, bf16[8,16,896]{2,1,0:T(8,128)(2,1)S(1)} %all_to_all.17.after.refs_0_), custom_call_target="tpu_custom_call" | custom-call | flops 100000000 | bytes 1000000 | tf_op jit(solution)/shard_map/early/pallas_call | solution.py:956
  20.5 6.7 %collective-permute-done.refs_2_ = bf16[8,16,896]{2,1,0:T(8,128)(2,1)S(1)} collective-permute-done((bf16[8,16,896]{2,1,0:T(8,128)(2,1)S(1)}, bf16[8,16,896]{2,1,0:T(8,128)(2,1)S(1)}, u32[]{:S(2)}, u32[]{:S(2)}) %collective-permute-start) | collective-permute-done | bytes 229408 | tf_op jit(solution)/shard_map/ppermute | solution.py:953
  28.6 1.2 %collective-permute-done.2.refs_1_ = bf16[8,16,896]{2,1,0:T(8,128)(2,1)S(1)} collective-permute-done((bf16[8,16,896]{2,1,0:T(8,128)(2,1)S(1)}, bf16[8,16,896]{2,1,0:T(8,128)(2,1)S(1)}, u32[]{:S(2)}, u32[]{:S(2)}) %collective-permute-start.2) | collective-permute-done | bytes 229408 | tf_op jit(solution)/shard_map/ppermute | solution.py:953
  30.2 29.8 %layer.1 = (bf16[192,2048]{1,0:T(8,128)(2,1)}, f32[192,2048]{1,0:T(8,128)}, s32[32,128]{1,0:T(8,128)S(1)}, bf16[192,512]{1,0:T(8,128)(2,1)S(1)}, bf16[192,512]{1...) custom-call(s32[32]{0:T(128)} %bitcast.36, ...), custom_call_target="tpu_custom_call" | custom-call | flops 6039797760 | bytes 8000000 | tf_op jit(solution)/shard_map/layer/pallas_call | solution.py:735
  60.6 1.0 collective-permute-done.7.refs_1_
  61.7 1.8 %collective-permute-start.8 = (bf16[8,16,896]{2,1,0:T(8,128)(2,1)S(1)}, bf16[8,16,896]{2,1,0:T(8,128)(2,1)S(1)}, u32[]{:S(2)}, u32[]{:S(2)}) collective-permute-start(bf16[8,16,896]{2,1,0:T(8,128)(2,1)S(1)} %core_sum.1), channel_id=1, source_target_pairs={{0,2},{1,3},{2,0},{3,1},{4,6},{5,7},{6,4},{7,5},{8,10},{9,11},{10,... | collective-permute-start | bytes 688136 | tf_op jit(solution)/shard_map/ppermute | solution.py:953
  63.5 5.9 %collective-permute-done.8.refs_2_ = bf16[8,16,896]{2,1,0:T(8,128)(2,1)S(1)} collective-permute-done((bf16[8,16,896]{2,1,0:T(8,128)(2,1)S(1)}, bf16[8,16,896]{2,1,0:T(8,128)(2,1)S(1)}, u32[]{:S(2)}, u32[]{:S(2)}) %collective-permute-start.8) | collective-permute-done | bytes 229408 | tf_op jit(solution)/shard_map/ppermute | solution.py:953
  69.4 0.6 skip_sum.1
  70.2 1.8 %collective-permute-start.9 = (bf16[4,16,896]{2,1,0:T(8,128)(2,1)S(1)}, bf16[4,16,896]{2,1,0:T(8,128)(2,1)S(1)}, u32[]{:S(2)}, u32[]{:S(2)}) collective-permute-start(bf16[4,16,896]{2,1,0:T(8,128)(2,1)S(1)} %get-tuple-element.101), channel_id=1, source_target_pairs={{0,4},{4,0},{8,12},{12,8},{16,20},{20,16},{24,28},{28,24},{1,5},{5... | collective-permute-start | bytes 344072 | tf_op jit(solution)/shard_map/ppermute | solution.py:953
  71.9 1.5 %collective-permute-start.13 = (bf16[192,512]{1,0:T(8,128)(2,1)S(1)}, bf16[192,512]{1,0:T(8,128)(2,1)S(1)}, u32[]{:S(2)}, u32[]{:S(2)}) collective-permute-start(bf16[192,512]{1,0:T(8,128)(2,1)S(1)} %get-tuple-element.108), channel_id=1, source_target_pairs={{0,2},{1,3},{2,0},{3,1},{4,6},{5,7},{6,4},{7,5},{8,10},{9,11},{10,... | collective-permute-start | bytes 589832 | tf_op jit(solution)/shard_map/ppermute | solution.py:953
  73.8 1.2 %collective-permute-done.9.came = bf16[4,16,896]{2,1,0:T(8,128)(2,1)S(1)} collective-permute-done((bf16[4,16,896]{2,1,0:T(8,128)(2,1)S(1)}, bf16[4,16,896]{2,1,0:T(8,128)(2,1)S(1)}, u32[]{:S(2)}, u32[]{:S(2)}) %collective-permute-start.9) | collective-permute-done | bytes 114720 | tf_op jit(solution)/shard_map/ppermute | solution.py:953
  75.0 1.9 %collective-permute-start.10 = (bf16[2,16,896]{2,1,0:T(8,128)(2,1)S(1)}, bf16[2,16,896]{2,1,0:T(8,128)(2,1)S(1)}, u32[]{:S(2)}, u32[]{:S(2)}) collective-permute-start(bf16[2,16,896]{2,1,0:T(8,128)(2,1)S(1)} %get-tuple-element.103), channel_id=1, source_target_pairs={{0,8},{4,12},{8,0},{12,4},{16,24},{20,28},{24,16},{28,20},{1,9},{5... | collective-permute-start | bytes 172040 | tf_op jit(solution)/shard_map/ppermute | solution.py:953
  76.9 2.4 %collective-permute-done.10.came = bf16[2,16,896]{2,1,0:T(8,128)(2,1)S(1)} collective-permute-done((bf16[2,16,896]{2,1,0:T(8,128)(2,1)S(1)}, bf16[2,16,896]{2,1,0:T(8,128)(2,1)S(1)}, u32[]{:S(2)}, u32[]{:S(2)}) %collective-permute-start.10) | collective-permute-done | bytes 57376 | tf_op jit(solution)/shard_map/ppermute | solution.py:953
  79.3 2.9 %collective-permute-start.11 = (bf16[1,16,896]{2,1,0:T(8,128)(2,1)S(1)}, bf16[1,16,896]{2,1,0:T(8,128)(2,1)S(1)}, u32[]{:S(2)}, u32[]{:S(2)}) collective-permute-start(bf16[1,16,896]{2,1,0:T(8,128)(2,1)S(1)} %get-tuple-element.105), channel_id=1, source_target_pairs={{0,16},{4,20},{8,24},{12,28},{16,0},{20,4},{24,8},{28,12},{1,17},{... | collective-permute-start | bytes 86024 | tf_op jit(solution)/shard_map/ppermute | solution.py:953
  82.2 0.9 collective-permute-done.14.refs_3_
  83.1 1.1 %collective-permute-done.11.came = bf16[1,16,896]{2,1,0:T(8,128)(2,1)S(1)} collective-permute-done((bf16[1,16,896]{2,1,0:T(8,128)(2,1)S(1)}, bf16[1,16,896]{2,1,0:T(8,128)(2,1)S(1)}, u32[]{:S(2)}, u32[]{:S(2)}) %collective-permute-start.11) | collective-permute-done | bytes 28704 | tf_op jit(solution)/shard_map/ppermute | solution.py:953
  84.1 0.7 slab_sum.1
  84.9 6.4 %all-to-all-start.1 = ((f32[32,1,128]{2,1,0:T(1,128)}), f32[32,1,128]{2,1,0:T(1,128)S(1)}, u32[]{:S(2)}, u32[]{:S(2)}) async-start(f32[32,1,128]{2,1,0:T(1,128)} %bitcast.13), calls=%async_computation.1 | async-start | bytes 32768 | tf_op jit(solution)/shard_map/all_to_all | solution.py:1086
  91.2 4.5 %returned.1 = f32[192,2048]{1,0:T(8,128)} custom-call(s32[4]{0:T(128)S(1)} %pad_add_fusion.here, s32[32,128]{1,0:T(8,128)S(1)} %get-tuple-element.112.everyone, f32[1,72]{1,0:T(1,128)S(1)} %get-tuple-element.113.after.vec_share, bf16[192,512]{1,0:T(8,128)(2,1)S(1)} %get-tuple-element.114.refs_0_, bf16[192,512]{1,0:T(8,128)(2,1)S(1)} %collective-permute-done.12.refs_1_, ...), custom_call_target="tpu_custom_call" | custom-call | flops 3000000 | bytes 3000000 | tf_op jit(solution)/shard_map/returned/pallas_call | solution.py:869
  95.7 2.6 %all-to-all-done.1 = f32[32,1,128]{2,1,0:T(1,128)S(1)} async-done(((f32[32,1,128]{2,1,0:T(1,128)}), f32[32,1,128]{2,1,0:T(1,128)S(1)}, u32[]{:S(2)}, u32[]{:S(2)}) %all-to-all-start.1) | async-done | bytes 16416 | tf_op jit(solution)/shard_map/all_to_all | solution.py:1086
  98.4 0.9 update.1
  (46 shorter events, 2.7 us)
Async XLA Ops:
  1.5 25.7 %collective-permute-start.1 = (bf16[2048,192]{0,1:T(8,128)(2,1)}, bf16[2048,192]{0,1:T(8,128)(2,1)S(1)}, u32[]{:S(2)}, u32[]{:S(2)}) collective-permute-start(bf16[2048,192]{0,1:T(8,128)(2,1)} %param.18), channel_id=1, source_target_pairs={{0,2},{1,3},{2,0},{3,1},{4,6},{5,7},{6,4},{7,5},{8,10},{9,11},{10,... | collective-permute-start | bytes 2359304 | tf_op jit(solution)/shard_map/ppermute | solution.py:953
  18.3 8.9 %collective-permute-start = (bf16[8,16,896]{2,1,0:T(8,128)(2,1)S(1)}, bf16[8,16,896]{2,1,0:T(8,128)(2,1)S(1)}, u32[]{:S(2)}, u32[]{:S(2)}) collective-permute-start(bf16[8,16,896]{2,1,0:T(8,128)(2,1)S(1)} %all_to_all.17.after.refs_0_), channel_id=1, source_target_pairs={{0,2},{1,3},{2,0},{3,1},{4,6},{5,7},{6,4},{7,5},{8,10},{9,11},{10,... | collective-permute-start | bytes 688136 | tf_op jit(solution)/shard_map/ppermute | solution.py:953
  18.8 10.9 %collective-permute-start.4 = (bf16[2048,192]{0,1:T(8,128)(2,1)}, bf16[2048,192]{0,1:T(8,128)(2,1)S(1)}, u32[]{:S(2)}, u32[]{:S(2)}) collective-permute-start(bf16[2048,192]{0,1:T(8,128)(2,1)} %param.18), channel_id=1, source_target_pairs={{0,1},{1,0},{2,3},{3,2},{4,5},{5,4},{6,7},{7,6},{8,9},{9,8},{10,11... | collective-permute-start | bytes 2359304 | tf_op jit(solution)/shard_map/ppermute | solution.py:953
  27.2 2.9 %collective-permute-start.5 = (bf16[2048,192]{0,1:T(8,128)(2,1)S(1)}, bf16[2048,192]{0,1:T(8,128)(2,1)}, u32[]{:S(2)}, u32[]{:S(2)}) collective-permute-start(bf16[2048,192]{0,1:T(8,128)(2,1)S(1)} %collective-permute-done.1), channel_id=1, source_target_pairs={{0,1},{1,0},{2,3},{3,2},{4,5},{5,4},{6,7},{7,6},{8,9},{9,8},{10,11... | collective-permute-start | bytes 2359304 | tf_op jit(solution)/shard_map/ppermute | solution.py:953
  27.2 2.5 %collective-permute-start.2 = (bf16[8,16,896]{2,1,0:T(8,128)(2,1)S(1)}, bf16[8,16,896]{2,1,0:T(8,128)(2,1)S(1)}, u32[]{:S(2)}, u32[]{:S(2)}) collective-permute-start(bf16[8,16,896]{2,1,0:T(8,128)(2,1)S(1)} %all_to_all.17.after.refs_0_), channel_id=1, source_target_pairs={{0,1},{1,0},{2,3},{3,2},{4,5},{5,4},{6,7},{7,6},{8,9},{9,8},{10,11... | collective-permute-start | bytes 688136 | tf_op jit(solution)/shard_map/ppermute | solution.py:953
  27.8 2.4 %collective-permute-start.3 = (bf16[8,16,896]{2,1,0:T(8,128)(2,1)S(1)}, bf16[8,16,896]{2,1,0:T(8,128)(2,1)S(1)}, u32[]{:S(2)}, u32[]{:S(2)}) collective-permute-start(bf16[8,16,896]{2,1,0:T(8,128)(2,1)S(1)} %collective-permute-done.refs_2_), channel_id=1, source_target_pairs={{0,1},{1,0},{2,3},{3,2},{4,5},{5,4},{6,7},{7,6},{8,9},{9,8},{10,11... | collective-permute-start | bytes 688136 | tf_op jit(solution)/shard_map/ppermute | solution.py:953
  60.0 1.6 %collective-permute-start.7 = (bf16[8,16,896]{2,1,0:T(8,128)(2,1)S(1)}, bf16[8,16,896]{2,1,0:T(8,128)(2,1)S(1)}, u32[]{:S(2)}, u32[]{:S(2)}) collective-permute-start(bf16[8,16,896]{2,1,0:T(8,128)(2,1)S(1)} %get-tuple-element.94), channel_id=1, source_target_pairs={{0,1},{1,0},{2,3},{3,2},{4,5},{5,4},{6,7},{7,6},{8,9},{9,8},{10,11... | collective-permute-start | bytes 688136 | tf_op jit(solution)/shard_map/ppermute | solution.py:953
  60.2 3.2 %collective-permute-start.6 = (bf16[8,16,896]{2,1,0:T(8,128)(2,1)S(1)}, bf16[8,16,896]{2,1,0:T(8,128)(2,1)S(1)}, u32[]{:S(2)}, u32[]{:S(2)}) collective-permute-start(bf16[8,16,896]{2,1,0:T(8,128)(2,1)S(1)} %get-tuple-element.92), channel_id=1, source_target_pairs={{0,1},{1,0},{2,3},{3,2},{4,5},{5,4},{6,7},{7,6},{8,9},{9,8},{10,11... | collective-permute-start | bytes 688136 | tf_op jit(solution)/shard_map/ppermute | solution.py:953
  61.7 7.7 %collective-permute-start.8 = (bf16[8,16,896]{2,1,0:T(8,128)(2,1)S(1)}, bf16[8,16,896]{2,1,0:T(8,128)(2,1)S(1)}, u32[]{:S(2)}, u32[]{:S(2)}) collective-permute-start(bf16[8,16,896]{2,1,0:T(8,128)(2,1)S(1)} %core_sum.1), channel_id=1, source_target_pairs={{0,2},{1,3},{2,0},{3,1},{4,6},{5,7},{6,4},{7,5},{8,10},{9,11},{10,... | collective-permute-start | bytes 688136 | tf_op jit(solution)/shard_map/ppermute | solution.py:953
  70.0 28.3 %copy-start = (f32[1,13824]{1,0:T(1,128)S(1)}, f32[1,13824]{1,0:T(1,128)}, u32[]{:S(2)}) copy-start(f32[1,13824]{1,0:T(1,128)} %refs_0_.1) | copy-start | bytes 165892
  70.0 28.3 %copy-start.1 = (f32[1,13824]{1,0:T(1,128)S(1)}, f32[1,13824]{1,0:T(1,128)}, u32[]{:S(2)}) copy-start(f32[1,13824]{1,0:T(1,128)} %refs_1_.1) | copy-start | bytes 165892
  70.0 28.3 %copy-start.2 = (f32[1,13824]{1,0:T(1,128)S(1)}, f32[1,13824]{1,0:T(1,128)}, u32[]{:S(2)}) copy-start(f32[1,13824]{1,0:T(1,128)} %refs_2_.1) | copy-start | bytes 165892
  70.1 28.3 %copy-start.3 = (f32[1,13824]{1,0:T(1,128)S(1)}, f32[1,13824]{1,0:T(1,128)}, u32[]{:S(2)}) copy-start(f32[1,13824]{1,0:T(1,128)} %refs_3_.1) | copy-start | bytes 165892
  70.1 28.3 %copy-start.4 = (f32[343,6]{0,1:T(8,128)S(1)}, f32[343,6]{0,1:T(8,128)}, u32[]{:S(2)}) copy-start(f32[343,6]{0,1:T(8,128)} %param.30) | copy-start | bytes 24700
  70.1 28.3 %copy-start.5 = (f32[343,6]{0,1:T(8,128)S(1)}, f32[343,6]{0,1:T(8,128)}, u32[]{:S(2)}) copy-start(f32[343,6]{0,1:T(8,128)} %param.31) | copy-start | bytes 24700
  70.1 28.3 %copy-start.6 = (f32[343,6]{0,1:T(8,128)S(1)}, f32[343,6]{0,1:T(8,128)}, u32[]{:S(2)}) copy-start(f32[343,6]{0,1:T(8,128)} %param.32) | copy-start | bytes 24700
  70.1 28.3 %copy-start.7 = (f32[343,6]{0,1:T(8,128)S(1)}, f32[343,6]{0,1:T(8,128)}, u32[]{:S(2)}) copy-start(f32[343,6]{0,1:T(8,128)} %param.33) | copy-start | bytes 24700
  70.2 4.9 %collective-permute-start.9 = (bf16[4,16,896]{2,1,0:T(8,128)(2,1)S(1)}, bf16[4,16,896]{2,1,0:T(8,128)(2,1)S(1)}, u32[]{:S(2)}, u32[]{:S(2)}) collective-permute-start(bf16[4,16,896]{2,1,0:T(8,128)(2,1)S(1)} %get-tuple-element.101), channel_id=1, source_target_pairs={{0,4},{4,0},{8,12},{12,8},{16,20},{20,16},{24,28},{28,24},{1,5},{5... | collective-permute-start | bytes 344072 | tf_op jit(solution)/shard_map/ppermute | solution.py:953
  71.9 10.3 %collective-permute-start.12 = (bf16[192,512]{1,0:T(8,128)(2,1)S(1)}, bf16[192,512]{1,0:T(8,128)(2,1)S(1)}, u32[]{:S(2)}, u32[]{:S(2)}) collective-permute-start(bf16[192,512]{1,0:T(8,128)(2,1)S(1)} %get-tuple-element.107), channel_id=1, source_target_pairs={{0,1},{1,0},{2,3},{3,2},{4,5},{5,4},{6,7},{7,6},{8,9},{9,8},{10,11... | collective-permute-start | bytes 589832 | tf_op jit(solution)/shard_map/ppermute | solution.py:953
  71.9 10.3 %collective-permute-start.13 = (bf16[192,512]{1,0:T(8,128)(2,1)S(1)}, bf16[192,512]{1,0:T(8,128)(2,1)S(1)}, u32[]{:S(2)}, u32[]{:S(2)}) collective-permute-start(bf16[192,512]{1,0:T(8,128)(2,1)S(1)} %get-tuple-element.108), channel_id=1, source_target_pairs={{0,2},{1,3},{2,0},{3,1},{4,6},{5,7},{6,4},{7,5},{8,10},{9,11},{10,... | collective-permute-start | bytes 589832 | tf_op jit(solution)/shard_map/ppermute | solution.py:953
  73.5 9.6 %collective-permute-start.14 = (bf16[192,512]{1,0:T(8,128)(2,1)S(1)}, bf16[192,512]{1,0:T(8,128)(2,1)S(1)}, u32[]{:S(2)}, u32[]{:S(2)}) collective-permute-start(bf16[192,512]{1,0:T(8,128)(2,1)S(1)} %get-tuple-element.109), channel_id=1, source_target_pairs={{0,3},{1,2},{2,1},{3,0},{4,7},{5,6},{6,5},{7,4},{8,11},{9,10},{10,... | collective-permute-start | bytes 589832 | tf_op jit(solution)/shard_map/ppermute | solution.py:953
  75.0 4.2 %collective-permute-start.10 = (bf16[2,16,896]{2,1,0:T(8,128)(2,1)S(1)}, bf16[2,16,896]{2,1,0:T(8,128)(2,1)S(1)}, u32[]{:S(2)}, u32[]{:S(2)}) collective-permute-start(bf16[2,16,896]{2,1,0:T(8,128)(2,1)S(1)} %get-tuple-element.103), channel_id=1, source_target_pairs={{0,8},{4,12},{8,0},{12,4},{16,24},{20,28},{24,16},{28,20},{1,9},{5... | collective-permute-start | bytes 172040 | tf_op jit(solution)/shard_map/ppermute | solution.py:953
  79.3 4.8 %collective-permute-start.11 = (bf16[1,16,896]{2,1,0:T(8,128)(2,1)S(1)}, bf16[1,16,896]{2,1,0:T(8,128)(2,1)S(1)}, u32[]{:S(2)}, u32[]{:S(2)}) collective-permute-start(bf16[1,16,896]{2,1,0:T(8,128)(2,1)S(1)} %get-tuple-element.105), channel_id=1, source_target_pairs={{0,16},{4,20},{8,24},{12,28},{16,0},{20,4},{24,8},{28,12},{1,17},{... | collective-permute-start | bytes 86024 | tf_op jit(solution)/shard_map/ppermute | solution.py:953
  84.9 13.5 %all-to-all-start.1 = ((f32[32,1,128]{2,1,0:T(1,128)}), f32[32,1,128]{2,1,0:T(1,128)S(1)}, u32[]{:S(2)}, u32[]{:S(2)}) async-start(f32[32,1,128]{2,1,0:T(1,128)} %bitcast.13), calls=%async_computation.1 | async-start | bytes 32768 | tf_op jit(solution)/shard_map/all_to_all | solution.py:1086
  (5 other events, 116.0 us)
